TPU v7x, 256 devices: a whole 4x4x8 slice. The times are simulated.
256 devices in a mesh: gx: 8 (over z), gy: 32 (over x, y, core).
Axes of the slice: x: 4, y: 4, z: 8, core: 2. Of those that a mesh axis runs over, the one named last changes fastest.
Arguments:
- initial_field: float32 [8, 64, 8192], P(None, 'gx', 'gy'), may hold values from -6 to 6
- target_field: float32 [8, 64, 8192], P(None, 'gx', 'gy'), may hold values from -8 to 8
- land_mask: int32 [64, 8192], P('gx', 'gy'), may hold values 0 or 1
- conv_one: float32 [64, 73], replicated, may hold values from -0.75 to 0.75
- conv_two: float32 [64, 577], replicated, may hold values from -0.25 to 0.25
- head_weights: float32 [32, 65], replicated, may hold values from -0.75 to 0.75
- dir_one: float32 [64, 73], replicated, may hold values from -6 to 6
- dir_two: float32 [64, 577], replicated, may hold values from -6 to 6
- dir_three: float32 [32, 65], replicated, may hold values from -6 to 6
- group_ids: int32 [160], replicated, may hold values from 0 to 5, as said below
Outputs:
- final_field: float32 [8, 64, 8192], P(None, 'gx', 'gy')
- update_one: float32 [64, 73], replicated
- update_two: float32 [64, 577], replicated
- update_three: float32 [32, 65], replicated
Inputs may be any that keep to these rules, and one draw needn't show every extreme that they name: `group_ids`: each of the 6 group numbers names 26 or 27 rows.
All inputs are finite; a program needn't handle non-finite values. No bound on the sum of `land_mask` on one device may be relied on, other than what follows from the above.
Results may differ from a plain program's by a relative error of at most 0.0024.
The roundings to bfloat16 on the way count: a program that leaves them out, or rounds other values in their place, can miss the bound.
Values may be sent and summed in bfloat16 or wider, within the bound.
No kernel may reach another device: no remote copies, remote signals or barrier semaphores. Data moves between devices by JAX's collectives and lax.ppermute only.
A program may use at most 64 MiB of HBM per device.

v0:
```python
import math

import jax
import jax.numpy as jnp
from jax import lax
from jax.experimental import pallas as pl
from jax.experimental.pallas import tpu as pltpu
from jax.sharding import Mesh
from jax.sharding import PartitionSpec as P

LEV = 8
C = 64
K = 32
GROUPS = 6
PARAMS = 43680
GY = ("gy_0", "gy_1", "gy_2")
H = 8
W = 256
PITCH = 384
REACH = 6
BF = jnp.bfloat16
F32 = jnp.float32
NT = (((1,), (1,)), ((), ()))


def dot(a, b):
    return jnp.dot(a, b, preferred_element_type=F32)


def dot_nt(a, b):
    return lax.dot_general(a, b, NT, preferred_element_type=F32)


def turned(v, by):
    return pltpu.roll(v, by % v.shape[1], 1)


def sigmoid(v):
    return 0.5 * jnp.tanh(0.5 * v) + 0.5


def silu_slope(v, s):
    return s * (1.0 + v * (1.0 - s))


def pack_rows(init_ref, target_ref, mask_ref, low_ref, high_ref):
    wet = mask_ref[...].astype(F32)
    low_ref[64:72, :] = wet
    high_ref[64:72, :] = wet
    for k in range(REACH):
        low_ref[k * 8 : k * 8 + 8, :] = init_ref[:, k, :] * wet[k : k + 1]
        r = H - REACH + k
        high_ref[k * 8 : k * 8 + 8, :] = init_ref[:, r, :] * wet[r : r + 1]
    for k in range(2):
        low_ref[48 + k * 8 : 56 + k * 8, :] = target_ref[:, k, :]
        high_ref[48 + k * 8 : 56 + k * 8, :] = target_ref[:, H - 2 + k, :]


def row_parts(r, init_ref, target_ref, mask_ref, below_ref, above_ref):
    if 0 <= r < H:
        wet = mask_ref[r : r + 1, :].astype(F32)
        return init_ref[:, r, :] * wet, wet, target_ref[:, r, :]
    ref, k = (below_ref, r + REACH) if r < 0 else (above_ref, r - H)
    field = ref[k * 8 : k * 8 + 8, :]
    m = r + H if r < 0 else r - H
    wet = ref[64 + m : 65 + m, :]
    target = None
    if -2 <= r < H + 2:
        t = r + 2 if r < 0 else r - H
        target = ref[48 + 8 * t : 56 + 8 * t, :]
    return field, wet, target


def pack_cols(init_ref, target_ref, mask_ref, below_ref, above_ref, left_ref, right_ref):
    lane = lax.broadcasted_iota(jnp.int32, (8, 128), 1)
    for r in range(-REACH, H + REACH):
        field, wet, target = row_parts(r, init_ref, target_ref, mask_ref, below_ref, above_ref)
        wet = jnp.broadcast_to(wet, (8, W))
        a = jnp.where(lane < 32, field[:, :128], turned(wet[:, :128], 32))
        b = jnp.where(lane >= 96, field[:, 128:], turned(wet[:, 128:], -32))
        if target is not None:
            a = jnp.where(lane < 64, a, turned(target[:, :128], 64))
            b = jnp.where(lane >= 64, b, turned(target[:, 128:], -64))
        at = (r + REACH) * 8
        left_ref[at : at + 8, :] = a
        right_ref[at : at + 8, :] = b


def prepare(one_ref, two_ref, head_ref, w1_ref, w2_ref, w3_ref, w3t_ref, w2t_ref, w1t_ref, bias_ref):
    one, two, head = one_ref[...], two_ref[...], head_ref[...]
    w1_ref[...] = one[:, : 9 * LEV].astype(BF)
    w2_ref[...] = two[:, : 9 * C].astype(BF)
    w3_ref[...] = head[:, :C].astype(BF)
    w3t_ref[...] = head[:, :C].T.astype(BF)
    w2t_ref[...] = jnp.concatenate(
        [two[:, (8 - k) * C : (9 - k) * C].T for k in range(9)], axis=1
    ).astype(BF)
    w1t_ref[...] = jnp.concatenate(
        [
            jnp.concatenate(
                [one[:, (3 * (2 - a) + b) * LEV : (3 * (2 - a) + b + 1) * LEV].T for a in range(3)],
                axis=1,
            )
            for b in range(3)
        ],
        axis=0,
    ).astype(BF)
    bias_ref[0:64, :] = jnp.broadcast_to(one[:, 9 * LEV :], (64, 128))
    bias_ref[64:128, :] = jnp.broadcast_to(two[:, 9 * C :], (64, 128))
    bias_ref[128:160, :] = jnp.broadcast_to(head[:, C:], (32, 128))


def lanes(parts):
    return parts[0] if len(parts) == 1 else jnp.concatenate(parts, axis=1)


def cut(v, n):
    return [v[:, k * PITCH : (k + 1) * PITCH] for k in range(n)]


def folded(v):
    total = v[:, :128]
    for k in range(1, v.shape[1] // 128):
        total = total + v[:, k * 128 : (k + 1) * 128]
    return total


def main(
    place_ref, init_ref, target_ref, mask_ref, below_ref, above_ref, fromleft_ref, fromright_ref,
    w1_ref, w2_ref, w3_ref, w3t_ref, w2t_ref, w1t_ref, bias_ref,
    final_ref, grad_ref,
    xc0, xc1, wet_s, tgt, hc0, hc1, h2s, sp10, sp11, sp2, wd, ec0, ec1, e1s, rem, up, down, fin,
    b1g, b2g, b3g, g1, g2, g3,
):
    lane = lax.broadcasted_iota(jnp.int32, (8, 128), 1)
    zero = jnp.zeros((8, 128), F32)
    for r in range(-REACH, H + REACH):
        field, wet, target = row_parts(r, init_ref, target_ref, mask_ref, below_ref, above_ref)
        at = (r + REACH) * 8
        fl, fr = fromleft_ref[at : at + 8, :], fromright_ref[at : at + 8, :]

        def rim(by):
            right, left = (turned(fr, -by), turned(fl, by)) if by else (fr, fl)
            return jnp.where(lane < 16, right, jnp.where(lane >= 112, left, zero))

        row = jnp.concatenate([field, rim(0)], axis=1)
        xc0[at * 3 : at * 3 + 24, :] = jnp.concatenate(
            [turned(row, 1), row, turned(row, -1)], axis=0
        )
        wet_s[at : at + 8, :] = jnp.concatenate([jnp.broadcast_to(wet, (8, W)), rim(32)], axis=1)
        if target is not None:
            tgt[at : at + 8, :] = jnp.concatenate([target, rim(64)], axis=1)
    for ref in (b1g, b2g, b3g, g1, g2, g3):
        ref[...] = jnp.zeros(ref.shape, F32)
    for r in (4, 5, 14, 15):
        ec0[r * 192 : r * 192 + 192, :] = jnp.zeros((192, PITCH), BF)

    col = lax.broadcasted_iota(jnp.int32, (1, PITCH), 1)
    col = jnp.where(col < 320, col, col - PITCH) + place_ref[1]
    col_in = jnp.where((col >= 0) & (col < place_ref[3]), 1.0, 0.0).astype(F32)

    def inside(r):
        i = place_ref[0] + r - REACH
        return col_in * jnp.where((i >= 0) & (i < place_ref[2]), 1.0, 0.0)

    def bias(at, n, times=1):
        b = bias_ref[at : at + n, :]
        return jnp.concatenate([b] * (3 * times), axis=1)

    def part(ref, r, size, first=0, count=None):
        start = r * size + first
        if not isinstance(start, int):
            start = pl.multiple_of(start, 8 if size % 16 or first % 16 else 16)
        return ref.at[pl.ds(start, size if count is None else count), :]

    def loop(lo, hi, per, body):
        def step(i, carry):
            body([lo + REACH + i * per + k for k in range(per)])
            return carry

        lax.fori_loop(0, (hi - lo) // per, step, 0)

    def thrice(v):
        return turned(v, 1), v, turned(v, -1)

    def store_thrice(ref, r, v):
        for k, piece in enumerate(thrice(v)):
            part(ref, r, 192, 64 * k, 64)[...] = piece.astype(BF)

    def first_layer(xc, hc, sp1):
        def body(rs):
            x9 = lanes([part(xc, r - 1, 24, 0, 72)[...].astype(BF) for r in rs])
            for r, z in zip(rs, cut(dot(w1_ref[...], x9), len(rs))):
                z = z + bias(0, 64)
                s = sigmoid(z)
                keep = inside(r)
                store_thrice(hc, r, z * s * keep)
                part(sp1, r, 64)[...] = silu_slope(z, s) * keep

        return body

    def second_layer(hc, rs):
        z = dot(w2_ref[...], lanes([part(hc, r - 1, 192, 0, 576)[...] for r in rs]))
        z = z + bias(64, 64, len(rs))
        s = sigmoid(z)
        h2 = (z * s).astype(BF)
        q = dot(w3_ref[...], h2) + bias(128, 32, len(rs))
        return h2, silu_slope(z, s), sigmoid(q)

    def slopes(xc, r):
        x = part(xc, r, 24, 8, 8)[...]
        beside = (
            part(xc, r + 1, 24, 8, 8)[...],
            part(xc, r - 1, 24, 8, 8)[...],
            part(xc, r, 24, 16, 8)[...],
            part(xc, r, 24, 0, 8)[...],
        )
        return x, [b - x for b in beside]

    def tail_zero(rs):
        h2, slope, p = second_layer(hc0, rs)
        n = len(rs)
        for r, h2r, sr, pr in zip(rs, cut(h2, n), cut(slope, n), cut(p, n)):
            part(h2s, r, 64)[...] = h2r
            part(sp2, r, 64)[...] = sr
            x, diff = slopes(xc0, r)
            wet = part(wet_s, r, 8)[...]
            change = jnp.zeros_like(x)
            for k in range(4):
                pk = pr[8 * k : 8 * k + 8]
                move = 0.25 * pk * diff[k]
                change = change + move
                part(wd, r, 32, 8 * k, 8)[...] = wet * move * (1.0 - pk)
            for k, piece in enumerate(thrice(x + wet * change)):
                part(xc1, r, 24, 8 * k, 8)[...] = piece

    def tail_grads(rs, e3, e2, h2, hc):
        b3g[...] += sum(folded(e[:, :W]) for e in e3)
        b2g[...] += sum(folded(e[:, :W]) for e in e2)
        g3[...] += dot_nt(
            lanes([e[:, :W].astype(BF) for e in e3]), lanes([v[:, :W] for v in h2])
        )
        g2[...] += dot_nt(
            lanes([e[:, :W].astype(BF) for e in e2]),
            lanes([part(hc, r - 1, 192, 0, 576)[:, :W] for r in rs]),
        )

    def tail_one(own):
        def body(rs):
            h2, slope, p = second_layer(hc1, rs)
            n = len(rs)
            e3s = []
            for r, pr in zip(rs, cut(p, n)):
                x, diff = slopes(xc1, r)
                wet = part(wet_s, r, 8)[...]
                c = [0.25 * pr[8 * k : 8 * k + 8] for k in range(4)]
                move = [c[k] * diff[k] for k in range(4)]
                new = x + wet * (move[0] + move[1] + move[2] + move[3])
                if own:
                    part(fin, r, 8)[...] = new
                g = wet * (new - part(tgt, r, 8)[...])
                wg = wet * g
                t = [wg * c[k] for k in range(4)]
                left = g - t[0] - t[1] - t[2] - t[3]
                part(rem, r, 8)[...] = left + turned(t[2], 1) + turned(t[3], -1)
                part(up, r, 8)[...] = t[0]
                part(down, r, 8)[...] = t[1]
                e3s.append(
                    jnp.concatenate(
                        [wg * move[k] * (1.0 - pr[8 * k : 8 * k + 8]) for k in range(4)], axis=0
                    )
                )
            e2 = dot(w3t_ref[...], lanes([e.astype(BF) for e in e3s])) * slope
            e2s = cut(e2, n)
            for r, e in zip(rs, e2s):
                store_thrice(ec1, r, e)
            if own:
                tail_grads(rs, e3s, e2s, cut(h2, n), hc1)

        return body

    def first_error(ec, sp1, rs):
        e = dot(w2t_ref[...], lanes([part(ec, r - 1, 192, 0, 576)[...] for r in rs]))
        return [v * part(sp1, r, 64)[...] for r, v in zip(rs, cut(e, len(rs)))]

    def first_grads(rs, e1, xc, width):
        b1g[...] += sum(folded(e[:, :width]) for e in e1)
        g1[...] += dot_nt(
            lanes([e[:, :width].astype(BF) for e in e1]),
            lanes([part(xc, r - 1, 24, 0, 72)[:, :width].astype(BF) for r in rs]),
        )

    def first_one(own):
        def body(rs):
            e1 = first_error(ec1, sp11, rs)
            for r, e in zip(rs, e1):
                part(e1s, r, 64)[...] = e.astype(BF)
            if own:
                first_grads(rs, e1, xc1, W)

        return body

    def back_zero(rs):
        y = dot(w1t_ref[...], lanes([part(e1s, r - 1, 64, 0, 192)[...] for r in rs]))
        e3s = []
        for r, yr in zip(rs, cut(y, len(rs))):
            g = part(rem, r, 8)[...] + part(up, r - 1, 8)[...] + part(down, r + 1, 8)[...]
            g = g + yr[8:16] + turned(yr[0:8], -1) + turned(yr[16:24], 1)
            e3 = jnp.concatenate([g] * 4, axis=0) * part(wd, r, 32)[...]
            e3s.append(jnp.concatenate([e3[:, :W], jnp.zeros((K, PITCH - W), F32)], axis=1))
        e2 = dot(w3t_ref[...], lanes([e.astype(BF) for e in e3s]))
        e2s = [v * part(sp2, r, 64)[...] for r, v in zip(rs, cut(e2, len(rs)))]
        for r, e in zip(rs, e2s):
            store_thrice(ec0, r, e)
        tail_grads(rs, e3s, e2s, [part(h2s, r, 64)[...] for r in rs], hc0)

    def first_zero(rs):
        first_grads(rs, first_error(ec0, sp10, rs), xc0, PITCH)

    loop(-5, 13, 2, first_layer(xc0, hc0, sp10))
    loop(-4, 12, 2, tail_zero)
    loop(-3, 11, 2, first_layer(xc1, hc1, sp11))
    tail_one(False)([4, 5])
    tail_one(False)([14, 15])
    loop(0, 8, 2, tail_one(True))
    first_one(False)([5, 14])
    loop(0, 8, 2, first_one(True))
    loop(0, 8, 2, back_zero)
    loop(-1, 9, 2, first_zero)

    for r in range(H):
        final_ref[:, r, :] = fin[(r + REACH) * 8 : (r + REACH) * 8 + 8, :W]
    for k in range(4):
        grad_ref[k * 64 : k * 64 + 64, :] = g2[:, k * 128 : k * 128 + 128]
    grad_ref[256:320, :] = jnp.concatenate([g2[:, 512:576], g1[:, 0:64]], axis=1)
    sums = [jnp.sum(ref[...], axis=1, keepdims=True) for ref in (b1g, b2g, b3g)]
    sums[2] = jnp.concatenate([sums[2], jnp.zeros((32, 1), F32)], axis=0)
    grad_ref[320:384, :] = jnp.concatenate(
        [
            g1[:, 64:72],
            *sums,
            jnp.zeros((64, 53), F32),
            jnp.concatenate([g3[...], jnp.zeros((32, 64), F32)], axis=0),
        ],
        axis=1,
    )


def finish(total_ref, d1_ref, d2_ref, d3_ref, gid_ref, u1_ref, u2_ref, u3_ref):
    t = [total_ref[k * 64 : k * 64 + 64, :] for k in range(6)]
    two = jnp.concatenate([*t[:4], t[4][:, :64], t[5][:, 9:10]], axis=1)
    one = jnp.concatenate([t[4][:, 64:], t[5][:, :8], t[5][:, 8:9]], axis=1)
    three = jnp.concatenate([t[5][:32, 64:], t[5][:32, 10:11]], axis=1)

    def row_sums(parts):
        return jnp.concatenate([jnp.sum(v * v, axis=1, keepdims=True) for v in parts], axis=0)

    grads = (one, two, three)
    dirs = (d1_ref[...], d2_ref[...], d3_ref[...])
    norm = jnp.sqrt(jnp.sum(row_sums(grads), axis=0, keepdims=True))
    factor = 1.0 / jnp.maximum(norm, 1.0)
    clipped = [v * factor for v in grads]
    group = lax.broadcasted_iota(jnp.int32, (160, 128), 1)
    choose = jnp.where(gid_ref[...] == group, 1.0, 0.0)
    clip_groups = jnp.sum(choose * row_sums(clipped), axis=0, keepdims=True)
    dir_groups = jnp.sum(choose * row_sums(dirs), axis=0, keepdims=True)
    ratios = jnp.sqrt(clip_groups) / jnp.sqrt(dir_groups + 1e-06)
    row_ratio = jnp.sum(choose * ratios, axis=1, keepdims=True)
    scaling = math.sqrt(PARAMS)
    at = 0
    for ref, v, d in zip((u1_ref, u2_ref, u3_ref), clipped, dirs):
        n = v.shape[0]
        ref[...] = scaling * (v + row_ratio[at : at + n] * d)
        at += n


def shape(dims, dtype=F32):
    return jax.ShapeDtypeStruct(dims, dtype)


def kernel(body, outs, cost, **more):
    return pl.pallas_call(
        body,
        out_shape=outs,
        cost_estimate=pl.CostEstimate(flops=cost, bytes_accessed=cost, transcendentals=0),
        compiler_params=pltpu.CompilerParams(vmem_limit_bytes=60 * 2**20),
        **more,
    )


def exchange(forward, backward, axis):
    count = lax.axis_size(axis)
    ahead = [(i, i + 1) for i in range(count - 1)]
    back = [(b, a) for a, b in ahead]
    return lax.ppermute(forward, axis, ahead), lax.ppermute(backward, axis, back)


def total_of(grad):
    near, far = ("gy_0", "gy_1"), ("gx", "gy_2")
    n = lax.axis_size(near)
    pieces = grad.reshape(n, -1, 128)
    own = jnp.sum(lax.all_to_all(pieces, near, 0, 0, tiled=True), axis=0)
    m = lax.axis_size(far)
    copies = jnp.broadcast_to(own, (m, *own.shape))
    own = jnp.sum(lax.all_to_all(copies, far, 0, 0, tiled=True), axis=0)
    copies = jnp.broadcast_to(own, (n, *own.shape))
    return lax.all_to_all(copies, near, 0, 0, tiled=True).reshape(grad.shape)


def per_device(init, target, mask, one, two, head, d1, d2, d3, gid):
    place = jnp.stack(
        [
            lax.axis_index("gx") * H,
            lax.axis_index(GY) * W,
            lax.axis_size("gx") * H,
            lax.axis_size(GY) * W,
        ]
    ).astype(jnp.int32)
    to_low, to_high = kernel(pack_rows, [shape((72, W))] * 2, 10**5)(init, target, mask)
    below, above = exchange(to_high, to_low, "gx")
    weights = kernel(
        prepare,
        [
            shape((C, 72), BF), shape((C, 576), BF), shape((K, C), BF), shape((C, K), BF),
            shape((C, 576), BF), shape((24, 192), BF), shape((160, 128)),
        ],
        10**6,
    )(one, two, head)
    to_left, to_right = kernel(pack_cols, [shape((160, 128))] * 2, 10**5)(
        init, target, mask, below, above
    )
    from_left, from_right = exchange(to_right, to_left, GY)

    def rows(size, dtype=F32):
        return pltpu.VMEM((20 * size, PITCH), dtype)

    vmem = pl.BlockSpec(memory_space=pltpu.VMEM)
    final, grad = kernel(
        main,
        [shape((LEV, H, W)), shape((384, 128))],
        10**7,
        in_specs=[pl.BlockSpec(memory_space=pltpu.SMEM)] + [vmem] * 14,
        out_specs=[vmem] * 2,
        scratch_shapes=[
            rows(24), rows(24), rows(8), rows(8), rows(192, BF), rows(192, BF), rows(64, BF),
            rows(64), rows(64), rows(64), rows(32), rows(192, BF), rows(192, BF), rows(64, BF),
            rows(8), rows(8), rows(8), rows(8),
            pltpu.VMEM((64, 128), F32), pltpu.VMEM((64, 128), F32), pltpu.VMEM((32, 128), F32),
            pltpu.VMEM((64, 72), F32), pltpu.VMEM((64, 576), F32), pltpu.VMEM((32, 64), F32),
        ],
    )(place, init, target, mask, below, above, from_left, from_right, *weights)
    total = total_of(grad)
    u1, u2, u3 = kernel(finish, [shape(one.shape), shape(two.shape), shape(head.shape)], 10**6)(
        total, d1, d2, d3, gid.reshape(-1, 1)
    )
    return final, u1, u2, u3


def solution(mesh):
    count = mesh.shape["gy"] // 8
    torus = Mesh(mesh.devices.reshape(mesh.shape["gx"], count, 4, 2), ("gx", *GY))
    placed = (P(None, "gx", GY), P(None, "gx", GY), P("gx", GY), P(), P(), P(), P(), P(), P(), P())
    return jax.shard_map(
        per_device,
        mesh=torus,
        in_specs=placed,
        out_specs=(P(None, "gx", GY), P(), P(), P()),
        check_vma=False,
    )
```

profile of v0, /device:TPU:1, one launch (start us, length us, event | category | flops | bytes accessed | tf_op | source)
XLA Modules:
  0.0 97.2 jit_solution(2917294326990144528)
XLA Ops:
  0.6 1.6 %shard_map.129 = (f32[72,256]{1,0:T(8,128)}, f32[72,256]{1,0:T(8,128)}) custom-call(f32[8,8,256]{2,1,0:T(8,128)} %init_ref.5, f32[8,8,256]{2,1,0:T(8,128)} %target_ref.5, s32[8,256]{1,0:T(8,128)} %mask_ref.5), custom_call_target="tpu_custom_call" | custom-call | flops 100000 | bytes 100000 | tf_op jit(solution)/shard_map/pallas_call | solution.py:419
  2.2 4.4 %collective-permute-start = (f32[72,256]{1,0:T(8,128)}, f32[72,256]{1,0:T(8,128)S(1)}, u32[]{:S(2)}, u32[]{:S(2)}) collective-permute-start(f32[72,256]{1,0:T(8,128)} %get-tuple-element.20), channel_id=1, source_target_pairs={{0,32},{32,64},{64,96},{96,128},{128,160},{160,192},{192,224},{1,3... | collective-permute-start | bytes 221192 | tf_op jit(solution)/shard_map/ppermute | solution.py:395
  6.6 1.3 %collective-permute-start.1 = (f32[72,256]{1,0:T(8,128)}, f32[72,256]{1,0:T(8,128)S(1)}, u32[]{:S(2)}, u32[]{:S(2)}) collective-permute-start(f32[72,256]{1,0:T(8,128)} %get-tuple-element.21), channel_id=1, source_target_pairs={{32,0},{64,32},{96,64},{128,96},{160,128},{192,160},{224,192},{33,... | collective-permute-start | bytes 221192 | tf_op jit(solution)/shard_map/ppermute | solution.py:395
  7.9 2.2 %shard_map.131 = (bf16[64,72]{1,0:T(8,128)(2,1)}, bf16[64,576]{1,0:T(8,128)(2,1)}, bf16[32,64]{1,0:T(8,128)(2,1)}, bf16[64,32]{1,0:T(8,128)(2,1)}, bf16[64,576]{...) custom-call(f32[64,73]{1,0:T(8,128)} %one_ref.1, f32[64,577]{1,0:T(8,128)} %two_ref.1, f32[32,65]{1,0:T(8,128)} %head_ref.1), custom_call_target="tpu_custom_call" | custom-call | flops 1000000 | bytes 1000000 | tf_op jit(solution)/shard_map/pallas_call | solution.py:421
  10.1 0.0 collective-permute-done.below_ref
  10.1 0.0 copy-start.1
  10.1 2.0 %collective-permute-done.1.above_ref = f32[72,256]{1,0:T(8,128)S(1)} collective-permute-done((f32[72,256]{1,0:T(8,128)}, f32[72,256]{1,0:T(8,128)S(1)}, u32[]{:S(2)}, u32[]{:S(2)}) %collective-permute-start.1) | collective-permute-done | bytes 73760 | tf_op jit(solution)/shard_map/ppermute | solution.py:395
  12.1 0.0 copy-done.1
  12.1 0.0 copy-start.2
  12.1 0.6 copy-done.2
  12.7 1.8 %shard_map.130 = (f32[160,128]{1,0:T(8,128)}, f32[160,128]{1,0:T(8,128)}) custom-call(f32[8,8,256]{2,1,0:T(8,128)} %init_ref.5, f32[8,8,256]{2,1,0:T(8,128)} %target_ref.5, s32[8,256]{1,0:T(8,128)} %mask_ref.5, f32[72,256]{1,0:T(8,128)} %copy-done.1, f32[72,256]{1,0:T(8,128)} %copy-done.2), custom_call_target="tpu_custom_call" | custom-call | flops 100000 | bytes 100000 | tf_op jit(solution)/shard_map/pallas_call | solution.py:429
  14.5 5.0 %collective-permute-start.2 = (f32[160,128]{1,0:T(8,128)}, f32[160,128]{1,0:T(8,128)S(1)}, u32[]{:S(2)}, u32[]{:S(2)}) collective-permute-start(f32[160,128]{1,0:T(8,128)} %get-tuple-element.22), channel_id=1, source_target_pairs={{0,1},{1,2},{2,3},{3,4},{4,5},{5,6},{6,7},{7,8},{8,9},{9,10},{10,1... | collective-permute-start | bytes 245768 | tf_op jit(solution)/shard_map/ppermute | solution.py:395
  19.5 1.9 %collective-permute-start.3 = (f32[160,128]{1,0:T(8,128)}, f32[160,128]{1,0:T(8,128)S(1)}, u32[]{:S(2)}, u32[]{:S(2)}) collective-permute-start(f32[160,128]{1,0:T(8,128)} %get-tuple-element.23), channel_id=1, source_target_pairs={{1,0},{2,1},{3,2},{4,3},{5,4},{6,5},{7,6},{8,7},{9,8},{10,9},{11,1... | collective-permute-start | bytes 245768 | tf_op jit(solution)/shard_map/ppermute | solution.py:395
  21.4 0.6 pad_add_fusion.place_ref
  22.1 0.0 collective-permute-done.2.fromleft_ref
  22.1 0.0 copy-start.3
  22.1 3.4 %collective-permute-done.3.fromright_ref = f32[160,128]{1,0:T(8,128)S(1)} collective-permute-done((f32[160,128]{1,0:T(8,128)}, f32[160,128]{1,0:T(8,128)S(1)}, u32[]{:S(2)}, u32[]{:S(2)}) %collective-permute-start.3) | collective-permute-done | bytes 81952 | tf_op jit(solution)/shard_map/ppermute | solution.py:395
  25.5 0.0 copy-start.4
  25.5 0.0 copy-done.3
  25.5 0.6 copy-done.4
  26.1 22.7 %shard_map.132 = (f32[8,8,256]{2,1,0:T(8,128)}, f32[384,128]{1,0:T(8,128)}) custom-call(s32[4]{0:T(128)} %pad_add_fusion.place_ref, f32[8,8,256]{2,1,0:T(8,128)} %init_ref.5, f32[8,8,256]{2,1,0:T(8,128)} %target_ref.5, s32[8,256]{1,0:T(8,128)} %mask_ref.5, f32[72,256]{1,0:T(8,128)} %copy-done.1, f32[72,256]{1,0:T(8,128)} %copy-done.2, f32[160,128]{1,0:T(8,128)} %copy-done.3, ...), custom_call_target="tpu_custom_call" | custom-call | flops 10000000 | bytes 10000000 | tf_op jit(solution)/shard_map/pallas_call | solution.py:438
  48.8 15.0 %all_to_all.15 = f32[16,24,128]{2,1,0:T(8,128)S(1)} all-to-all(f32[16,24,128]{2,1,0:T(8,128)} %bitcast.6), channel_id=1, replica_groups=mesh['gx'=8,'gy_0'=4,'gy_1'=4,'gy_2'=2] {'gy_0','gy_1'}, dimensions={0} | all-to-all | bytes 393216 | tf_op jit(solution)/shard_map/all_to_all | solution.py:402
  63.9 18.6 %all_to_all.16 = f32[16,24,128]{2,1,0:T(8,128)S(1)} all-to-all(f32[16,24,128]{2,1,0:T(8,128)S(1)} %broadcast_in_dim.6), channel_id=1, replica_groups=mesh['gx'=8,'gy_0'=4,'gy_1'=4,'gy_2'=2] {'gx','gy_2'}, dimensions={0} | all-to-all | bytes 393216 | tf_op jit(solution)/shard_map/all_to_all | solution.py:405
  82.5 0.7 broadcast_in_dim.7
  83.2 3.5 %all-to-all-start.2 = ((f32[16,24,128]{2,1,0:T(8,128)}), f32[16,24,128]{2,1,0:T(8,128)S(1)}, u32[]{:S(2)}, u32[]{:S(2)}) async-start(f32[16,24,128]{2,1,0:T(8,128)} %broadcast_in_dim.7), calls=%async_computation.2 | async-start | bytes 393216 | tf_op jit(solution)/shard_map/all_to_all | solution.py:407
  86.7 0.0 copy-start.5
  86.7 0.7 copy-done.5
  87.4 0.8 copy.15.gid_ref
  88.1 6.0 %all-to-all-done.2 = f32[16,24,128]{2,1,0:T(8,128)S(1)} async-done(((f32[16,24,128]{2,1,0:T(8,128)}), f32[16,24,128]{2,1,0:T(8,128)S(1)}, u32[]{:S(2)}, u32[]{:S(2)}) %all-to-all-start.2) | async-done | bytes 196640 | tf_op jit(solution)/shard_map/all_to_all | solution.py:407
  94.1 0.0 copy-start
  94.1 0.7 copy-done
  94.8 2.4 %shard_map.133 = (f32[64,73]{1,0:T(8,128)}, f32[64,577]{1,0:T(8,128)}, f32[32,65]{1,0:T(8,128)}) custom-call(f32[384,128]{1,0:T(8,128)} %bitcast.5, f32[64,73]{1,0:T(8,128)} %d1_ref.1, f32[64,577]{1,0:T(8,128)} %d2_ref.1, f32[32,65]{1,0:T(8,128)} %d3_ref.1, s32[160,1]{1,0:T(8,128)} %copy.15.gid_ref), custom_call_target="tpu_custom_call" | custom-call | flops 1000000 | bytes 1000000 | tf_op jit(solution)/shard_map/pallas_call | solution.py:453
  (3 shorter events, 0.1 us)
Async XLA Ops:
  2.2 7.9 %collective-permute-start = (f32[72,256]{1,0:T(8,128)}, f32[72,256]{1,0:T(8,128)S(1)}, u32[]{:S(2)}, u32[]{:S(2)}) collective-permute-start(f32[72,256]{1,0:T(8,128)} %get-tuple-element.20), channel_id=1, source_target_pairs={{0,32},{32,64},{64,96},{96,128},{128,160},{160,192},{192,224},{1,3... | collective-permute-start | bytes 221192 | tf_op jit(solution)/shard_map/ppermute | solution.py:395
  6.6 5.5 %collective-permute-start.1 = (f32[72,256]{1,0:T(8,128)}, f32[72,256]{1,0:T(8,128)S(1)}, u32[]{:S(2)}, u32[]{:S(2)}) collective-permute-start(f32[72,256]{1,0:T(8,128)} %get-tuple-element.21), channel_id=1, source_target_pairs={{32,0},{64,32},{96,64},{128,96},{160,128},{192,160},{224,192},{33,... | collective-permute-start | bytes 221192 | tf_op jit(solution)/shard_map/ppermute | solution.py:395
  10.1 2.0 %copy-start.1 = (f32[72,256]{1,0:T(8,128)}, f32[72,256]{1,0:T(8,128)S(1)}, u32[]{:S(2)}) copy-start(f32[72,256]{1,0:T(8,128)S(1)} %collective-permute-done.below_ref) | copy-start | bytes 221188
  12.1 0.6 copy-start.2
  14.5 7.6 %collective-permute-start.2 = (f32[160,128]{1,0:T(8,128)}, f32[160,128]{1,0:T(8,128)S(1)}, u32[]{:S(2)}, u32[]{:S(2)}) collective-permute-start(f32[160,128]{1,0:T(8,128)} %get-tuple-element.22), channel_id=1, source_target_pairs={{0,1},{1,2},{2,3},{3,4},{4,5},{5,6},{6,7},{7,8},{8,9},{9,10},{10,1... | collective-permute-start | bytes 245768 | tf_op jit(solution)/shard_map/ppermute | solution.py:395
  19.5 6.0 %collective-permute-start.3 = (f32[160,128]{1,0:T(8,128)}, f32[160,128]{1,0:T(8,128)S(1)}, u32[]{:S(2)}, u32[]{:S(2)}) collective-permute-start(f32[160,128]{1,0:T(8,128)} %get-tuple-element.23), channel_id=1, source_target_pairs={{1,0},{2,1},{3,2},{4,3},{5,4},{6,5},{7,6},{8,7},{9,8},{10,9},{11,1... | collective-permute-start | bytes 245768 | tf_op jit(solution)/shard_map/ppermute | solution.py:395
  22.1 3.4 %copy-start.3 = (f32[160,128]{1,0:T(8,128)}, f32[160,128]{1,0:T(8,128)S(1)}, u32[]{:S(2)}) copy-start(f32[160,128]{1,0:T(8,128)S(1)} %collective-permute-done.2.fromleft_ref) | copy-start | bytes 245764
  25.5 0.6 copy-start.4
  83.2 11.0 %all-to-all-start.2 = ((f32[16,24,128]{2,1,0:T(8,128)}), f32[16,24,128]{2,1,0:T(8,128)S(1)}, u32[]{:S(2)}, u32[]{:S(2)}) async-start(f32[16,24,128]{2,1,0:T(8,128)} %broadcast_in_dim.7), calls=%async_computation.2 | async-start | bytes 393216 | tf_op jit(solution)/shard_map/all_to_all | solution.py:407
  86.7 0.7 copy-start.5
  94.1 0.7 copy-start
where the time goes:
time: 97.8 us; the launch traced here: 97.2 us
  blocking collectives  33.5 us (34%)
  Pallas kernels  30.7 us (31%)
  starting transfers between devices  16.1 us (16%)
  waiting for transfers between devices  11.4 us (12%)
  local copies, waits for them, and re-layouts  4.08 us (4%)
    pallas_call x1, Pallas kernels, per_device(): kernel(main, [shape((LEV, H, W)), shape((384, 128))], 10 ** 7, in_specs=[...  22.7 us
    all_to_all x1, blocking collectives, total_of(): own = jnp.sum(lax.all_to_all(copies, far, 0, 0, tiled=True), axis=0)  18.6 us
    all_to_all x1, blocking collectives, total_of(): own = jnp.sum(lax.all_to_all(pieces, near, 0, 0, tiled=True), axis=0)  15 us
    ppermute x2, starting transfers between devices, exchange(): lax.ppermute(forward, axis, ahead)  9.36 us
    all_to_all x1, waiting for transfers between devices, total_of(): return lax.all_to_all(copies, near, 0, 0, tiled=True).reshape(grad.shape)  6.01 us
    ppermute x2, waiting for transfers between devices, exchange(): lax.ppermute(backward, axis, back)  5.37 us
    all_to_all x1, starting transfers between devices, total_of(): return lax.all_to_all(copies, near, 0, 0, tiled=True).reshape(grad.shape)  3.52 us
    ppermute x2, starting transfers between devices, exchange(): lax.ppermute(backward, axis, back)  3.21 us
  transfers between devices with their start and end apart: 5, of which 3 were waited for; matrix products, arithmetic and copies ran while one was open for 1% of the time, Pallas kernels for 2%

commit v1 on v0

--- a/solution.py
+++ b/solution.py
@@ -126,7 +126,7 @@
 
 
 def main(
-    place_ref, init_ref, target_ref, mask_ref, below_ref, above_ref, fromleft_ref, fromright_ref,
+    init_ref, target_ref, mask_ref, below_ref, above_ref, fromleft_ref, fromright_ref,
     w1_ref, w2_ref, w3_ref, w3t_ref, w2t_ref, w1t_ref, bias_ref,
     final_ref, grad_ref,
     xc0, xc1, wet_s, tgt, hc0, hc1, h2s, sp10, sp11, sp2, wd, ec0, ec1, e1s, rem, up, down, fin,
@@ -156,12 +156,14 @@
         ec0[r * 192 : r * 192 + 192, :] = jnp.zeros((192, PITCH), BF)
 
     col = lax.broadcasted_iota(jnp.int32, (1, PITCH), 1)
-    col = jnp.where(col < 320, col, col - PITCH) + place_ref[1]
-    col_in = jnp.where((col >= 0) & (col < place_ref[3]), 1.0, 0.0).astype(F32)
+    col = jnp.where(col < 320, col, col - PITCH) + lax.axis_index(GY) * W
+    col_in = jnp.where((col >= 0) & (col < lax.axis_size(GY) * W), 1.0, 0.0).astype(F32)
+
+    row0 = lax.axis_index("gx") * H
 
     def inside(r):
-        i = place_ref[0] + r - REACH
-        return col_in * jnp.where((i >= 0) & (i < place_ref[2]), 1.0, 0.0)
+        i = row0 + r - REACH
+        return col_in * jnp.where((i >= 0) & (i < lax.axis_size("gx") * H), 1.0, 0.0)
 
     def bias(at, n, times=1):
         b = bias_ref[at : at + n, :]
@@ -169,16 +171,11 @@
 
     def part(ref, r, size, first=0, count=None):
         start = r * size + first
-        if not isinstance(start, int):
-            start = pl.multiple_of(start, 8 if size % 16 or first % 16 else 16)
-        return ref.at[pl.ds(start, size if count is None else count), :]
+        return ref.at[start : start + (size if count is None else count), :]
 
     def loop(lo, hi, per, body):
-        def step(i, carry):
-            body([lo + REACH + i * per + k for k in range(per)])
-            return carry
-
-        lax.fori_loop(0, (hi - lo) // per, step, 0)
+        for first in range(lo, hi, per):
+            body([first + REACH + k for k in range(per)])
 
     def thrice(v):
         return turned(v, 1), v, turned(v, -1)
@@ -317,16 +314,15 @@
     def first_zero(rs):
         first_grads(rs, first_error(ec0, sp10, rs), xc0, PITCH)
 
-    loop(-5, 13, 2, first_layer(xc0, hc0, sp10))
-    loop(-4, 12, 2, tail_zero)
-    loop(-3, 11, 2, first_layer(xc1, hc1, sp11))
-    tail_one(False)([4, 5])
-    tail_one(False)([14, 15])
-    loop(0, 8, 2, tail_one(True))
+    loop(-5, 13, 9, first_layer(xc0, hc0, sp10))
+    loop(-4, 12, 16, tail_zero)
+    loop(-3, 11, 14, first_layer(xc1, hc1, sp11))
+    tail_one(False)([4, 5, 14, 15])
+    loop(0, 8, 8, tail_one(True))
     first_one(False)([5, 14])
-    loop(0, 8, 2, first_one(True))
-    loop(0, 8, 2, back_zero)
-    loop(-1, 9, 2, first_zero)
+    loop(0, 8, 8, first_one(True))
+    loop(0, 8, 8, back_zero)
+    loop(-1, 9, 10, first_zero)
 
     for r in range(H):
         final_ref[:, r, :] = fin[(r + REACH) * 8 : (r + REACH) * 8 + 8, :W]
@@ -346,31 +342,35 @@
     )
 
 
-def finish(total_ref, d1_ref, d2_ref, d3_ref, gid_ref, u1_ref, u2_ref, u3_ref):
+def row_sums(parts):
+    return jnp.concatenate([jnp.sum(v * v, axis=1, keepdims=True) for v in parts], axis=0)
+
+
+def groups(d1_ref, d2_ref, d3_ref, gid_ref, choose_ref, below_ref):
+    group = lax.broadcasted_iota(jnp.int32, (128, 160), 0)
+    choose = jnp.where(gid_ref[...] == group, 1.0, 0.0).T
+    choose_ref[...] = choose
+    sums = jnp.sum(choose * row_sums((d1_ref[...], d2_ref[...], d3_ref[...])), axis=0, keepdims=True)
+    below_ref[...] = jnp.sqrt(sums + 1e-06)
+
+
+def finish(total_ref, d1_ref, d2_ref, d3_ref, choose_ref, below_ref, u1_ref, u2_ref, u3_ref):
     t = [total_ref[k * 64 : k * 64 + 64, :] for k in range(6)]
     two = jnp.concatenate([*t[:4], t[4][:, :64], t[5][:, 9:10]], axis=1)
     one = jnp.concatenate([t[4][:, 64:], t[5][:, :8], t[5][:, 8:9]], axis=1)
     three = jnp.concatenate([t[5][:32, 64:], t[5][:32, 10:11]], axis=1)
-
-    def row_sums(parts):
-        return jnp.concatenate([jnp.sum(v * v, axis=1, keepdims=True) for v in parts], axis=0)
-
     grads = (one, two, three)
-    dirs = (d1_ref[...], d2_ref[...], d3_ref[...])
     norm = jnp.sqrt(jnp.sum(row_sums(grads), axis=0, keepdims=True))
     factor = 1.0 / jnp.maximum(norm, 1.0)
     clipped = [v * factor for v in grads]
-    group = lax.broadcasted_iota(jnp.int32, (160, 128), 1)
-    choose = jnp.where(gid_ref[...] == group, 1.0, 0.0)
-    clip_groups = jnp.sum(choose * row_sums(clipped), axis=0, keepdims=True)
-    dir_groups = jnp.sum(choose * row_sums(dirs), axis=0, keepdims=True)
-    ratios = jnp.sqrt(clip_groups) / jnp.sqrt(dir_groups + 1e-06)
+    choose = choose_ref[...]
+    ratios = jnp.sqrt(jnp.sum(choose * row_sums(clipped), axis=0, keepdims=True)) / below_ref[...]
     row_ratio = jnp.sum(choose * ratios, axis=1, keepdims=True)
     scaling = math.sqrt(PARAMS)
     at = 0
-    for ref, v, d in zip((u1_ref, u2_ref, u3_ref), clipped, dirs):
+    for ref, v, d_ref in zip((u1_ref, u2_ref, u3_ref), clipped, (d1_ref, d2_ref, d3_ref)):
         n = v.shape[0]
-        ref[...] = scaling * (v + row_ratio[at : at + n] * d)
+        ref[...] = scaling * (v + row_ratio[at : at + n] * d_ref[...])
         at += n
 
 
@@ -378,12 +378,12 @@
     return jax.ShapeDtypeStruct(dims, dtype)
 
 
-def kernel(body, outs, cost, **more):
+def kernel(body, outs, cost, mib, **more):
     return pl.pallas_call(
         body,
         out_shape=outs,
         cost_estimate=pl.CostEstimate(flops=cost, bytes_accessed=cost, transcendentals=0),
-        compiler_params=pltpu.CompilerParams(vmem_limit_bytes=60 * 2**20),
+        compiler_params=pltpu.CompilerParams(vmem_limit_bytes=mib * 2**20),
         **more,
     )
 
@@ -408,15 +408,7 @@
 
 
 def per_device(init, target, mask, one, two, head, d1, d2, d3, gid):
-    place = jnp.stack(
-        [
-            lax.axis_index("gx") * H,
-            lax.axis_index(GY) * W,
-            lax.axis_size("gx") * H,
-            lax.axis_size(GY) * W,
-        ]
-    ).astype(jnp.int32)
-    to_low, to_high = kernel(pack_rows, [shape((72, W))] * 2, 10**5)(init, target, mask)
+    to_low, to_high = kernel(pack_rows, [shape((72, W))] * 2, 10**5, 4)(init, target, mask)
     below, above = exchange(to_high, to_low, "gx")
     weights = kernel(
         prepare,
@@ -425,8 +417,12 @@
             shape((C, 576), BF), shape((24, 192), BF), shape((160, 128)),
         ],
         10**6,
+        8,
     )(one, two, head)
-    to_left, to_right = kernel(pack_cols, [shape((160, 128))] * 2, 10**5)(
+    choose, below_ratio = kernel(groups, [shape((160, 128)), shape((1, 128))], 10**6, 8)(
+        d1, d2, d3, gid.reshape(1, -1)
+    )
+    to_left, to_right = kernel(pack_cols, [shape((160, 128))] * 2, 10**5, 4)(
         init, target, mask, below, above
     )
     from_left, from_right = exchange(to_right, to_left, GY)
@@ -434,13 +430,11 @@
     def rows(size, dtype=F32):
         return pltpu.VMEM((20 * size, PITCH), dtype)
 
-    vmem = pl.BlockSpec(memory_space=pltpu.VMEM)
     final, grad = kernel(
         main,
         [shape((LEV, H, W)), shape((384, 128))],
         10**7,
-        in_specs=[pl.BlockSpec(memory_space=pltpu.SMEM)] + [vmem] * 14,
-        out_specs=[vmem] * 2,
+        40,
         scratch_shapes=[
             rows(24), rows(24), rows(8), rows(8), rows(192, BF), rows(192, BF), rows(64, BF),
             rows(64), rows(64), rows(64), rows(32), rows(192, BF), rows(192, BF), rows(64, BF),
@@ -448,10 +442,10 @@
             pltpu.VMEM((64, 128), F32), pltpu.VMEM((64, 128), F32), pltpu.VMEM((32, 128), F32),
             pltpu.VMEM((64, 72), F32), pltpu.VMEM((64, 576), F32), pltpu.VMEM((32, 64), F32),
         ],
-    )(place, init, target, mask, below, above, from_left, from_right, *weights)
+    )(init, target, mask, below, above, from_left, from_right, *weights)
     total = total_of(grad)
-    u1, u2, u3 = kernel(finish, [shape(one.shape), shape(two.shape), shape(head.shape)], 10**6)(
-        total, d1, d2, d3, gid.reshape(-1, 1)
+    u1, u2, u3 = kernel(finish, [shape(one.shape), shape(two.shape), shape(head.shape)], 10**6, 8)(
+        total, d1, d2, d3, choose, below_ratio
     )
     return final, u1, u2, u3
 

time: 97.8 us -> 79.7 us (0.81)
  Pallas kernels: 30.7 us -> 11 us
  waiting for transfers between devices: 11.4 us -> 13.6 us
    pallas_call x3 -> x4, Pallas kernels: 26.1 us -> 9.12 us  [the longest x1 8.66 us: per_device(): kernel(main, [shape((LEV, H, W)), shape((384, 128))], 10 ** 7, 40, scratc...]
    ppermute x2, waiting for transfers between devices: 5.37 us -> 7.03 us  [exchange(): lax.ppermute(backward, axis, back)]
    pallas_call x1, Pallas kernels: 2.22 us -> 0.66 us  [per_device(): kernel(prepare, [shape((C, 72), BF), shape((C, 576), BF), shape((K, C), B...]
    pallas_call x1, Pallas kernels: 2.36 us -> 1.26 us  [per_device(): kernel(finish, [shape(one.shape), shape(two.shape), shape(head.shape)], 1...]
    unnamed x12 -> x26, local copies, waits for them, and re-layouts: 2.62 us -> 3.06 us
  transfers between devices with their start and end apart: 5 -> 5, of which waited for: 3 -> 4; matrix products, arithmetic and copies ran while one was open for 1% -> 0% of each run, Pallas kernels for 2% -> 1%
where the time goes in v1:
time: 79.7 us; the launch traced here: 79.1 us
  blocking collectives  33.3 us (42%)
  starting transfers between devices  16.5 us (21%)
  waiting for transfers between devices  13.6 us (17%)
  Pallas kernels  11 us (14%)
  local copies, waits for them, and re-layouts  3.76 us (5%)
  between operations  0.83 us (1%)
    all_to_all x1, blocking collectives, total_of(): own = jnp.sum(lax.all_to_all(copies, far, 0, 0, tiled=True), axis=0)  18.6 us
    all_to_all x1, blocking collectives, total_of(): own = jnp.sum(lax.all_to_all(pieces, near, 0, 0, tiled=True), axis=0)  14.8 us
    ppermute x2, starting transfers between devices, exchange(): lax.ppermute(forward, axis, ahead)  9.52 us
    pallas_call x1, Pallas kernels, per_device(): kernel(main, [shape((LEV, H, W)), shape((384, 128))], 10 ** 7, 40, scratc...  8.66 us
    ppermute x2, waiting for transfers between devices, exchange(): lax.ppermute(backward, axis, back)  7.03 us
    all_to_all x1, waiting for transfers between devices, total_of(): return lax.all_to_all(copies, near, 0, 0, tiled=True).reshape(grad.shape)  6.47 us
    all_to_all x1, starting transfers between devices, total_of(): return lax.all_to_all(copies, near, 0, 0, tiled=True).reshape(grad.shape)  3.65 us
    ppermute x2, starting transfers between devices, exchange(): lax.ppermute(backward, axis, back)  3.34 us
  transfers between devices with their start and end apart: 5, of which 4 were waited for; matrix products, arithmetic and copies ran while one was open for 0% of the time, Pallas kernels for 1%

profile of v1, /device:TPU:1, one launch (start us, length us, event | category | flops | bytes accessed | tf_op | source)
XLA Modules:
  0.0 79.1 jit_solution(797726645492868822)
XLA Ops:
  0.6 0.0 copy-start.1
  0.6 0.8 %copy-done.1 = f32[8,8,256]{2,1,0:T(8,128)S(1)} copy-done((f32[8,8,256]{2,1,0:T(8,128)S(1)}, f32[8,8,256]{2,1,0:T(8,128)}, u32[]{:S(2)}) %copy-start.1) | copy-done | bytes 65560
  1.5 0.0 copy-start.3
  1.5 0.8 %copy-done.3 = f32[8,8,256]{2,1,0:T(8,128)S(1)} copy-done((f32[8,8,256]{2,1,0:T(8,128)S(1)}, f32[8,8,256]{2,1,0:T(8,128)}, u32[]{:S(2)}) %copy-start.3) | copy-done | bytes 65560
  2.3 0.0 copy-start.7
  2.3 0.7 copy-done.7
  3.1 0.0 copy-start.5
  3.1 4.5 %collective-permute-start = (f32[72,256]{1,0:T(8,128)S(1)}, f32[72,256]{1,0:T(8,128)S(1)}, u32[]{:S(2)}, u32[]{:S(2)}) collective-permute-start(f32[72,256]{1,0:T(8,128)S(1)} %get-tuple-element.22), channel_id=1, source_target_pairs={{0,32},{32,64},{64,96},{96,128},{128,160},{160,192},{192,224},{1,3... | collective-permute-start | bytes 221192 | tf_op jit(solution)/shard_map/ppermute | solution.py:395
  7.6 0.0 copy-start.10
  7.6 0.0 copy-start.11
  7.6 1.3 %collective-permute-start.1 = (f32[72,256]{1,0:T(8,128)S(1)}, f32[72,256]{1,0:T(8,128)S(1)}, u32[]{:S(2)}, u32[]{:S(2)}) collective-permute-start(f32[72,256]{1,0:T(8,128)S(1)} %get-tuple-element.23), channel_id=1, source_target_pairs={{32,0},{64,32},{96,64},{128,96},{160,128},{192,160},{224,192},{33,... | collective-permute-start | bytes 221192 | tf_op jit(solution)/shard_map/ppermute | solution.py:395
  8.9 0.1 collective-permute-done.below_ref
  9.0 3.9 %collective-permute-done.1.above_ref = f32[72,256]{1,0:T(8,128)S(1)} collective-permute-done((f32[72,256]{1,0:T(8,128)S(1)}, f32[72,256]{1,0:T(8,128)S(1)}, u32[]{:S(2)}, u32[]{:S(2)}) %collective-permute-start.1) | collective-permute-done | bytes 73760 | tf_op jit(solution)/shard_map/ppermute | solution.py:395
  12.9 0.1 shard_map.130
  13.0 5.0 %collective-permute-start.2 = (f32[160,128]{1,0:T(8,128)S(1)}, f32[160,128]{1,0:T(8,128)S(1)}, u32[]{:S(2)}, u32[]{:S(2)}) collective-permute-start(f32[160,128]{1,0:T(8,128)S(1)} %get-tuple-element.24), channel_id=1, source_target_pairs={{0,1},{1,2},{2,3},{3,4},{4,5},{5,6},{6,7},{7,8},{8,9},{9,10},{10,1... | collective-permute-start | bytes 245768 | tf_op jit(solution)/shard_map/ppermute | solution.py:395
  18.0 0.0 copy-start.2
  18.1 0.0 copy-start.4
  18.1 2.1 %collective-permute-start.3 = (f32[160,128]{1,0:T(8,128)S(1)}, f32[160,128]{1,0:T(8,128)S(1)}, u32[]{:S(2)}, u32[]{:S(2)}) collective-permute-start(f32[160,128]{1,0:T(8,128)S(1)} %get-tuple-element.25), channel_id=1, source_target_pairs={{1,0},{2,1},{3,2},{4,3},{5,4},{6,5},{7,6},{8,7},{9,8},{10,9},{11,1... | collective-permute-start | bytes 245768 | tf_op jit(solution)/shard_map/ppermute | solution.py:395
  20.1 0.0 copy-done.5
  20.1 0.0 copy-done.10
  20.1 0.0 copy-done.11
  20.2 0.7 shard_map.131
  20.8 0.0 copy-start.8
  20.8 0.0 collective-permute-done.2.fromleft_ref
  20.8 3.1 %collective-permute-done.3.fromright_ref = f32[160,128]{1,0:T(8,128)S(1)} collective-permute-done((f32[160,128]{1,0:T(8,128)S(1)}, f32[160,128]{1,0:T(8,128)S(1)}, u32[]{:S(2)}, u32[]{:S(2)}) %collective-permute-start.3) | collective-permute-done | bytes 81952 | tf_op jit(solution)/shard_map/ppermute | solution.py:395
  24.0 0.0 copy-done.2
  24.0 0.0 copy-done.4
  24.0 0.0 copy-done.8
  24.0 8.7 %shard_map.132 = (f32[8,8,256]{2,1,0:T(8,128)}, f32[384,128]{1,0:T(8,128)S(1)}) custom-call(f32[8,8,256]{2,1,0:T(8,128)S(1)} %copy-done.2, f32[8,8,256]{2,1,0:T(8,128)S(1)} %copy-done.4, s32[8,256]{1,0:T(8,128)S(1)} %copy-done.8, f32[72,256]{1,0:T(8,128)S(1)} %collective-permute-done.below_ref, f32[72,256]{1,0:T(8,128)S(1)} %collective-permute-done.1.above_ref, ...), custom_call_target="tpu_custom_call" | custom-call | flops 10000000 | bytes 10000000 | tf_op jit(solution)/shard_map/pallas_call | solution.py:433
  32.6 14.8 %all_to_all.15 = f32[16,24,128]{2,1,0:T(8,128)S(1)} all-to-all(f32[16,24,128]{2,1,0:T(8,128)S(1)} %bitcast.4), channel_id=1, replica_groups=mesh['gx'=8,'gy_0'=4,'gy_1'=4,'gy_2'=2] {'gy_0','gy_1'}, dimensions={0} | all-to-all | bytes 393216 | tf_op jit(solution)/shard_map/all_to_all | solution.py:402
  47.5 18.6 %all_to_all.16 = f32[16,24,128]{2,1,0:T(8,128)S(1)} all-to-all(f32[16,24,128]{2,1,0:T(8,128)S(1)} %broadcast_in_dim.6), channel_id=1, replica_groups=mesh['gx'=8,'gy_0'=4,'gy_1'=4,'gy_2'=2] {'gx','gy_2'}, dimensions={0} | all-to-all | bytes 393216 | tf_op jit(solution)/shard_map/all_to_all | solution.py:405
  66.1 0.7 broadcast_in_dim.7
  66.7 0.0 copy-start
  66.7 0.0 copy-start.6
  66.7 0.0 copy-start.9
  66.7 3.7 %all-to-all-start.2 = ((f32[16,24,128]{2,1,0:T(8,128)}), f32[16,24,128]{2,1,0:T(8,128)S(1)}, u32[]{:S(2)}, u32[]{:S(2)}) async-start(f32[16,24,128]{2,1,0:T(8,128)} %broadcast_in_dim.7), calls=%async_computation.2 | async-start | bytes 393216 | tf_op jit(solution)/shard_map/all_to_all | solution.py:407
  70.4 0.0 copy-start.12
  70.4 0.0 copy-done
  70.4 0.0 copy-done.6
  70.4 0.0 copy-done.9
  70.4 0.6 copy-done.12
  71.1 0.3 shard_map.133
  71.4 6.5 %all-to-all-done.2 = f32[16,24,128]{2,1,0:T(8,128)S(1)} async-done(((f32[16,24,128]{2,1,0:T(8,128)}), f32[16,24,128]{2,1,0:T(8,128)S(1)}, u32[]{:S(2)}, u32[]{:S(2)}) %all-to-all-start.2) | async-done | bytes 196640 | tf_op jit(solution)/shard_map/all_to_all | solution.py:407
  77.8 1.3 %shard_map.134 = (f32[64,73]{1,0:T(8,128)}, f32[64,577]{1,0:T(8,128)}, f32[32,65]{1,0:T(8,128)}) custom-call(f32[384,128]{1,0:T(8,128)S(1)} %bitcast.3, f32[64,73]{1,0:T(8,128)S(1)} %copy-done.6, f32[64,577]{1,0:T(8,128)S(1)} %copy-done, f32[32,65]{1,0:T(8,128)S(1)} %copy-done.9, f32[160,128]{1,0:T(8,128)S(1)} %get-tuple-element.35.choose_ref, ...), custom_call_target="tpu_custom_call" | custom-call | flops 1000000 | bytes 1000000 | tf_op jit(solution)/shard_map/pallas_call | solution.py:447
  (4 shorter events, 0.1 us)
Async XLA Ops:
  0.6 0.8 %copy-start.1 = (f32[8,8,256]{2,1,0:T(8,128)S(1)}, f32[8,8,256]{2,1,0:T(8,128)}, u32[]{:S(2)}) copy-start(f32[8,8,256]{2,1,0:T(8,128)} %init_ref.5) | copy-start | bytes 196612
  1.5 0.8 %copy-start.3 = (f32[8,8,256]{2,1,0:T(8,128)S(1)}, f32[8,8,256]{2,1,0:T(8,128)}, u32[]{:S(2)}) copy-start(f32[8,8,256]{2,1,0:T(8,128)} %target_ref.5) | copy-start | bytes 196612
  2.3 0.7 copy-start.7
  3.1 17.1 %copy-start.5 = (f32[64,577]{1,0:T(8,128)S(1)}, f32[64,577]{1,0:T(8,128)}, u32[]{:S(2)}) copy-start(f32[64,577]{1,0:T(8,128)} %two_ref.1) | copy-start | bytes 443140
  3.1 5.9 %collective-permute-start = (f32[72,256]{1,0:T(8,128)S(1)}, f32[72,256]{1,0:T(8,128)S(1)}, u32[]{:S(2)}, u32[]{:S(2)}) collective-permute-start(f32[72,256]{1,0:T(8,128)S(1)} %get-tuple-element.22), channel_id=1, source_target_pairs={{0,32},{32,64},{64,96},{96,128},{128,160},{160,192},{192,224},{1,3... | collective-permute-start | bytes 221192 | tf_op jit(solution)/shard_map/ppermute | solution.py:395
  7.6 12.6 %copy-start.10 = (f32[64,73]{1,0:T(8,128)S(1)}, f32[64,73]{1,0:T(8,128)}, u32[]{:S(2)}) copy-start(f32[64,73]{1,0:T(8,128)} %one_ref.1) | copy-start | bytes 56068
  7.6 12.6 %copy-start.11 = (f32[32,65]{1,0:T(8,128)S(1)}, f32[32,65]{1,0:T(8,128)}, u32[]{:S(2)}) copy-start(f32[32,65]{1,0:T(8,128)} %head_ref.1) | copy-start | bytes 24964
  7.6 5.3 %collective-permute-start.1 = (f32[72,256]{1,0:T(8,128)S(1)}, f32[72,256]{1,0:T(8,128)S(1)}, u32[]{:S(2)}, u32[]{:S(2)}) collective-permute-start(f32[72,256]{1,0:T(8,128)S(1)} %get-tuple-element.23), channel_id=1, source_target_pairs={{32,0},{64,32},{96,64},{128,96},{160,128},{192,160},{224,192},{33,... | collective-permute-start | bytes 221192 | tf_op jit(solution)/shard_map/ppermute | solution.py:395
  13.0 7.8 %collective-permute-start.2 = (f32[160,128]{1,0:T(8,128)S(1)}, f32[160,128]{1,0:T(8,128)S(1)}, u32[]{:S(2)}, u32[]{:S(2)}) collective-permute-start(f32[160,128]{1,0:T(8,128)S(1)} %get-tuple-element.24), channel_id=1, source_target_pairs={{0,1},{1,2},{2,3},{3,4},{4,5},{5,6},{6,7},{7,8},{8,9},{9,10},{10,1... | collective-permute-start | bytes 245768 | tf_op jit(solution)/shard_map/ppermute | solution.py:395
  18.0 5.9 %copy-start.2 = (f32[8,8,256]{2,1,0:T(8,128)S(1)}, f32[8,8,256]{2,1,0:T(8,128)}, u32[]{:S(2)}) copy-start(f32[8,8,256]{2,1,0:T(8,128)} %init_ref.5) | copy-start | bytes 196612
  18.1 5.9 %copy-start.4 = (f32[8,8,256]{2,1,0:T(8,128)S(1)}, f32[8,8,256]{2,1,0:T(8,128)}, u32[]{:S(2)}) copy-start(f32[8,8,256]{2,1,0:T(8,128)} %target_ref.5) | copy-start | bytes 196612
  18.1 5.9 %collective-permute-start.3 = (f32[160,128]{1,0:T(8,128)S(1)}, f32[160,128]{1,0:T(8,128)S(1)}, u32[]{:S(2)}, u32[]{:S(2)}) collective-permute-start(f32[160,128]{1,0:T(8,128)S(1)} %get-tuple-element.25), channel_id=1, source_target_pairs={{1,0},{2,1},{3,2},{4,3},{5,4},{6,5},{7,6},{8,7},{9,8},{10,9},{11,1... | collective-permute-start | bytes 245768 | tf_op jit(solution)/shard_map/ppermute | solution.py:395
  20.8 3.1 %copy-start.8 = (s32[8,256]{1,0:T(8,128)S(1)}, s32[8,256]{1,0:T(8,128)}, u32[]{:S(2)}) copy-start(s32[8,256]{1,0:T(8,128)} %mask_ref.5) | copy-start | bytes 24580
  66.7 3.7 %copy-start = (f32[64,577]{1,0:T(8,128)S(1)}, f32[64,577]{1,0:T(8,128)}, u32[]{:S(2)}) copy-start(f32[64,577]{1,0:T(8,128)} %d2_ref.3) | copy-start | bytes 443140
  66.7 3.7 %copy-start.6 = (f32[64,73]{1,0:T(8,128)S(1)}, f32[64,73]{1,0:T(8,128)}, u32[]{:S(2)}) copy-start(f32[64,73]{1,0:T(8,128)} %d1_ref.3) | copy-start | bytes 56068
  66.7 3.7 %copy-start.9 = (f32[32,65]{1,0:T(8,128)S(1)}, f32[32,65]{1,0:T(8,128)}, u32[]{:S(2)}) copy-start(f32[32,65]{1,0:T(8,128)} %d3_ref.3) | copy-start | bytes 24964
  66.7 11.1 %all-to-all-start.2 = ((f32[16,24,128]{2,1,0:T(8,128)}), f32[16,24,128]{2,1,0:T(8,128)S(1)}, u32[]{:S(2)}, u32[]{:S(2)}) async-start(f32[16,24,128]{2,1,0:T(8,128)} %broadcast_in_dim.7), calls=%async_computation.2 | async-start | bytes 393216 | tf_op jit(solution)/shard_map/all_to_all | solution.py:407
  70.4 0.7 copy-start.12

commit v2 on v1

--- a/solution.py
+++ b/solution.py
@@ -73,20 +73,33 @@
 
 def pack_cols(init_ref, target_ref, mask_ref, below_ref, above_ref, left_ref, right_ref):
     lane = lax.broadcasted_iota(jnp.int32, (8, 128), 1)
+    zero = jnp.zeros((8, 128), F32)
+    packed = [zero] * 6
     for r in range(-REACH, H + REACH):
         field, wet, target = row_parts(r, init_ref, target_ref, mask_ref, below_ref, above_ref)
         wet = jnp.broadcast_to(wet, (8, W))
-        a = jnp.where(lane < 32, field[:, :128], turned(wet[:, :128], 32))
-        b = jnp.where(lane >= 96, field[:, 128:], turned(wet[:, 128:], -32))
-        if target is not None:
-            a = jnp.where(lane < 64, a, turned(target[:, :128], 64))
-            b = jnp.where(lane >= 64, b, turned(target[:, 128:], -64))
-        at = (r + REACH) * 8
-        left_ref[at : at + 8, :] = a
-        right_ref[at : at + 8, :] = b
-
-
-def prepare(one_ref, two_ref, head_ref, w1_ref, w2_ref, w3_ref, w3t_ref, w2t_ref, w1t_ref, bias_ref):
+        at, by = divmod(r + REACH, 8)
+        inner = lane - 16 * by
+        for side, first, moves in ((0, 0, (0, 6, 10)), (3, 128, (6, 10, 12))):
+            move = [by * 16 + m for m in moves]
+            v = turned(field[:, first : first + 128], move[0])
+            v = jnp.where(inner < 6, v, turned(wet[:, first : first + 128], move[1]))
+            if target is not None:
+                v = jnp.where(inner < 10, v, turned(target[:, first : first + 128], move[2]))
+            packed[side + at] = jnp.where((inner >= 0) & (inner < 12), v, packed[side + at])
+    for k in range(3):
+        left_ref[k * 8 : k * 8 + 8, :] = packed[k]
+        right_ref[k * 8 : k * 8 + 8, :] = packed[3 + k]
+
+
+def row_sums(parts):
+    return jnp.concatenate([jnp.sum(v * v, axis=1, keepdims=True) for v in parts], axis=0)
+
+
+def prepare(
+    one_ref, two_ref, head_ref, d1_ref, d2_ref, d3_ref, gid_ref,
+    w1_ref, w2_ref, w3_ref, w3t_ref, w2t_ref, w1t_ref, bias_ref, choose_ref, below_ref,
+):
     one, two, head = one_ref[...], two_ref[...], head_ref[...]
     w1_ref[...] = one[:, : 9 * LEV].astype(BF)
     w2_ref[...] = two[:, : 9 * C].astype(BF)
@@ -108,6 +121,11 @@
     bias_ref[0:64, :] = jnp.broadcast_to(one[:, 9 * LEV :], (64, 128))
     bias_ref[64:128, :] = jnp.broadcast_to(two[:, 9 * C :], (64, 128))
     bias_ref[128:160, :] = jnp.broadcast_to(head[:, C:], (32, 128))
+    group = lax.broadcasted_iota(jnp.int32, (128, 160), 0)
+    choose = jnp.where(gid_ref[...] == group, 1.0, 0.0).T
+    choose_ref[...] = choose
+    sums = jnp.sum(choose * row_sums((d1_ref[...], d2_ref[...], d3_ref[...])), axis=0, keepdims=True)
+    below_ref[...] = jnp.sqrt(sums + 1e-06)
 
 
 def lanes(parts):
@@ -130,26 +148,29 @@
     w1_ref, w2_ref, w3_ref, w3t_ref, w2t_ref, w1t_ref, bias_ref,
     final_ref, grad_ref,
     xc0, xc1, wet_s, tgt, hc0, hc1, h2s, sp10, sp11, sp2, wd, ec0, ec1, e1s, rem, up, down, fin,
-    b1g, b2g, b3g, g1, g2, g3,
+    b1g, b2g, b3g, g1, g2, g3, final_v, sem,
 ):
     lane = lax.broadcasted_iota(jnp.int32, (8, 128), 1)
     zero = jnp.zeros((8, 128), F32)
     for r in range(-REACH, H + REACH):
         field, wet, target = row_parts(r, init_ref, target_ref, mask_ref, below_ref, above_ref)
         at = (r + REACH) * 8
-        fl, fr = fromleft_ref[at : at + 8, :], fromright_ref[at : at + 8, :]
-
-        def rim(by):
-            right, left = (turned(fr, -by), turned(fl, by)) if by else (fr, fl)
-            return jnp.where(lane < 16, right, jnp.where(lane >= 112, left, zero))
-
-        row = jnp.concatenate([field, rim(0)], axis=1)
+        block, by = divmod(r + REACH, 8)
+        fl = fromleft_ref[block * 8 : block * 8 + 8, :]
+        fr = fromright_ref[block * 8 : block * 8 + 8, :]
+
+        def rim(first, width):
+            right = turned(fr, -(by * 16 + first))
+            left = turned(fl, -(by * 16 + first) - width)
+            return jnp.where(lane < width, right, jnp.where(lane >= 128 - width, left, zero))
+
+        row = jnp.concatenate([field, rim(0, 6)], axis=1)
         xc0[at * 3 : at * 3 + 24, :] = jnp.concatenate(
             [turned(row, 1), row, turned(row, -1)], axis=0
         )
-        wet_s[at : at + 8, :] = jnp.concatenate([jnp.broadcast_to(wet, (8, W)), rim(32)], axis=1)
+        wet_s[at : at + 8, :] = jnp.concatenate([jnp.broadcast_to(wet, (8, W)), rim(6, 4)], axis=1)
         if target is not None:
-            tgt[at : at + 8, :] = jnp.concatenate([target, rim(64)], axis=1)
+            tgt[at : at + 8, :] = jnp.concatenate([target, rim(10, 2)], axis=1)
     for ref in (b1g, b2g, b3g, g1, g2, g3):
         ref[...] = jnp.zeros(ref.shape, F32)
     for r in (4, 5, 14, 15):
@@ -319,13 +340,15 @@
     loop(-3, 11, 14, first_layer(xc1, hc1, sp11))
     tail_one(False)([4, 5, 14, 15])
     loop(0, 8, 8, tail_one(True))
+    for r in range(H):
+        final_v[:, r, :] = fin[(r + REACH) * 8 : (r + REACH) * 8 + 8, :W]
+    out = pltpu.make_async_copy(final_v, final_ref, sem)
+    out.start()
     first_one(False)([5, 14])
     loop(0, 8, 8, first_one(True))
     loop(0, 8, 8, back_zero)
     loop(-1, 9, 10, first_zero)
 
-    for r in range(H):
-        final_ref[:, r, :] = fin[(r + REACH) * 8 : (r + REACH) * 8 + 8, :W]
     for k in range(4):
         grad_ref[k * 64 : k * 64 + 64, :] = g2[:, k * 128 : k * 128 + 128]
     grad_ref[256:320, :] = jnp.concatenate([g2[:, 512:576], g1[:, 0:64]], axis=1)
@@ -340,18 +363,7 @@
         ],
         axis=1,
     )
-
-
-def row_sums(parts):
-    return jnp.concatenate([jnp.sum(v * v, axis=1, keepdims=True) for v in parts], axis=0)
-
-
-def groups(d1_ref, d2_ref, d3_ref, gid_ref, choose_ref, below_ref):
-    group = lax.broadcasted_iota(jnp.int32, (128, 160), 0)
-    choose = jnp.where(gid_ref[...] == group, 1.0, 0.0).T
-    choose_ref[...] = choose
-    sums = jnp.sum(choose * row_sums((d1_ref[...], d2_ref[...], d3_ref[...])), axis=0, keepdims=True)
-    below_ref[...] = jnp.sqrt(sums + 1e-06)
+    out.wait()
 
 
 def finish(total_ref, d1_ref, d2_ref, d3_ref, choose_ref, below_ref, u1_ref, u2_ref, u3_ref):
@@ -396,36 +408,37 @@
 
 
 def total_of(grad):
-    near, far = ("gy_0", "gy_1"), ("gx", "gy_2")
+    near = ("gy_0", "gy_1")
     n = lax.axis_size(near)
     pieces = grad.reshape(n, -1, 128)
     own = jnp.sum(lax.all_to_all(pieces, near, 0, 0, tiled=True), axis=0)
-    m = lax.axis_size(far)
+    own = own + lax.ppermute(own, "gy_2", [(0, 1), (1, 0)])
+    m = lax.axis_size("gx")
     copies = jnp.broadcast_to(own, (m, *own.shape))
-    own = jnp.sum(lax.all_to_all(copies, far, 0, 0, tiled=True), axis=0)
+    own = jnp.sum(lax.all_to_all(copies, "gx", 0, 0, tiled=True), axis=0)
     copies = jnp.broadcast_to(own, (n, *own.shape))
     return lax.all_to_all(copies, near, 0, 0, tiled=True).reshape(grad.shape)
 
 
 def per_device(init, target, mask, one, two, head, d1, d2, d3, gid):
-    to_low, to_high = kernel(pack_rows, [shape((72, W))] * 2, 10**5, 4)(init, target, mask)
+    hbm = pl.BlockSpec(memory_space=pltpu.HBM)
+    vmem = pl.BlockSpec(memory_space=pltpu.VMEM)
+    to_low, to_high = kernel(pack_rows, [shape((72, W))] * 2, 10**5, 60)(init, target, mask)
     below, above = exchange(to_high, to_low, "gx")
-    weights = kernel(
+    to_left, to_right = kernel(pack_cols, [shape((24, 128))] * 2, 10**5, 4)(
+        init, target, mask, below, above
+    )
+    from_left, from_right = exchange(to_right, to_left, GY)
+    *weights, choose, below_ratio = kernel(
         prepare,
         [
             shape((C, 72), BF), shape((C, 576), BF), shape((K, C), BF), shape((C, K), BF),
             shape((C, 576), BF), shape((24, 192), BF), shape((160, 128)),
+            shape((160, 128)), shape((1, 128)),
         ],
         10**6,
         8,
-    )(one, two, head)
-    choose, below_ratio = kernel(groups, [shape((160, 128)), shape((1, 128))], 10**6, 8)(
-        d1, d2, d3, gid.reshape(1, -1)
-    )
-    to_left, to_right = kernel(pack_cols, [shape((160, 128))] * 2, 10**5, 4)(
-        init, target, mask, below, above
-    )
-    from_left, from_right = exchange(to_right, to_left, GY)
+    )(one, two, head, d1, d2, d3, gid.reshape(1, -1))
 
     def rows(size, dtype=F32):
         return pltpu.VMEM((20 * size, PITCH), dtype)
@@ -435,12 +448,15 @@
         [shape((LEV, H, W)), shape((384, 128))],
         10**7,
         40,
+        in_specs=[vmem] * 14,
+        out_specs=[hbm, vmem],
         scratch_shapes=[
             rows(24), rows(24), rows(8), rows(8), rows(192, BF), rows(192, BF), rows(64, BF),
             rows(64), rows(64), rows(64), rows(32), rows(192, BF), rows(192, BF), rows(64, BF),
             rows(8), rows(8), rows(8), rows(8),
             pltpu.VMEM((64, 128), F32), pltpu.VMEM((64, 128), F32), pltpu.VMEM((32, 128), F32),
             pltpu.VMEM((64, 72), F32), pltpu.VMEM((64, 576), F32), pltpu.VMEM((32, 64), F32),
+            pltpu.VMEM((LEV, H, W), F32), pltpu.SemaphoreType.DMA,
         ],
     )(init, target, mask, below, above, from_left, from_right, *weights)
     total = total_of(grad)

time: 79.7 us -> 75.3 us (0.945)
  blocking collectives: 33.3 us -> 40.3 us
  waiting for transfers between devices: 13.6 us -> 6.61 us
  starting transfers between devices: 16.5 us -> 12.8 us
  local copies, waits for them, and re-layouts: 3.76 us -> 0.98 us
  Pallas kernels: 11 us -> 12.7 us
    all_to_all x1 -> x2, blocking collectives: 18.6 us -> 25.5 us  [the longest x1 15.3 us: total_of(): own = jnp.sum(lax.all_to_all(copies, 'gx', 0, 0, tiled=True), axis=0)]
    all_to_all x1 -> x0, waiting for transfers between devices: 6.47 us -> none  [total_of(): return lax.all_to_all(copies, near, 0, 0, tiled=True).reshape(grad.shape)]
    all_to_all x1 -> x0, starting transfers between devices: 3.65 us -> none  [total_of(): return lax.all_to_all(copies, near, 0, 0, tiled=True).reshape(grad.shape)]
    unnamed x26 -> x20, local copies, waits for them, and re-layouts: 3.06 us -> 0.96 us
    ppermute x2, waiting for transfers between devices: 7.03 us -> 5.07 us  [exchange(): lax.ppermute(backward, axis, back)]
    pallas_call x4 -> x3, Pallas kernels: 9.12 us -> 10.6 us  [the longest x1 8.81 us: per_device(): kernel(main, [shape((LEV, H, W)), shape((384, 128))], 10 ** 7, 40, in_spe...]
    ppermute x0 -> x1, waiting for transfers between devices: none -> 1.16 us  [total_of(): own = own + lax.ppermute(own, 'gy_2', [(0, 1), (1, 0)])]
where the time goes in v2:
time: 75.3 us; the launch traced here: 74.3 us
  blocking collectives  40.3 us (54%)
  starting transfers between devices  12.8 us (17%)
  Pallas kernels  12.7 us (17%)
  waiting for transfers between devices  6.61 us (9%)
  local copies, waits for them, and re-layouts  0.98 us (1%)
  between operations  0.84 us (1%)
    all_to_all x1, blocking collectives, total_of(): own = jnp.sum(lax.all_to_all(copies, 'gx', 0, 0, tiled=True), axis=0)  15.3 us
    all_to_all x1, blocking collectives, total_of(): own = jnp.sum(lax.all_to_all(pieces, near, 0, 0, tiled=True), axis=0)  14.8 us
    all_to_all x1, blocking collectives, total_of(): return lax.all_to_all(copies, near, 0, 0, tiled=True).reshape(grad.shape)  10.2 us
    ppermute x2, starting transfers between devices, exchange(): lax.ppermute(forward, axis, ahead)  9.5 us
    pallas_call x1, Pallas kernels, per_device(): kernel(main, [shape((LEV, H, W)), shape((384, 128))], 10 ** 7, 40, in_spe...  8.81 us
    ppermute x2, waiting for transfers between devices, exchange(): lax.ppermute(backward, axis, back)  5.07 us
    ppermute x2, starting transfers between devices, exchange(): lax.ppermute(backward, axis, back)  3.21 us
    pallas_call x1, Pallas kernels, per_device(): kernel(pack_rows, [shape((72, W))] * 2, 10 ** 5, 60)(init, target, mask)  1.6 us
  transfers between devices with their start and end apart: 5, of which 4 were waited for; matrix products, arithmetic and copies ran while one was open for 0% of the time, Pallas kernels for 1%

profile of v2, /device:TPU:1, one launch (start us, length us, event | category | flops | bytes accessed | tf_op | source)
XLA Modules:
  0.0 74.3 jit_solution(1479995174340609428)
XLA Ops:
  0.6 0.0 copy-start.2
  0.6 0.0 copy-start.1
  0.7 0.0 copy-start.5
  0.7 1.6 %shard_map.129 = (f32[72,256]{1,0:T(8,128)}, f32[72,256]{1,0:T(8,128)}) custom-call(f32[8,8,256]{2,1,0:T(8,128)} %init_ref.5, f32[8,8,256]{2,1,0:T(8,128)} %target_ref.5, s32[8,256]{1,0:T(8,128)} %mask_ref.5), custom_call_target="tpu_custom_call" | custom-call | flops 100000 | bytes 100000 | tf_op jit(solution)/shard_map/pallas_call | solution.py:426
  2.3 0.0 copy-start
  2.3 4.5 %collective-permute-start = (f32[72,256]{1,0:T(8,128)}, f32[72,256]{1,0:T(8,128)S(1)}, u32[]{:S(2)}, u32[]{:S(2)}) collective-permute-start(f32[72,256]{1,0:T(8,128)} %get-tuple-element.22), channel_id=1, source_target_pairs={{0,32},{32,64},{64,96},{96,128},{128,160},{160,192},{192,224},{1,3... | collective-permute-start | bytes 221192 | tf_op jit(solution)/shard_map/ppermute | solution.py:407
  6.8 0.0 copy-start.4
  6.8 0.0 copy-start.7
  6.8 1.3 %collective-permute-start.1 = (f32[72,256]{1,0:T(8,128)}, f32[72,256]{1,0:T(8,128)S(1)}, u32[]{:S(2)}, u32[]{:S(2)}) collective-permute-start(f32[72,256]{1,0:T(8,128)} %get-tuple-element.23), channel_id=1, source_target_pairs={{32,0},{64,32},{96,64},{128,96},{160,128},{192,160},{224,192},{33,... | collective-permute-start | bytes 221192 | tf_op jit(solution)/shard_map/ppermute | solution.py:407
  8.1 0.4 collective-permute-done.below_ref
  8.5 3.8 %collective-permute-done.1.above_ref = f32[72,256]{1,0:T(8,128)S(1)} collective-permute-done((f32[72,256]{1,0:T(8,128)}, f32[72,256]{1,0:T(8,128)S(1)}, u32[]{:S(2)}, u32[]{:S(2)}) %collective-permute-start.1) | collective-permute-done | bytes 73760 | tf_op jit(solution)/shard_map/ppermute | solution.py:407
  12.3 0.0 copy-done.2
  12.3 0.0 copy-done.1
  12.3 0.0 copy-done.5
  12.3 0.0 copy-start.6
  12.3 0.0 copy-start.8
  12.3 0.2 shard_map.130
  12.5 5.0 %collective-permute-start.2 = (f32[24,128]{1,0:T(8,128)S(1)}, f32[24,128]{1,0:T(8,128)S(1)}, u32[]{:S(2)}, u32[]{:S(2)}) collective-permute-start(f32[24,128]{1,0:T(8,128)S(1)} %get-tuple-element.24), channel_id=1, source_target_pairs={{0,1},{1,2},{2,3},{3,4},{4,5},{5,6},{6,7},{7,8},{8,9},{9,10},{10,1... | collective-permute-start | bytes 36872 | tf_op jit(solution)/shard_map/ppermute | solution.py:407
  17.5 0.0 copy-start.9
  17.5 1.9 %collective-permute-start.3 = (f32[24,128]{1,0:T(8,128)S(1)}, f32[24,128]{1,0:T(8,128)S(1)}, u32[]{:S(2)}, u32[]{:S(2)}) collective-permute-start(f32[24,128]{1,0:T(8,128)S(1)} %get-tuple-element.25), channel_id=1, source_target_pairs={{1,0},{2,1},{3,2},{4,3},{5,4},{6,5},{7,6},{8,7},{9,8},{10,9},{11,1... | collective-permute-start | bytes 36872 | tf_op jit(solution)/shard_map/ppermute | solution.py:407
  19.5 0.0 copy-done
  19.5 0.0 copy-done.4
  19.5 0.0 copy-done.7
  19.5 0.0 copy-done.6
  19.5 0.0 copy-done.8
  19.5 0.0 copy-done.9
  19.5 0.0 copy-start.3
  19.5 0.9 %copy-done.3 = f32[64,577]{1,0:T(8,128)S(1)} copy-done((f32[64,577]{1,0:T(8,128)S(1)}, f32[64,577]{1,0:T(8,128)}, u32[]{:S(2)}) %copy-start.3) | copy-done | bytes 147736
  20.4 0.8 %shard_map.131 = (bf16[64,72]{1,0:T(8,128)(2,1)S(1)}, bf16[64,576]{1,0:T(8,128)(2,1)S(1)}, bf16[32,64]{1,0:T(8,128)(2,1)S(1)}, bf16[64,32]{1,0:T(8,128)(2,1)S(1)...) custom-call(f32[64,73]{1,0:T(8,128)S(1)} %copy-done.7, ...), custom_call_target="tpu_custom_call" | custom-call | flops 1000000 | bytes 1000000 | tf_op jit(solution)/shard_map/pallas_call | solution.py:432
  21.3 0.0 collective-permute-done.2.fromleft_ref
  21.3 1.3 %collective-permute-done.3.fromright_ref = f32[24,128]{1,0:T(8,128)S(1)} collective-permute-done((f32[24,128]{1,0:T(8,128)S(1)}, f32[24,128]{1,0:T(8,128)S(1)}, u32[]{:S(2)}, u32[]{:S(2)}) %collective-permute-start.3) | collective-permute-done | bytes 12320 | tf_op jit(solution)/shard_map/ppermute | solution.py:407
  22.5 8.8 %shard_map.132 = (f32[8,8,256]{2,1,0:T(8,128)}, f32[384,128]{1,0:T(8,128)S(1)}) custom-call(f32[8,8,256]{2,1,0:T(8,128)S(1)} %copy-done.1, f32[8,8,256]{2,1,0:T(8,128)S(1)} %copy-done.2, s32[8,256]{1,0:T(8,128)S(1)} %copy-done.5, f32[72,256]{1,0:T(8,128)S(1)} %collective-permute-done.below_ref, f32[72,256]{1,0:T(8,128)S(1)} %collective-permute-done.1.above_ref, ...), custom_call_target="tpu_custom_call" | custom-call | flops 10000000 | bytes 10000000 | tf_op jit(solution)/shard_map/pallas_call | solution.py:446
  31.4 14.8 %all_to_all.15 = f32[16,24,128]{2,1,0:T(8,128)S(1)} all-to-all(f32[16,24,128]{2,1,0:T(8,128)S(1)} %bitcast.4), channel_id=1, replica_groups=mesh['gx'=8,'gy_0'=4,'gy_1'=4,'gy_2'=2] {'gy_0','gy_1'}, dimensions={0} | all-to-all | bytes 393216 | tf_op jit(solution)/shard_map/all_to_all | solution.py:414
  46.2 0.1 collective-permute-start.4
  46.3 1.2 %collective-permute-done.4 = f32[24,128]{1,0:T(8,128)S(1)} collective-permute-done((f32[24,128]{1,0:T(8,128)S(1)}, f32[24,128]{1,0:T(8,128)S(1)}, u32[]{:S(2)}, u32[]{:S(2)}) %collective-permute-start.4) | collective-permute-done | bytes 12320 | tf_op jit(solution)/shard_map/ppermute | solution.py:415
  47.5 15.3 %all_to_all.16 = f32[8,24,128]{2,1,0:T(8,128)S(1)} all-to-all(f32[8,24,128]{2,1,0:T(8,128)S(1)} %broadcast_in_dim.6), channel_id=1, replica_groups=mesh['gx'=8,'gy_0'=4,'gy_1'=4,'gy_2'=2] {'gx'}, dimensions={0} | all-to-all | bytes 196608 | tf_op jit(solution)/shard_map/all_to_all | solution.py:418
  62.8 10.2 %all_to_all.17 = f32[16,24,128]{2,1,0:T(8,128)S(1)} all-to-all(f32[16,24,128]{2,1,0:T(8,128)S(1)} %broadcast_in_dim.7), channel_id=1, replica_groups=mesh['gx'=8,'gy_0'=4,'gy_1'=4,'gy_2'=2] {'gy_0','gy_1'}, dimensions={0} | all-to-all | bytes 393216 | tf_op jit(solution)/shard_map/all_to_all | solution.py:420
  73.0 1.3 %shard_map.133 = (f32[64,73]{1,0:T(8,128)}, f32[64,577]{1,0:T(8,128)}, f32[32,65]{1,0:T(8,128)}) custom-call(f32[384,128]{1,0:T(8,128)S(1)} %bitcast.3, f32[64,73]{1,0:T(8,128)S(1)} %copy-done.4, f32[64,577]{1,0:T(8,128)S(1)} %copy-done, f32[32,65]{1,0:T(8,128)S(1)} %copy-done.6, f32[160,128]{1,0:T(8,128)S(1)} %get-tuple-element.35.choose_ref, ...), custom_call_target="tpu_custom_call" | custom-call | flops 1000000 | bytes 1000000 | tf_op jit(solution)/shard_map/pallas_call | solution.py:463
  (5 shorter events, 0.1 us)
Async XLA Ops:
  0.6 11.7 %copy-start.2 = (f32[8,8,256]{2,1,0:T(8,128)S(1)}, f32[8,8,256]{2,1,0:T(8,128)}, u32[]{:S(2)}) copy-start(f32[8,8,256]{2,1,0:T(8,128)} %target_ref.5) | copy-start | bytes 196612
  0.6 11.6 %copy-start.1 = (f32[8,8,256]{2,1,0:T(8,128)S(1)}, f32[8,8,256]{2,1,0:T(8,128)}, u32[]{:S(2)}) copy-start(f32[8,8,256]{2,1,0:T(8,128)} %init_ref.5) | copy-start | bytes 196612
  0.7 11.6 %copy-start.5 = (s32[8,256]{1,0:T(8,128)S(1)}, s32[8,256]{1,0:T(8,128)}, u32[]{:S(2)}) copy-start(s32[8,256]{1,0:T(8,128)} %mask_ref.5) | copy-start | bytes 24580
  2.3 17.2 %copy-start = (f32[64,577]{1,0:T(8,128)S(1)}, f32[64,577]{1,0:T(8,128)}, u32[]{:S(2)}) copy-start(f32[64,577]{1,0:T(8,128)} %d2_ref.3) | copy-start | bytes 443140
  2.3 6.2 %collective-permute-start = (f32[72,256]{1,0:T(8,128)}, f32[72,256]{1,0:T(8,128)S(1)}, u32[]{:S(2)}, u32[]{:S(2)}) collective-permute-start(f32[72,256]{1,0:T(8,128)} %get-tuple-element.22), channel_id=1, source_target_pairs={{0,32},{32,64},{64,96},{96,128},{128,160},{160,192},{192,224},{1,3... | collective-permute-start | bytes 221192 | tf_op jit(solution)/shard_map/ppermute | solution.py:407
  6.8 12.7 %copy-start.4 = (f32[64,73]{1,0:T(8,128)S(1)}, f32[64,73]{1,0:T(8,128)}, u32[]{:S(2)}) copy-start(f32[64,73]{1,0:T(8,128)} %d1_ref.3) | copy-start | bytes 56068
  6.8 12.7 %copy-start.7 = (f32[64,73]{1,0:T(8,128)S(1)}, f32[64,73]{1,0:T(8,128)}, u32[]{:S(2)}) copy-start(f32[64,73]{1,0:T(8,128)} %one_ref.1) | copy-start | bytes 56068
  6.8 5.5 %collective-permute-start.1 = (f32[72,256]{1,0:T(8,128)}, f32[72,256]{1,0:T(8,128)S(1)}, u32[]{:S(2)}, u32[]{:S(2)}) collective-permute-start(f32[72,256]{1,0:T(8,128)} %get-tuple-element.23), channel_id=1, source_target_pairs={{32,0},{64,32},{96,64},{128,96},{160,128},{192,160},{224,192},{33,... | collective-permute-start | bytes 221192 | tf_op jit(solution)/shard_map/ppermute | solution.py:407
  12.3 7.2 %copy-start.6 = (f32[32,65]{1,0:T(8,128)S(1)}, f32[32,65]{1,0:T(8,128)}, u32[]{:S(2)}) copy-start(f32[32,65]{1,0:T(8,128)} %d3_ref.3) | copy-start | bytes 24964
  12.3 7.2 %copy-start.8 = (f32[32,65]{1,0:T(8,128)S(1)}, f32[32,65]{1,0:T(8,128)}, u32[]{:S(2)}) copy-start(f32[32,65]{1,0:T(8,128)} %head_ref.1) | copy-start | bytes 24964
  12.5 8.8 %collective-permute-start.2 = (f32[24,128]{1,0:T(8,128)S(1)}, f32[24,128]{1,0:T(8,128)S(1)}, u32[]{:S(2)}, u32[]{:S(2)}) collective-permute-start(f32[24,128]{1,0:T(8,128)S(1)} %get-tuple-element.24), channel_id=1, source_target_pairs={{0,1},{1,2},{2,3},{3,4},{4,5},{5,6},{6,7},{7,8},{8,9},{9,10},{10,1... | collective-permute-start | bytes 36872 | tf_op jit(solution)/shard_map/ppermute | solution.py:407
  17.5 2.0 %copy-start.9 = (s32[160]{0:T(256)S(1)}, s32[160]{0:T(256)}, u32[]{:S(2)}) copy-start(s32[160]{0:T(256)} %param.19) | copy-start | bytes 1924
  17.5 5.0 %collective-permute-start.3 = (f32[24,128]{1,0:T(8,128)S(1)}, f32[24,128]{1,0:T(8,128)S(1)}, u32[]{:S(2)}, u32[]{:S(2)}) collective-permute-start(f32[24,128]{1,0:T(8,128)S(1)} %get-tuple-element.25), channel_id=1, source_target_pairs={{1,0},{2,1},{3,2},{4,3},{5,4},{6,5},{7,6},{8,7},{9,8},{10,9},{11,1... | collective-permute-start | bytes 36872 | tf_op jit(solution)/shard_map/ppermute | solution.py:407
  19.5 0.9 %copy-start.3 = (f32[64,577]{1,0:T(8,128)S(1)}, f32[64,577]{1,0:T(8,128)}, u32[]{:S(2)}) copy-start(f32[64,577]{1,0:T(8,128)} %two_ref.1) | copy-start | bytes 443140
  46.2 1.3 %collective-permute-start.4 = (f32[24,128]{1,0:T(8,128)S(1)}, f32[24,128]{1,0:T(8,128)S(1)}, u32[]{:S(2)}, u32[]{:S(2)}) collective-permute-start(f32[24,128]{1,0:T(8,128)S(1)} %reduce_sum.18), channel_id=1, source_target_pairs={{0,1},{1,0},{2,3},{3,2},{4,5},{5,4},{6,7},{7,6},{8,9},{9,8},{10,11... | collective-permute-start | bytes 36872 | tf_op jit(solution)/shard_map/ppermute | solution.py:415

commit v3 on v2

--- a/solution.py
+++ b/solution.py
@@ -43,23 +43,23 @@
     return s * (1.0 + v * (1.0 - s))
 
 
-def pack_rows(init_ref, target_ref, mask_ref, low_ref, high_ref):
-    wet = mask_ref[...].astype(F32)
+def pack_rows(own_ref, low_ref, high_ref):
+    wet = own_ref[2 * LEV, :, :]
     low_ref[64:72, :] = wet
     high_ref[64:72, :] = wet
     for k in range(REACH):
-        low_ref[k * 8 : k * 8 + 8, :] = init_ref[:, k, :] * wet[k : k + 1]
+        low_ref[k * 8 : k * 8 + 8, :] = own_ref[0:LEV, k, :] * wet[k : k + 1]
         r = H - REACH + k
-        high_ref[k * 8 : k * 8 + 8, :] = init_ref[:, r, :] * wet[r : r + 1]
+        high_ref[k * 8 : k * 8 + 8, :] = own_ref[0:LEV, r, :] * wet[r : r + 1]
     for k in range(2):
-        low_ref[48 + k * 8 : 56 + k * 8, :] = target_ref[:, k, :]
-        high_ref[48 + k * 8 : 56 + k * 8, :] = target_ref[:, H - 2 + k, :]
-
-
-def row_parts(r, init_ref, target_ref, mask_ref, below_ref, above_ref):
+        low_ref[48 + k * 8 : 56 + k * 8, :] = own_ref[LEV : 2 * LEV, k, :]
+        high_ref[48 + k * 8 : 56 + k * 8, :] = own_ref[LEV : 2 * LEV, H - 2 + k, :]
+
+
+def row_parts(r, own_ref, below_ref, above_ref):
     if 0 <= r < H:
-        wet = mask_ref[r : r + 1, :].astype(F32)
-        return init_ref[:, r, :] * wet, wet, target_ref[:, r, :]
+        wet = own_ref[2 * LEV, r : r + 1, :]
+        return own_ref[0:LEV, r, :] * wet, wet, own_ref[LEV : 2 * LEV, r, :]
     ref, k = (below_ref, r + REACH) if r < 0 else (above_ref, r - H)
     field = ref[k * 8 : k * 8 + 8, :]
     m = r + H if r < 0 else r - H
@@ -71,12 +71,12 @@
     return field, wet, target
 
 
-def pack_cols(init_ref, target_ref, mask_ref, below_ref, above_ref, left_ref, right_ref):
+def pack_cols(own_ref, below_ref, above_ref, left_ref, right_ref):
     lane = lax.broadcasted_iota(jnp.int32, (8, 128), 1)
     zero = jnp.zeros((8, 128), F32)
     packed = [zero] * 6
     for r in range(-REACH, H + REACH):
-        field, wet, target = row_parts(r, init_ref, target_ref, mask_ref, below_ref, above_ref)
+        field, wet, target = row_parts(r, own_ref, below_ref, above_ref)
         wet = jnp.broadcast_to(wet, (8, W))
         at, by = divmod(r + REACH, 8)
         inner = lane - 16 * by
@@ -102,11 +102,25 @@
 ):
     one, two, head = one_ref[...], two_ref[...], head_ref[...]
     w1_ref[...] = one[:, : 9 * LEV].astype(BF)
-    w2_ref[...] = two[:, : 9 * C].astype(BF)
+    w2_ref[...] = jnp.concatenate(
+        [
+            jnp.concatenate(
+                [two[:, (3 * a + b) * C : (3 * a + b + 1) * C] for a in range(3)], axis=1
+            )
+            for b in range(3)
+        ],
+        axis=0,
+    ).astype(BF)
     w3_ref[...] = head[:, :C].astype(BF)
     w3t_ref[...] = head[:, :C].T.astype(BF)
     w2t_ref[...] = jnp.concatenate(
-        [two[:, (8 - k) * C : (9 - k) * C].T for k in range(9)], axis=1
+        [
+            jnp.concatenate(
+                [two[:, (8 - 3 * a - b) * C : (9 - 3 * a - b) * C].T for a in range(3)], axis=1
+            )
+            for b in range(3)
+        ],
+        axis=0,
     ).astype(BF)
     w1t_ref[...] = jnp.concatenate(
         [
@@ -144,16 +158,16 @@
 
 
 def main(
-    init_ref, target_ref, mask_ref, below_ref, above_ref, fromleft_ref, fromright_ref,
+    own_ref, below_ref, above_ref, fromleft_ref, fromright_ref,
     w1_ref, w2_ref, w3_ref, w3t_ref, w2t_ref, w1t_ref, bias_ref,
     final_ref, grad_ref,
-    xc0, xc1, wet_s, tgt, hc0, hc1, h2s, sp10, sp11, sp2, wd, ec0, ec1, e1s, rem, up, down, fin,
+    xc0, xc1, wet_s, tgt, hm0, hm1, hc0, hc1, h2s, sp10, sp11, sp2, wd, em0, em1, e1s, rem, up, down, fin,
     b1g, b2g, b3g, g1, g2, g3, final_v, sem,
 ):
     lane = lax.broadcasted_iota(jnp.int32, (8, 128), 1)
     zero = jnp.zeros((8, 128), F32)
     for r in range(-REACH, H + REACH):
-        field, wet, target = row_parts(r, init_ref, target_ref, mask_ref, below_ref, above_ref)
+        field, wet, target = row_parts(r, own_ref, below_ref, above_ref)
         at = (r + REACH) * 8
         block, by = divmod(r + REACH, 8)
         fl = fromleft_ref[block * 8 : block * 8 + 8, :]
@@ -174,7 +188,7 @@
     for ref in (b1g, b2g, b3g, g1, g2, g3):
         ref[...] = jnp.zeros(ref.shape, F32)
     for r in (4, 5, 14, 15):
-        ec0[r * 192 : r * 192 + 192, :] = jnp.zeros((192, PITCH), BF)
+        em0[r * 64 : r * 64 + 64, :] = jnp.zeros((64, PITCH), BF)
 
     col = lax.broadcasted_iota(jnp.int32, (1, PITCH), 1)
     col = jnp.where(col < 320, col, col - PITCH) + lax.axis_index(GY) * W
@@ -186,9 +200,9 @@
         i = row0 + r - REACH
         return col_in * jnp.where((i >= 0) & (i < lax.axis_size("gx") * H), 1.0, 0.0)
 
-    def bias(at, n, times=1):
+    def bias(at, n):
         b = bias_ref[at : at + n, :]
-        return jnp.concatenate([b] * (3 * times), axis=1)
+        return jnp.concatenate([b] * 3, axis=1)
 
     def part(ref, r, size, first=0, count=None):
         start = r * size + first
@@ -201,29 +215,37 @@
     def thrice(v):
         return turned(v, 1), v, turned(v, -1)
 
-    def store_thrice(ref, r, v):
-        for k, piece in enumerate(thrice(v)):
-            part(ref, r, 192, 64 * k, 64)[...] = piece.astype(BF)
-
-    def first_layer(xc, hc, sp1):
+    def conv(weights, ref, rs):
+        y = dot(weights, lanes([part(ref, r - 1, 64, 0, 192)[...] for r in rs]))
+        return [
+            turned(v[0:64], 1) + v[64:128] + turned(v[128:192], -1) for v in cut(y, len(rs))
+        ]
+
+    def first_layer(xc, hm, hc, sp1):
         def body(rs):
             x9 = lanes([part(xc, r - 1, 24, 0, 72)[...].astype(BF) for r in rs])
             for r, z in zip(rs, cut(dot(w1_ref[...], x9), len(rs))):
                 z = z + bias(0, 64)
                 s = sigmoid(z)
                 keep = inside(r)
-                store_thrice(hc, r, z * s * keep)
-                part(sp1, r, 64)[...] = silu_slope(z, s) * keep
+                h = (z * s * keep).astype(BF)
+                part(hm, r, 64)[...] = h
+                if -1 <= r - REACH <= H:
+                    for k, piece in enumerate(thrice(h)):
+                        part(hc, r, 192, 64 * k, 64)[...] = piece
+                    part(sp1, r, 64)[...] = silu_slope(z, s) * keep
 
         return body
 
-    def second_layer(hc, rs):
-        z = dot(w2_ref[...], lanes([part(hc, r - 1, 192, 0, 576)[...] for r in rs]))
-        z = z + bias(64, 64, len(rs))
-        s = sigmoid(z)
-        h2 = (z * s).astype(BF)
-        q = dot(w3_ref[...], h2) + bias(128, 32, len(rs))
-        return h2, silu_slope(z, s), sigmoid(q)
+    def second_layer(hm, rs):
+        h2, slope = [], []
+        for z in conv(w2_ref[...], hm, rs):
+            z = z + bias(64, 64)
+            s = sigmoid(z)
+            h2.append((z * s).astype(BF))
+            slope.append(silu_slope(z, s))
+        q = cut(dot(w3_ref[...], lanes(h2)), len(rs))
+        return lanes(h2), lanes(slope), lanes([sigmoid(v + bias(128, 32)) for v in q])
 
     def slopes(xc, r):
         x = part(xc, r, 24, 8, 8)[...]
@@ -236,7 +258,7 @@
         return x, [b - x for b in beside]
 
     def tail_zero(rs):
-        h2, slope, p = second_layer(hc0, rs)
+        h2, slope, p = second_layer(hm0, rs)
         n = len(rs)
         for r, h2r, sr, pr in zip(rs, cut(h2, n), cut(slope, n), cut(p, n)):
             part(h2s, r, 64)[...] = h2r
@@ -259,13 +281,13 @@
             lanes([e[:, :W].astype(BF) for e in e3]), lanes([v[:, :W] for v in h2])
         )
         g2[...] += dot_nt(
+            lanes([part(hc, r - 1, 192, 0, 576)[:, :W] for r in rs]),
             lanes([e[:, :W].astype(BF) for e in e2]),
-            lanes([part(hc, r - 1, 192, 0, 576)[:, :W] for r in rs]),
         )
 
     def tail_one(own):
         def body(rs):
-            h2, slope, p = second_layer(hc1, rs)
+            h2, slope, p = second_layer(hm1, rs)
             n = len(rs)
             e3s = []
             for r, pr in zip(rs, cut(p, n)):
@@ -291,15 +313,14 @@
             e2 = dot(w3t_ref[...], lanes([e.astype(BF) for e in e3s])) * slope
             e2s = cut(e2, n)
             for r, e in zip(rs, e2s):
-                store_thrice(ec1, r, e)
+                part(em1, r, 64)[...] = e.astype(BF)
             if own:
                 tail_grads(rs, e3s, e2s, cut(h2, n), hc1)
 
         return body
 
-    def first_error(ec, sp1, rs):
-        e = dot(w2t_ref[...], lanes([part(ec, r - 1, 192, 0, 576)[...] for r in rs]))
-        return [v * part(sp1, r, 64)[...] for r, v in zip(rs, cut(e, len(rs)))]
+    def first_error(em, sp1, rs):
+        return [v * part(sp1, r, 64)[...] for r, v in zip(rs, conv(w2t_ref[...], em, rs))]
 
     def first_grads(rs, e1, xc, width):
         b1g[...] += sum(folded(e[:, :width]) for e in e1)
@@ -310,7 +331,7 @@
 
     def first_one(own):
         def body(rs):
-            e1 = first_error(ec1, sp11, rs)
+            e1 = first_error(em1, sp11, rs)
             for r, e in zip(rs, e1):
                 part(e1s, r, 64)[...] = e.astype(BF)
             if own:
@@ -329,15 +350,15 @@
         e2 = dot(w3t_ref[...], lanes([e.astype(BF) for e in e3s]))
         e2s = [v * part(sp2, r, 64)[...] for r, v in zip(rs, cut(e2, len(rs)))]
         for r, e in zip(rs, e2s):
-            store_thrice(ec0, r, e)
+            part(em0, r, 64)[...] = e.astype(BF)
         tail_grads(rs, e3s, e2s, [part(h2s, r, 64)[...] for r in rs], hc0)
 
     def first_zero(rs):
-        first_grads(rs, first_error(ec0, sp10, rs), xc0, PITCH)
-
-    loop(-5, 13, 9, first_layer(xc0, hc0, sp10))
+        first_grads(rs, first_error(em0, sp10, rs), xc0, PITCH)
+
+    loop(-5, 13, 9, first_layer(xc0, hm0, hc0, sp10))
     loop(-4, 12, 16, tail_zero)
-    loop(-3, 11, 14, first_layer(xc1, hc1, sp11))
+    loop(-3, 11, 14, first_layer(xc1, hm1, hc1, sp11))
     tail_one(False)([4, 5, 14, 15])
     loop(0, 8, 8, tail_one(True))
     for r in range(H):
@@ -349,9 +370,8 @@
     loop(0, 8, 8, back_zero)
     loop(-1, 9, 10, first_zero)
 
-    for k in range(4):
-        grad_ref[k * 64 : k * 64 + 64, :] = g2[:, k * 128 : k * 128 + 128]
-    grad_ref[256:320, :] = jnp.concatenate([g2[:, 512:576], g1[:, 0:64]], axis=1)
+    grad_ref[0:256, :] = jnp.concatenate([g2[0:256, :], g2[256:512, :]], axis=1)
+    grad_ref[256:320, :] = jnp.concatenate([g2[512:576, :], g1[:, 0:64]], axis=1)
     sums = [jnp.sum(ref[...], axis=1, keepdims=True) for ref in (b1g, b2g, b3g)]
     sums[2] = jnp.concatenate([sums[2], jnp.zeros((32, 1), F32)], axis=0)
     grad_ref[320:384, :] = jnp.concatenate(
@@ -368,15 +388,16 @@
 
 def finish(total_ref, d1_ref, d2_ref, d3_ref, choose_ref, below_ref, u1_ref, u2_ref, u3_ref):
     t = [total_ref[k * 64 : k * 64 + 64, :] for k in range(6)]
-    two = jnp.concatenate([*t[:4], t[4][:, :64], t[5][:, 9:10]], axis=1)
+    two = jnp.concatenate([v[:, :64].T for v in t[:4]] + [v[:, 64:].T for v in t[:4]] + [t[4][:, :64].T, t[5][:, 9:10]], axis=1)
     one = jnp.concatenate([t[4][:, 64:], t[5][:, :8], t[5][:, 8:9]], axis=1)
     three = jnp.concatenate([t[5][:32, 64:], t[5][:32, 10:11]], axis=1)
     grads = (one, two, three)
-    norm = jnp.sqrt(jnp.sum(row_sums(grads), axis=0, keepdims=True))
+    squares = row_sums(grads)
+    norm = jnp.sqrt(jnp.sum(squares, axis=0, keepdims=True))
     factor = 1.0 / jnp.maximum(norm, 1.0)
     clipped = [v * factor for v in grads]
     choose = choose_ref[...]
-    ratios = jnp.sqrt(jnp.sum(choose * row_sums(clipped), axis=0, keepdims=True)) / below_ref[...]
+    ratios = factor * jnp.sqrt(jnp.sum(choose * squares, axis=0, keepdims=True)) / below_ref[...]
     row_ratio = jnp.sum(choose * ratios, axis=1, keepdims=True)
     scaling = math.sqrt(PARAMS)
     at = 0
@@ -423,17 +444,21 @@
 def per_device(init, target, mask, one, two, head, d1, d2, d3, gid):
     hbm = pl.BlockSpec(memory_space=pltpu.HBM)
     vmem = pl.BlockSpec(memory_space=pltpu.VMEM)
-    to_low, to_high = kernel(pack_rows, [shape((72, W))] * 2, 10**5, 60)(init, target, mask)
+    def widened(v, first):
+        return jnp.pad(v, ((first, 2 * LEV + 1 - first - v.shape[0]), (0, 0), (0, 0)))
+
+    own = widened(init, 0) + widened(target, LEV) + widened(mask[None], 2 * LEV).astype(F32)
+    to_low, to_high = kernel(pack_rows, [shape((72, W))] * 2, 10**5, 4)(own)
     below, above = exchange(to_high, to_low, "gx")
     to_left, to_right = kernel(pack_cols, [shape((24, 128))] * 2, 10**5, 4)(
-        init, target, mask, below, above
+        own, below, above
     )
     from_left, from_right = exchange(to_right, to_left, GY)
     *weights, choose, below_ratio = kernel(
         prepare,
         [
-            shape((C, 72), BF), shape((C, 576), BF), shape((K, C), BF), shape((C, K), BF),
-            shape((C, 576), BF), shape((24, 192), BF), shape((160, 128)),
+            shape((C, 72), BF), shape((192, 192), BF), shape((K, C), BF), shape((C, K), BF),
+            shape((192, 192), BF), shape((24, 192), BF), shape((160, 128)),
             shape((160, 128)), shape((1, 128)),
         ],
         10**6,
@@ -448,17 +473,17 @@
         [shape((LEV, H, W)), shape((384, 128))],
         10**7,
         40,
-        in_specs=[vmem] * 14,
+        in_specs=[vmem] * 12,
         out_specs=[hbm, vmem],
         scratch_shapes=[
-            rows(24), rows(24), rows(8), rows(8), rows(192, BF), rows(192, BF), rows(64, BF),
-            rows(64), rows(64), rows(64), rows(32), rows(192, BF), rows(192, BF), rows(64, BF),
+            rows(24), rows(24), rows(8), rows(8), rows(64, BF), rows(64, BF), rows(192, BF), rows(192, BF), rows(64, BF),
+            rows(64), rows(64), rows(64), rows(32), rows(64, BF), rows(64, BF), rows(64, BF),
             rows(8), rows(8), rows(8), rows(8),
             pltpu.VMEM((64, 128), F32), pltpu.VMEM((64, 128), F32), pltpu.VMEM((32, 128), F32),
-            pltpu.VMEM((64, 72), F32), pltpu.VMEM((64, 576), F32), pltpu.VMEM((32, 64), F32),
+            pltpu.VMEM((64, 72), F32), pltpu.VMEM((576, 64), F32), pltpu.VMEM((32, 64), F32),
             pltpu.VMEM((LEV, H, W), F32), pltpu.SemaphoreType.DMA,
         ],
-    )(init, target, mask, below, above, from_left, from_right, *weights)
+    )(own, below, above, from_left, from_right, *weights)
     total = total_of(grad)
     u1, u2, u3 = kernel(finish, [shape(one.shape), shape(two.shape), shape(head.shape)], 10**6, 8)(
         total, d1, d2, d3, choose, below_ratio

time: 75.3 us -> 73.5 us (0.976)
  Pallas kernels: 12.7 us -> 10.3 us
  local copies, waits for them, and re-layouts: 0.98 us -> 0.06 us
  other arithmetic: 0.04 us -> 0.94 us
    pallas_call x3, Pallas kernels: 2.61 us -> 1.1 us  [the longest x1 0.89 us: per_device(): kernel(prepare, [shape((C, 72), BF), shape((192, 192), BF), shape((K, C),...]
    ppermute x2, waiting for transfers between devices: 5.07 us -> 6.03 us  [exchange(): lax.ppermute(backward, axis, back)]
    unnamed x20 -> x14, local copies, waits for them, and re-layouts: 0.96 us -> 0.04 us
    add x0 -> x1, other arithmetic: none -> 0.9 us  [per_device(): widened(init, 0) + widened(target, LEV)]
    pallas_call x1, Pallas kernels: 8.81 us -> 7.99 us  [per_device(): kernel(main, [shape((LEV, H, W)), shape((384, 128))], 10 ** 7, 40, in_spe...]
where the time goes in v3:
time: 73.5 us; the launch traced here: 72.5 us
  blocking collectives  40.3 us (55%)
  starting transfers between devices  12.8 us (17%)
  Pallas kernels  10.3 us (14%)
  waiting for transfers between devices  7.26 us (10%)
  other arithmetic  0.94 us (1%)
  between operations  0.83 us (1%)
    all_to_all x1, blocking collectives, total_of(): own = jnp.sum(lax.all_to_all(copies, 'gx', 0, 0, tiled=True), axis=0)  15.3 us
    all_to_all x1, blocking collectives, total_of(): own = jnp.sum(lax.all_to_all(pieces, near, 0, 0, tiled=True), axis=0)  14.8 us
    all_to_all x1, blocking collectives, total_of(): return lax.all_to_all(copies, near, 0, 0, tiled=True).reshape(grad.shape)  10.2 us
    ppermute x2, starting transfers between devices, exchange(): lax.ppermute(forward, axis, ahead)  9.52 us
    pallas_call x1, Pallas kernels, per_device(): kernel(main, [shape((LEV, H, W)), shape((384, 128))], 10 ** 7, 40, in_spe...  7.99 us
    ppermute x2, waiting for transfers between devices, exchange(): lax.ppermute(backward, axis, back)  6.03 us
    ppermute x2, starting transfers between devices, exchange(): lax.ppermute(backward, axis, back)  3.21 us
  transfers between devices with their start and end apart: 5, of which 4 were waited for; matrix products, arithmetic and copies ran while one was open for 0% of the time, Pallas kernels for 1%

profile of v3, /device:TPU:1, one launch (start us, length us, event | category | flops | bytes accessed | tf_op | source)
XLA Modules:
  0.0 72.5 jit_solution(12101794350769658580)
XLA Ops:
  0.6 0.9 %convert_add_fusion.own_ref = f32[17,8,256]{2,1,0:T(8,128)S(1)} fusion(s32[1,8,256]{2,1,0:T(8,128)} %bitcast.7, f32[8,8,256]{2,1,0:T(8,128)} %param.11, f32[8,8,256]{2,1,0:T(8,128)} %param.10), kind=kLoop, calls=%fused_computation | loop fusion | flops 104448 | bytes 278528 | tf_op jit(solution)/shard_map/add | solution.py:450
  1.5 0.0 copy-start.1
  1.6 0.0 copy-start
  1.6 4.5 %collective-permute-start = (f32[72,256]{1,0:T(8,128)S(1)}, f32[72,256]{1,0:T(8,128)S(1)}, u32[]{:S(2)}, u32[]{:S(2)}) collective-permute-start(f32[72,256]{1,0:T(8,128)S(1)} %get-tuple-element.22), channel_id=1, source_target_pairs={{0,32},{32,64},{64,96},{96,128},{128,160},{160,192},{192,224},{1,3... | collective-permute-start | bytes 221192 | tf_op jit(solution)/shard_map/ppermute | solution.py:428
  6.1 0.0 copy-start.2
  6.1 0.0 copy-start.4
  6.1 1.3 %collective-permute-start.1 = (f32[72,256]{1,0:T(8,128)S(1)}, f32[72,256]{1,0:T(8,128)S(1)}, u32[]{:S(2)}, u32[]{:S(2)}) collective-permute-start(f32[72,256]{1,0:T(8,128)S(1)} %get-tuple-element.23), channel_id=1, source_target_pairs={{32,0},{64,32},{96,64},{128,96},{160,128},{192,160},{224,192},{33,... | collective-permute-start | bytes 221192 | tf_op jit(solution)/shard_map/ppermute | solution.py:428
  7.4 0.1 collective-permute-done.below_ref
  7.5 3.9 %collective-permute-done.1.above_ref = f32[72,256]{1,0:T(8,128)S(1)} collective-permute-done((f32[72,256]{1,0:T(8,128)S(1)}, f32[72,256]{1,0:T(8,128)S(1)}, u32[]{:S(2)}, u32[]{:S(2)}) %collective-permute-start.1) | collective-permute-done | bytes 73760 | tf_op jit(solution)/shard_map/ppermute | solution.py:428
  11.4 0.0 copy-start.3
  11.4 0.0 copy-start.5
  11.4 0.2 shard_map.130
  11.6 5.0 %collective-permute-start.2 = (f32[24,128]{1,0:T(8,128)S(1)}, f32[24,128]{1,0:T(8,128)S(1)}, u32[]{:S(2)}, u32[]{:S(2)}) collective-permute-start(f32[24,128]{1,0:T(8,128)S(1)} %get-tuple-element.24), channel_id=1, source_target_pairs={{0,1},{1,2},{2,3},{3,4},{4,5},{5,6},{6,7},{7,8},{8,9},{9,10},{10,1... | collective-permute-start | bytes 36872 | tf_op jit(solution)/shard_map/ppermute | solution.py:428
  16.6 0.0 copy-start.6
  16.6 1.9 %collective-permute-start.3 = (f32[24,128]{1,0:T(8,128)S(1)}, f32[24,128]{1,0:T(8,128)S(1)}, u32[]{:S(2)}, u32[]{:S(2)}) collective-permute-start(f32[24,128]{1,0:T(8,128)S(1)} %get-tuple-element.25), channel_id=1, source_target_pairs={{1,0},{2,1},{3,2},{4,3},{5,4},{6,5},{7,6},{8,7},{9,8},{10,9},{11,1... | collective-permute-start | bytes 36872 | tf_op jit(solution)/shard_map/ppermute | solution.py:428
  18.6 0.0 copy-done.1
  18.6 0.0 copy-done
  18.6 0.0 copy-done.2
  18.6 0.0 copy-done.4
  18.6 0.0 copy-done.3
  18.6 0.0 copy-done.5
  18.6 0.0 copy-done.6
  18.6 0.9 %shard_map.131 = (bf16[64,72]{1,0:T(8,128)(2,1)S(1)}, bf16[192,192]{1,0:T(8,128)(2,1)S(1)}, bf16[32,64]{1,0:T(8,128)(2,1)S(1)}, bf16[64,32]{1,0:T(8,128)(2,1)S(1...) custom-call(f32[64,73]{1,0:T(8,128)S(1)} %copy-done.4, ...), custom_call_target="tpu_custom_call" | custom-call | flops 1000000 | bytes 1000000 | tf_op jit(solution)/shard_map/pallas_call | solution.py:457
  19.5 0.0 collective-permute-done.2.fromleft_ref
  19.5 2.1 %collective-permute-done.3.fromright_ref = f32[24,128]{1,0:T(8,128)S(1)} collective-permute-done((f32[24,128]{1,0:T(8,128)S(1)}, f32[24,128]{1,0:T(8,128)S(1)}, u32[]{:S(2)}, u32[]{:S(2)}) %collective-permute-start.3) | collective-permute-done | bytes 12320 | tf_op jit(solution)/shard_map/ppermute | solution.py:428
  21.7 8.0 %shard_map.132 = (f32[8,8,256]{2,1,0:T(8,128)}, f32[384,128]{1,0:T(8,128)S(1)}) custom-call(f32[17,8,256]{2,1,0:T(8,128)S(1)} %convert_add_fusion.own_ref, f32[72,256]{1,0:T(8,128)S(1)} %collective-permute-done.below_ref, f32[72,256]{1,0:T(8,128)S(1)} %collective-permute-done.1.above_ref, f32[24,128]{1,0:T(8,128)S(1)} %collective-permute-done.2.fromleft_ref, ...), custom_call_target="tpu_custom_call" | custom-call | flops 10000000 | bytes 10000000 | tf_op jit(solution)/shard_map/pallas_call | solution.py:471
  29.6 14.8 %all_to_all.15 = f32[16,24,128]{2,1,0:T(8,128)S(1)} all-to-all(f32[16,24,128]{2,1,0:T(8,128)S(1)} %bitcast.5), channel_id=1, replica_groups=mesh['gx'=8,'gy_0'=4,'gy_1'=4,'gy_2'=2] {'gy_0','gy_1'}, dimensions={0} | all-to-all | bytes 393216 | tf_op jit(solution)/shard_map/all_to_all | solution.py:435
  44.5 0.1 collective-permute-start.4
  44.6 1.2 %collective-permute-done.4 = f32[24,128]{1,0:T(8,128)S(1)} collective-permute-done((f32[24,128]{1,0:T(8,128)S(1)}, f32[24,128]{1,0:T(8,128)S(1)}, u32[]{:S(2)}, u32[]{:S(2)}) %collective-permute-start.4) | collective-permute-done | bytes 12320 | tf_op jit(solution)/shard_map/ppermute | solution.py:436
  45.7 15.3 %all_to_all.16 = f32[8,24,128]{2,1,0:T(8,128)S(1)} all-to-all(f32[8,24,128]{2,1,0:T(8,128)S(1)} %broadcast_in_dim.10), channel_id=1, replica_groups=mesh['gx'=8,'gy_0'=4,'gy_1'=4,'gy_2'=2] {'gx'}, dimensions={0} | all-to-all | bytes 196608 | tf_op jit(solution)/shard_map/all_to_all | solution.py:439
  61.1 10.2 %all_to_all.17 = f32[16,24,128]{2,1,0:T(8,128)S(1)} all-to-all(f32[16,24,128]{2,1,0:T(8,128)S(1)} %broadcast_in_dim.11), channel_id=1, replica_groups=mesh['gx'=8,'gy_0'=4,'gy_1'=4,'gy_2'=2] {'gy_0','gy_1'}, dimensions={0} | all-to-all | bytes 393216 | tf_op jit(solution)/shard_map/all_to_all | solution.py:441
  71.3 1.2 %shard_map.133 = (f32[64,73]{1,0:T(8,128)}, f32[64,577]{1,0:T(8,128)}, f32[32,65]{1,0:T(8,128)}) custom-call(f32[384,128]{1,0:T(8,128)S(1)} %bitcast.4, f32[64,73]{1,0:T(8,128)S(1)} %copy-done.2, f32[64,577]{1,0:T(8,128)S(1)} %copy-done, f32[32,65]{1,0:T(8,128)S(1)} %copy-done.3, f32[160,128]{1,0:T(8,128)S(1)} %get-tuple-element.35.choose_ref, ...), custom_call_target="tpu_custom_call" | custom-call | flops 1000000 | bytes 1000000 | tf_op jit(solution)/shard_map/pallas_call | solution.py:488
  (6 shorter events, 0.1 us)
Async XLA Ops:
  1.5 17.0 %copy-start.1 = (f32[64,577]{1,0:T(8,128)S(1)}, f32[64,577]{1,0:T(8,128)}, u32[]{:S(2)}) copy-start(f32[64,577]{1,0:T(8,128)} %two_ref.1) | copy-start | bytes 443140
  1.6 17.0 %copy-start = (f32[64,577]{1,0:T(8,128)S(1)}, f32[64,577]{1,0:T(8,128)}, u32[]{:S(2)}) copy-start(f32[64,577]{1,0:T(8,128)} %d2_ref.3) | copy-start | bytes 443140
  1.6 5.9 %collective-permute-start = (f32[72,256]{1,0:T(8,128)S(1)}, f32[72,256]{1,0:T(8,128)S(1)}, u32[]{:S(2)}, u32[]{:S(2)}) collective-permute-start(f32[72,256]{1,0:T(8,128)S(1)} %get-tuple-element.22), channel_id=1, source_target_pairs={{0,32},{32,64},{64,96},{96,128},{128,160},{160,192},{192,224},{1,3... | collective-permute-start | bytes 221192 | tf_op jit(solution)/shard_map/ppermute | solution.py:428
  6.1 12.5 %copy-start.2 = (f32[64,73]{1,0:T(8,128)S(1)}, f32[64,73]{1,0:T(8,128)}, u32[]{:S(2)}) copy-start(f32[64,73]{1,0:T(8,128)} %d1_ref.3) | copy-start | bytes 56068
  6.1 12.5 %copy-start.4 = (f32[64,73]{1,0:T(8,128)S(1)}, f32[64,73]{1,0:T(8,128)}, u32[]{:S(2)}) copy-start(f32[64,73]{1,0:T(8,128)} %one_ref.1) | copy-start | bytes 56068
  6.1 5.3 %collective-permute-start.1 = (f32[72,256]{1,0:T(8,128)S(1)}, f32[72,256]{1,0:T(8,128)S(1)}, u32[]{:S(2)}, u32[]{:S(2)}) collective-permute-start(f32[72,256]{1,0:T(8,128)S(1)} %get-tuple-element.23), channel_id=1, source_target_pairs={{32,0},{64,32},{96,64},{128,96},{160,128},{192,160},{224,192},{33,... | collective-permute-start | bytes 221192 | tf_op jit(solution)/shard_map/ppermute | solution.py:428
  11.4 7.2 %copy-start.3 = (f32[32,65]{1,0:T(8,128)S(1)}, f32[32,65]{1,0:T(8,128)}, u32[]{:S(2)}) copy-start(f32[32,65]{1,0:T(8,128)} %d3_ref.3) | copy-start | bytes 24964
  11.4 7.2 %copy-start.5 = (f32[32,65]{1,0:T(8,128)S(1)}, f32[32,65]{1,0:T(8,128)}, u32[]{:S(2)}) copy-start(f32[32,65]{1,0:T(8,128)} %head_ref.1) | copy-start | bytes 24964
  11.6 7.9 %collective-permute-start.2 = (f32[24,128]{1,0:T(8,128)S(1)}, f32[24,128]{1,0:T(8,128)S(1)}, u32[]{:S(2)}, u32[]{:S(2)}) collective-permute-start(f32[24,128]{1,0:T(8,128)S(1)} %get-tuple-element.24), channel_id=1, source_target_pairs={{0,1},{1,2},{2,3},{3,4},{4,5},{5,6},{6,7},{7,8},{8,9},{9,10},{10,1... | collective-permute-start | bytes 36872 | tf_op jit(solution)/shard_map/ppermute | solution.py:428
  16.6 2.0 %copy-start.6 = (s32[160]{0:T(256)S(1)}, s32[160]{0:T(256)}, u32[]{:S(2)}) copy-start(s32[160]{0:T(256)} %param.19) | copy-start | bytes 1924
  16.6 5.0 %collective-permute-start.3 = (f32[24,128]{1,0:T(8,128)S(1)}, f32[24,128]{1,0:T(8,128)S(1)}, u32[]{:S(2)}, u32[]{:S(2)}) collective-permute-start(f32[24,128]{1,0:T(8,128)S(1)} %get-tuple-element.25), channel_id=1, source_target_pairs={{1,0},{2,1},{3,2},{4,3},{5,4},{6,5},{7,6},{8,7},{9,8},{10,9},{11,1... | collective-permute-start | bytes 36872 | tf_op jit(solution)/shard_map/ppermute | solution.py:428
  44.5 1.3 %collective-permute-start.4 = (f32[24,128]{1,0:T(8,128)S(1)}, f32[24,128]{1,0:T(8,128)S(1)}, u32[]{:S(2)}, u32[]{:S(2)}) collective-permute-start(f32[24,128]{1,0:T(8,128)S(1)} %reduce_sum.18), channel_id=1, source_target_pairs={{0,1},{1,0},{2,3},{3,2},{4,5},{5,4},{6,7},{7,6},{8,9},{9,8},{10,11... | collective-permute-start | bytes 36872 | tf_op jit(solution)/shard_map/ppermute | solution.py:436

commit v4 on v3

--- a/solution.py
+++ b/solution.py
@@ -43,17 +43,37 @@
     return s * (1.0 + v * (1.0 - s))
 
 
-def pack_rows(own_ref, low_ref, high_ref):
+def pack_rows(own_ref, first_ref, second_ref):
+    even = is_even("gx")
     wet = own_ref[2 * LEV, :, :]
-    low_ref[64:72, :] = wet
-    high_ref[64:72, :] = wet
+
+    def put(at, low, high):
+        first_ref[at : at + 8, :] = jnp.where(even, high, low)
+        second_ref[at : at + 8, :] = jnp.where(even, low, high)
+
+    put(64, wet, wet)
     for k in range(REACH):
-        low_ref[k * 8 : k * 8 + 8, :] = own_ref[0:LEV, k, :] * wet[k : k + 1]
         r = H - REACH + k
-        high_ref[k * 8 : k * 8 + 8, :] = own_ref[0:LEV, r, :] * wet[r : r + 1]
+        put(k * 8, own_ref[0:LEV, k, :] * wet[k : k + 1], own_ref[0:LEV, r, :] * wet[r : r + 1])
     for k in range(2):
-        low_ref[48 + k * 8 : 56 + k * 8, :] = own_ref[LEV : 2 * LEV, k, :]
-        high_ref[48 + k * 8 : 56 + k * 8, :] = own_ref[LEV : 2 * LEV, H - 2 + k, :]
+        put(48 + k * 8, own_ref[LEV : 2 * LEV, k, :], own_ref[LEV : 2 * LEV, H - 2 + k, :])
+
+
+def is_even(axis):
+    return lax.rem(lax.axis_index(axis), 2) == 0
+
+
+class Chosen:
+    def __init__(self, condition, first, second):
+        self.condition, self.first, self.second = condition, first, second
+
+    def __getitem__(self, index):
+        return jnp.where(self.condition, self.first[index], self.second[index])
+
+
+def by_side(axis, first_ref, second_ref):
+    even = is_even(axis)
+    return Chosen(even, second_ref, first_ref), Chosen(even, first_ref, second_ref)
 
 
 def row_parts(r, own_ref, below_ref, above_ref):
@@ -71,7 +91,9 @@
     return field, wet, target
 
 
-def pack_cols(own_ref, below_ref, above_ref, left_ref, right_ref):
+def pack_cols(own_ref, swap_one_ref, swap_two_ref, first_ref, second_ref):
+    below_ref, above_ref = by_side("gx", swap_one_ref, swap_two_ref)
+    even = is_even(GY)
     lane = lax.broadcasted_iota(jnp.int32, (8, 128), 1)
     zero = jnp.zeros((8, 128), F32)
     packed = [zero] * 6
@@ -88,8 +110,8 @@
                 v = jnp.where(inner < 10, v, turned(target[:, first : first + 128], move[2]))
             packed[side + at] = jnp.where((inner >= 0) & (inner < 12), v, packed[side + at])
     for k in range(3):
-        left_ref[k * 8 : k * 8 + 8, :] = packed[k]
-        right_ref[k * 8 : k * 8 + 8, :] = packed[3 + k]
+        first_ref[k * 8 : k * 8 + 8, :] = jnp.where(even, packed[3 + k], packed[k])
+        second_ref[k * 8 : k * 8 + 8, :] = jnp.where(even, packed[k], packed[3 + k])
 
 
 def row_sums(parts):
@@ -158,12 +180,14 @@
 
 
 def main(
-    own_ref, below_ref, above_ref, fromleft_ref, fromright_ref,
+    own_ref, row_one_ref, row_two_ref, col_one_ref, col_two_ref,
     w1_ref, w2_ref, w3_ref, w3t_ref, w2t_ref, w1t_ref, bias_ref,
     final_ref, grad_ref,
     xc0, xc1, wet_s, tgt, hm0, hm1, hc0, hc1, h2s, sp10, sp11, sp2, wd, em0, em1, e1s, rem, up, down, fin,
     b1g, b2g, b3g, g1, g2, g3, final_v, sem,
 ):
+    below_ref, above_ref = by_side("gx", row_one_ref, row_two_ref)
+    fromleft_ref, fromright_ref = by_side(GY, col_one_ref, col_two_ref)
     lane = lax.broadcasted_iota(jnp.int32, (8, 128), 1)
     zero = jnp.zeros((8, 128), F32)
     for r in range(-REACH, H + REACH):
@@ -421,11 +445,11 @@
     )
 
 
-def exchange(forward, backward, axis):
+def exchange(first, second, axis):
     count = lax.axis_size(axis)
-    ahead = [(i, i + 1) for i in range(count - 1)]
-    back = [(b, a) for a, b in ahead]
-    return lax.ppermute(forward, axis, ahead), lax.ppermute(backward, axis, back)
+    pairs = [[(i, i + 1) for i in range(start, count - 1, 2)] for start in (0, 1)]
+    swaps = [[*p, *((b, a) for a, b in p)] for p in pairs]
+    return lax.ppermute(first, axis, swaps[0]), lax.ppermute(second, axis, swaps[1])
 
 
 def total_of(grad):
@@ -448,12 +472,12 @@
         return jnp.pad(v, ((first, 2 * LEV + 1 - first - v.shape[0]), (0, 0), (0, 0)))
 
     own = widened(init, 0) + widened(target, LEV) + widened(mask[None], 2 * LEV).astype(F32)
-    to_low, to_high = kernel(pack_rows, [shape((72, W))] * 2, 10**5, 4)(own)
-    below, above = exchange(to_high, to_low, "gx")
-    to_left, to_right = kernel(pack_cols, [shape((24, 128))] * 2, 10**5, 4)(
-        own, below, above
+    packs = kernel(pack_rows, [shape((72, W))] * 2, 10**5, 4)(own)
+    rows_in = exchange(*packs, "gx")
+    packs = kernel(pack_cols, [shape((24, 128))] * 2, 10**5, 4)(
+        own, *rows_in
     )
-    from_left, from_right = exchange(to_right, to_left, GY)
+    cols_in = exchange(*packs, GY)
     *weights, choose, below_ratio = kernel(
         prepare,
         [
@@ -483,7 +507,7 @@
             pltpu.VMEM((64, 72), F32), pltpu.VMEM((576, 64), F32), pltpu.VMEM((32, 64), F32),
             pltpu.VMEM((LEV, H, W), F32), pltpu.SemaphoreType.DMA,
         ],
-    )(own, below, above, from_left, from_right, *weights)
+    )(own, *rows_in, *cols_in, *weights)
     total = total_of(grad)
     u1, u2, u3 = kernel(finish, [shape(one.shape), shape(two.shape), shape(head.shape)], 10**6, 8)(
         total, d1, d2, d3, choose, below_ratio

time: 73.5 us -> 69.9 us (0.951)
  starting transfers between devices: 12.8 us -> 8.94 us
  blocking collectives: 40.3 us -> 43.7 us
  waiting for transfers between devices: 7.26 us -> 4.22 us
    all_to_all x1, blocking collectives: 15.3 us -> 19.7 us  [total_of(): own = jnp.sum(lax.all_to_all(copies, 'gx', 0, 0, tiled=True), axis=0)]
    ppermute x4, starting transfers between devices: 12.7 us -> 8.85 us  [the longest x2 6.02 us: exchange(): lax.ppermute(first, axis, swaps[0])]
    ppermute x4, waiting for transfers between devices: 6.09 us -> 3.06 us  [the longest x2 2.11 us: exchange(): lax.ppermute(second, axis, swaps[1])]
    all_to_all x1, blocking collectives: 14.8 us -> 13.8 us  [total_of(): own = jnp.sum(lax.all_to_all(pieces, near, 0, 0, tiled=True), axis=0)]
  transfers between devices with their start and end apart: 5 -> 5, of which waited for: 4 -> 3; matrix products, arithmetic and copies ran while one was open for 0% -> 0% of each run, Pallas kernels for 1% -> 1%
where the time goes in v4:
time: 69.9 us; the launch traced here: 69 us
  blocking collectives  43.7 us (63%)
  Pallas kernels  10.4 us (15%)
  starting transfers between devices  8.94 us (13%)
  waiting for transfers between devices  4.22 us (6%)
  other arithmetic  0.94 us (1%)
  between operations  0.79 us (1%)
    all_to_all x1, blocking collectives, total_of(): own = jnp.sum(lax.all_to_all(copies, 'gx', 0, 0, tiled=True), axis=0)  19.7 us
    all_to_all x1, blocking collectives, total_of(): own = jnp.sum(lax.all_to_all(pieces, near, 0, 0, tiled=True), axis=0)  13.8 us
    all_to_all x1, blocking collectives, total_of(): return lax.all_to_all(copies, near, 0, 0, tiled=True).reshape(grad.shape)  10.2 us
    pallas_call x1, Pallas kernels, per_device(): kernel(main, [shape((LEV, H, W)), shape((384, 128))], 10 ** 7, 40, in_spe...  8.04 us
    ppermute x2, starting transfers between devices, exchange(): lax.ppermute(first, axis, swaps[0])  6.02 us
    ppermute x2, starting transfers between devices, exchange(): lax.ppermute(second, axis, swaps[1])  2.82 us
    ppermute x2, waiting for transfers between devices, exchange(): lax.ppermute(second, axis, swaps[1])  2.11 us
  transfers between devices with their start and end apart: 5, of which 3 were waited for; matrix products, arithmetic and copies ran while one was open for 0% of the time, Pallas kernels for 1%

profile of v4, /device:TPU:1, one launch (start us, length us, event | category | flops | bytes accessed | tf_op | source)
XLA Modules:
  0.0 69.0 jit_solution(11287234910333141161)
XLA Ops:
  0.6 0.9 %convert_add_fusion.own_ref = f32[17,8,256]{2,1,0:T(8,128)S(1)} fusion(s32[1,8,256]{2,1,0:T(8,128)} %bitcast.7, f32[8,8,256]{2,1,0:T(8,128)} %param.11, f32[8,8,256]{2,1,0:T(8,128)} %param.10), kind=kLoop, calls=%fused_computation | loop fusion | flops 104448 | bytes 278528 | tf_op jit(solution)/shard_map/add | solution.py:474
  1.5 0.0 copy-start.1
  1.5 0.1 shard_map.129
  1.6 0.0 copy-start
  1.6 2.6 %collective-permute-start = (f32[72,256]{1,0:T(8,128)S(1)}, f32[72,256]{1,0:T(8,128)S(1)}, u32[]{:S(2)}, u32[]{:S(2)}) collective-permute-start(f32[72,256]{1,0:T(8,128)S(1)} %get-tuple-element.22), channel_id=1, source_target_pairs={{0,32},{64,96},{128,160},{192,224},{32,0},{96,64},{160,128},{224,1... | collective-permute-start | bytes 221192 | tf_op jit(solution)/shard_map/ppermute | solution.py:452
  4.2 0.0 copy-start.2
  4.2 0.0 copy-start.4
  4.2 0.8 %collective-permute-start.1 = (f32[72,256]{1,0:T(8,128)S(1)}, f32[72,256]{1,0:T(8,128)S(1)}, u32[]{:S(2)}, u32[]{:S(2)}) collective-permute-start(f32[72,256]{1,0:T(8,128)S(1)} %get-tuple-element.23), channel_id=1, source_target_pairs={{32,64},{96,128},{160,192},{64,32},{128,96},{192,160},{33,65},{97,... | collective-permute-start | bytes 221192 | tf_op jit(solution)/shard_map/ppermute | solution.py:452
  5.0 0.9 %collective-permute-done.swap_one_ref.row_one_ref = f32[72,256]{1,0:T(8,128)S(1)} collective-permute-done((f32[72,256]{1,0:T(8,128)S(1)}, f32[72,256]{1,0:T(8,128)S(1)}, u32[]{:S(2)}, u32[]{:S(2)}) %collective-permute-start) | collective-permute-done | bytes 73760 | tf_op jit(solution)/shard_map/ppermute | solution.py:452
  5.9 0.0 collective-permute-done.1.swap_two_ref.row_two_ref
  5.9 0.0 copy-start.3
  5.9 0.0 copy-start.5
  5.9 0.2 shard_map.130
  6.1 3.5 %collective-permute-start.2 = (f32[24,128]{1,0:T(8,128)S(1)}, f32[24,128]{1,0:T(8,128)S(1)}, u32[]{:S(2)}, u32[]{:S(2)}) collective-permute-start(f32[24,128]{1,0:T(8,128)S(1)} %get-tuple-element.24), channel_id=1, source_target_pairs={{0,1},{2,3},{4,5},{6,7},{8,9},{10,11},{12,13},{14,15},{16,17},{18,... | collective-permute-start | bytes 36872 | tf_op jit(solution)/shard_map/ppermute | solution.py:452
  9.6 0.0 copy-start.6
  9.6 2.0 %collective-permute-start.3 = (f32[24,128]{1,0:T(8,128)S(1)}, f32[24,128]{1,0:T(8,128)S(1)}, u32[]{:S(2)}, u32[]{:S(2)}) collective-permute-start(f32[24,128]{1,0:T(8,128)S(1)} %get-tuple-element.25), channel_id=1, source_target_pairs={{1,2},{3,4},{5,6},{7,8},{9,10},{11,12},{13,14},{15,16},{17,18},{19... | collective-permute-start | bytes 36872 | tf_op jit(solution)/shard_map/ppermute | solution.py:452
  11.6 0.0 copy-done.1
  11.6 0.0 copy-done
  11.7 0.0 copy-done.2
  11.7 0.0 copy-done.4
  11.7 0.0 copy-done.3
  11.7 0.0 copy-done.5
  11.7 0.0 copy-done.6
  11.7 0.9 %shard_map.131 = (bf16[64,72]{1,0:T(8,128)(2,1)S(1)}, bf16[192,192]{1,0:T(8,128)(2,1)S(1)}, bf16[32,64]{1,0:T(8,128)(2,1)S(1)}, bf16[64,32]{1,0:T(8,128)(2,1)S(1...) custom-call(f32[64,73]{1,0:T(8,128)S(1)} %copy-done.4, ...), custom_call_target="tpu_custom_call" | custom-call | flops 1000000 | bytes 1000000 | tf_op jit(solution)/shard_map/pallas_call | solution.py:481
  12.6 0.0 collective-permute-done.2.col_one_ref
  12.6 2.1 %collective-permute-done.3.col_two_ref = f32[24,128]{1,0:T(8,128)S(1)} collective-permute-done((f32[24,128]{1,0:T(8,128)S(1)}, f32[24,128]{1,0:T(8,128)S(1)}, u32[]{:S(2)}, u32[]{:S(2)}) %collective-permute-start.3) | collective-permute-done | bytes 12320 | tf_op jit(solution)/shard_map/ppermute | solution.py:452
  14.7 8.0 %shard_map.132 = (f32[8,8,256]{2,1,0:T(8,128)}, f32[384,128]{1,0:T(8,128)S(1)}) custom-call(f32[17,8,256]{2,1,0:T(8,128)S(1)} %convert_add_fusion.own_ref, f32[72,256]{1,0:T(8,128)S(1)} %collective-permute-done.swap_one_ref.row_one_ref, f32[72,256]{1,0:T(8,128)S(1)} %collective-permute-done.1.swap_two_ref.row_two_ref, ...), custom_call_target="tpu_custom_call" | custom-call | flops 10000000 | bytes 10000000 | tf_op jit(solution)/shard_map/pallas_call | solution.py:495
  22.8 13.8 %all_to_all.15 = f32[16,24,128]{2,1,0:T(8,128)S(1)} all-to-all(f32[16,24,128]{2,1,0:T(8,128)S(1)} %bitcast.5), channel_id=1, replica_groups=mesh['gx'=8,'gy_0'=4,'gy_1'=4,'gy_2'=2] {'gy_0','gy_1'}, dimensions={0} | all-to-all | bytes 393216 | tf_op jit(solution)/shard_map/all_to_all | solution.py:459
  36.6 0.1 collective-permute-start.4
  36.7 1.2 %collective-permute-done.4 = f32[24,128]{1,0:T(8,128)S(1)} collective-permute-done((f32[24,128]{1,0:T(8,128)S(1)}, f32[24,128]{1,0:T(8,128)S(1)}, u32[]{:S(2)}, u32[]{:S(2)}) %collective-permute-start.4) | collective-permute-done | bytes 12320 | tf_op jit(solution)/shard_map/ppermute | solution.py:460
  37.8 19.7 %all_to_all.16 = f32[8,24,128]{2,1,0:T(8,128)S(1)} all-to-all(f32[8,24,128]{2,1,0:T(8,128)S(1)} %broadcast_in_dim.10), channel_id=1, replica_groups=mesh['gx'=8,'gy_0'=4,'gy_1'=4,'gy_2'=2] {'gx'}, dimensions={0} | all-to-all | bytes 196608 | tf_op jit(solution)/shard_map/all_to_all | solution.py:463
  57.6 10.2 %all_to_all.17 = f32[16,24,128]{2,1,0:T(8,128)S(1)} all-to-all(f32[16,24,128]{2,1,0:T(8,128)S(1)} %broadcast_in_dim.11), channel_id=1, replica_groups=mesh['gx'=8,'gy_0'=4,'gy_1'=4,'gy_2'=2] {'gy_0','gy_1'}, dimensions={0} | all-to-all | bytes 393216 | tf_op jit(solution)/shard_map/all_to_all | solution.py:465
  67.8 1.2 %shard_map.133 = (f32[64,73]{1,0:T(8,128)}, f32[64,577]{1,0:T(8,128)}, f32[32,65]{1,0:T(8,128)}) custom-call(f32[384,128]{1,0:T(8,128)S(1)} %bitcast.4, f32[64,73]{1,0:T(8,128)S(1)} %copy-done.2, f32[64,577]{1,0:T(8,128)S(1)} %copy-done, f32[32,65]{1,0:T(8,128)S(1)} %copy-done.3, f32[160,128]{1,0:T(8,128)S(1)} %get-tuple-element.35.choose_ref, ...), custom_call_target="tpu_custom_call" | custom-call | flops 1000000 | bytes 1000000 | tf_op jit(solution)/shard_map/pallas_call | solution.py:512
  (5 shorter events, 0.1 us)
Async XLA Ops:
  1.5 10.1 %copy-start.1 = (f32[64,577]{1,0:T(8,128)S(1)}, f32[64,577]{1,0:T(8,128)}, u32[]{:S(2)}) copy-start(f32[64,577]{1,0:T(8,128)} %two_ref.1) | copy-start | bytes 443140
  1.6 10.0 %copy-start = (f32[64,577]{1,0:T(8,128)S(1)}, f32[64,577]{1,0:T(8,128)}, u32[]{:S(2)}) copy-start(f32[64,577]{1,0:T(8,128)} %d2_ref.3) | copy-start | bytes 443140
  1.6 4.3 %collective-permute-start = (f32[72,256]{1,0:T(8,128)S(1)}, f32[72,256]{1,0:T(8,128)S(1)}, u32[]{:S(2)}, u32[]{:S(2)}) collective-permute-start(f32[72,256]{1,0:T(8,128)S(1)} %get-tuple-element.22), channel_id=1, source_target_pairs={{0,32},{64,96},{128,160},{192,224},{32,0},{96,64},{160,128},{224,1... | collective-permute-start | bytes 221192 | tf_op jit(solution)/shard_map/ppermute | solution.py:452
  4.2 7.5 %copy-start.2 = (f32[64,73]{1,0:T(8,128)S(1)}, f32[64,73]{1,0:T(8,128)}, u32[]{:S(2)}) copy-start(f32[64,73]{1,0:T(8,128)} %d1_ref.3) | copy-start | bytes 56068
  4.2 7.5 %copy-start.4 = (f32[64,73]{1,0:T(8,128)S(1)}, f32[64,73]{1,0:T(8,128)}, u32[]{:S(2)}) copy-start(f32[64,73]{1,0:T(8,128)} %one_ref.1) | copy-start | bytes 56068
  4.2 1.7 %collective-permute-start.1 = (f32[72,256]{1,0:T(8,128)S(1)}, f32[72,256]{1,0:T(8,128)S(1)}, u32[]{:S(2)}, u32[]{:S(2)}) collective-permute-start(f32[72,256]{1,0:T(8,128)S(1)} %get-tuple-element.23), channel_id=1, source_target_pairs={{32,64},{96,128},{160,192},{64,32},{128,96},{192,160},{33,65},{97,... | collective-permute-start | bytes 221192 | tf_op jit(solution)/shard_map/ppermute | solution.py:452
  5.9 5.8 %copy-start.3 = (f32[32,65]{1,0:T(8,128)S(1)}, f32[32,65]{1,0:T(8,128)}, u32[]{:S(2)}) copy-start(f32[32,65]{1,0:T(8,128)} %d3_ref.3) | copy-start | bytes 24964
  5.9 5.8 %copy-start.5 = (f32[32,65]{1,0:T(8,128)S(1)}, f32[32,65]{1,0:T(8,128)}, u32[]{:S(2)}) copy-start(f32[32,65]{1,0:T(8,128)} %head_ref.1) | copy-start | bytes 24964
  6.1 6.5 %collective-permute-start.2 = (f32[24,128]{1,0:T(8,128)S(1)}, f32[24,128]{1,0:T(8,128)S(1)}, u32[]{:S(2)}, u32[]{:S(2)}) collective-permute-start(f32[24,128]{1,0:T(8,128)S(1)} %get-tuple-element.24), channel_id=1, source_target_pairs={{0,1},{2,3},{4,5},{6,7},{8,9},{10,11},{12,13},{14,15},{16,17},{18,... | collective-permute-start | bytes 36872 | tf_op jit(solution)/shard_map/ppermute | solution.py:452
  9.6 2.1 %copy-start.6 = (s32[160]{0:T(256)S(1)}, s32[160]{0:T(256)}, u32[]{:S(2)}) copy-start(s32[160]{0:T(256)} %param.19) | copy-start | bytes 1924
  9.6 5.1 %collective-permute-start.3 = (f32[24,128]{1,0:T(8,128)S(1)}, f32[24,128]{1,0:T(8,128)S(1)}, u32[]{:S(2)}, u32[]{:S(2)}) collective-permute-start(f32[24,128]{1,0:T(8,128)S(1)} %get-tuple-element.25), channel_id=1, source_target_pairs={{1,2},{3,4},{5,6},{7,8},{9,10},{11,12},{13,14},{15,16},{17,18},{19... | collective-permute-start | bytes 36872 | tf_op jit(solution)/shard_map/ppermute | solution.py:452
  36.6 1.3 %collective-permute-start.4 = (f32[24,128]{1,0:T(8,128)S(1)}, f32[24,128]{1,0:T(8,128)S(1)}, u32[]{:S(2)}, u32[]{:S(2)}) collective-permute-start(f32[24,128]{1,0:T(8,128)S(1)} %reduce_sum.18), channel_id=1, source_target_pairs={{0,1},{1,0},{2,3},{3,2},{4,5},{5,4},{6,7},{7,6},{8,9},{9,8},{10,11... | collective-permute-start | bytes 36872 | tf_op jit(solution)/shard_map/ppermute | solution.py:460

commit v5 on v4

--- a/solution.py
+++ b/solution.py
@@ -44,12 +44,12 @@
 
 
 def pack_rows(own_ref, first_ref, second_ref):
-    even = is_even("gx")
+    upward = first_is_higher("gx")
     wet = own_ref[2 * LEV, :, :]
 
     def put(at, low, high):
-        first_ref[at : at + 8, :] = jnp.where(even, high, low)
-        second_ref[at : at + 8, :] = jnp.where(even, low, high)
+        first_ref[at : at + 8, :] = jnp.where(upward, high, low)
+        second_ref[at : at + 8, :] = jnp.where(upward, low, high)
 
     put(64, wet, wet)
     for k in range(REACH):
@@ -59,8 +59,11 @@
         put(48 + k * 8, own_ref[LEV : 2 * LEV, k, :], own_ref[LEV : 2 * LEV, H - 2 + k, :])
 
 
-def is_even(axis):
-    return lax.rem(lax.axis_index(axis), 2) == 0
+FIRST_SWAP = {"gx": 0, GY: 1}
+
+
+def first_is_higher(axis):
+    return lax.rem(lax.axis_index(axis), 2) == FIRST_SWAP[axis]
 
 
 class Chosen:
@@ -72,8 +75,8 @@
 
 
 def by_side(axis, first_ref, second_ref):
-    even = is_even(axis)
-    return Chosen(even, second_ref, first_ref), Chosen(even, first_ref, second_ref)
+    upward = first_is_higher(axis)
+    return Chosen(upward, second_ref, first_ref), Chosen(upward, first_ref, second_ref)
 
 
 def row_parts(r, own_ref, below_ref, above_ref):
@@ -91,9 +94,9 @@
     return field, wet, target
 
 
-def pack_cols(own_ref, swap_one_ref, swap_two_ref, first_ref, second_ref):
+def pack_cols(own_ref, swap_one_ref, swap_two_ref, after_ref, first_ref, second_ref):
     below_ref, above_ref = by_side("gx", swap_one_ref, swap_two_ref)
-    even = is_even(GY)
+    upward = first_is_higher(GY)
     lane = lax.broadcasted_iota(jnp.int32, (8, 128), 1)
     zero = jnp.zeros((8, 128), F32)
     packed = [zero] * 6
@@ -110,8 +113,8 @@
                 v = jnp.where(inner < 10, v, turned(target[:, first : first + 128], move[2]))
             packed[side + at] = jnp.where((inner >= 0) & (inner < 12), v, packed[side + at])
     for k in range(3):
-        first_ref[k * 8 : k * 8 + 8, :] = jnp.where(even, packed[3 + k], packed[k])
-        second_ref[k * 8 : k * 8 + 8, :] = jnp.where(even, packed[k], packed[3 + k])
+        first_ref[k * 8 : k * 8 + 8, :] = jnp.where(upward, packed[3 + k], packed[k])
+        second_ref[k * 8 : k * 8 + 8, :] = jnp.where(upward, packed[k], packed[3 + k])
 
 
 def row_sums(parts):
@@ -447,7 +450,8 @@
 
 def exchange(first, second, axis):
     count = lax.axis_size(axis)
-    pairs = [[(i, i + 1) for i in range(start, count - 1, 2)] for start in (0, 1)]
+    starts = (FIRST_SWAP[axis], 1 - FIRST_SWAP[axis])
+    pairs = [[(i, i + 1) for i in range(start, count - 1, 2)] for start in starts]
     swaps = [[*p, *((b, a) for a, b in p)] for p in pairs]
     return lax.ppermute(first, axis, swaps[0]), lax.ppermute(second, axis, swaps[1])
 
@@ -474,10 +478,6 @@
     own = widened(init, 0) + widened(target, LEV) + widened(mask[None], 2 * LEV).astype(F32)
     packs = kernel(pack_rows, [shape((72, W))] * 2, 10**5, 4)(own)
     rows_in = exchange(*packs, "gx")
-    packs = kernel(pack_cols, [shape((24, 128))] * 2, 10**5, 4)(
-        own, *rows_in
-    )
-    cols_in = exchange(*packs, GY)
     *weights, choose, below_ratio = kernel(
         prepare,
         [
@@ -488,6 +488,10 @@
         10**6,
         8,
     )(one, two, head, d1, d2, d3, gid.reshape(1, -1))
+    packs = kernel(pack_cols, [shape((24, 128))] * 2, 10**5, 4)(
+        own, *rows_in, weights[6]
+    )
+    cols_in = exchange(*packs, GY)
 
     def rows(size, dtype=F32):
         return pltpu.VMEM((20 * size, PITCH), dtype)

time: 69.9 us -> 69.2 us (0.990)
  waiting for transfers between devices: 4.22 us -> 2.24 us
  blocking collectives: 43.7 us -> 45.2 us
  starting transfers between devices: 8.94 us -> 7.77 us
  local copies, waits for them, and re-layouts: 0.06 us -> 0.77 us
    ppermute x2, waiting for transfers between devices: 2.11 us -> 0.01 us  [exchange(): lax.ppermute(second, axis, swaps[1])]
    all_to_all x1, blocking collectives: 13.8 us -> 15.8 us  [total_of(): own = jnp.sum(lax.all_to_all(pieces, near, 0, 0, tiled=True), axis=0)]
    ppermute x2, starting transfers between devices: 2.82 us -> 0.88 us  [exchange(): lax.ppermute(second, axis, swaps[1])]
    unnamed x14, local copies, waits for them, and re-layouts: 0.03 us -> 0.74 us
  transfers between devices with their start and end apart: 5 -> 5, of which waited for: 3 -> 2; matrix products, arithmetic and copies ran while one was open for 0% -> 0% of each run, Pallas kernels for 1% -> 1%
where the time goes in v5:
time: 69.2 us; the launch traced here: 68.2 us
  blocking collectives  45.2 us (65%)
  Pallas kernels  10.3 us (15%)
  starting transfers between devices  7.77 us (11%)
  waiting for transfers between devices  2.24 us (3%)
  other arithmetic  0.98 us (1%)
  between operations  0.82 us (1%)
  local copies, waits for them, and re-layouts  0.77 us (1%)
    all_to_all x1, blocking collectives, total_of(): own = jnp.sum(lax.all_to_all(copies, 'gx', 0, 0, tiled=True), axis=0)  19.2 us
    all_to_all x1, blocking collectives, total_of(): own = jnp.sum(lax.all_to_all(pieces, near, 0, 0, tiled=True), axis=0)  15.8 us
    all_to_all x1, blocking collectives, total_of(): return lax.all_to_all(copies, near, 0, 0, tiled=True).reshape(grad.shape)  10.2 us
    pallas_call x1, Pallas kernels, per_device(): kernel(main, [shape((LEV, H, W)), shape((384, 128))], 10 ** 7, 40, in_spe...  8 us
    ppermute x2, starting transfers between devices, exchange(): lax.ppermute(first, axis, swaps[0])  6.6 us
  transfers between devices with their start and end apart: 5, of which 2 were waited for; matrix products, arithmetic and copies ran while one was open for 0% of the time, Pallas kernels for 1%

profile of v5, /device:TPU:1, one launch (start us, length us, event | category | flops | bytes accessed | tf_op | source)
XLA Modules:
  0.0 68.2 jit_solution(2110824395242317707)
XLA Ops:
  0.6 0.0 copy-start
  0.6 0.0 copy-start.1
  0.7 0.9 %convert_add_fusion.own_ref = f32[17,8,256]{2,1,0:T(8,128)S(1)} fusion(s32[1,8,256]{2,1,0:T(8,128)} %bitcast.7, f32[8,8,256]{2,1,0:T(8,128)} %param.11, f32[8,8,256]{2,1,0:T(8,128)} %param.10), kind=kLoop, calls=%fused_computation | loop fusion | flops 104448 | bytes 278528 | tf_op jit(solution)/shard_map/add | solution.py:478
  1.6 0.0 copy-start.2
  1.6 0.0 copy-start.3
  1.6 0.0 copy-start.4
  1.6 0.1 shard_map.129
  1.7 2.6 %collective-permute-start = (f32[72,256]{1,0:T(8,128)S(1)}, f32[72,256]{1,0:T(8,128)S(1)}, u32[]{:S(2)}, u32[]{:S(2)}) collective-permute-start(f32[72,256]{1,0:T(8,128)S(1)} %get-tuple-element.22), channel_id=1, source_target_pairs={{0,32},{64,96},{128,160},{192,224},{32,0},{96,64},{160,128},{224,1... | collective-permute-start | bytes 221192 | tf_op jit(solution)/shard_map/ppermute | solution.py:456
  4.2 0.0 copy-start.6
  4.2 0.8 %collective-permute-start.1 = (f32[72,256]{1,0:T(8,128)S(1)}, f32[72,256]{1,0:T(8,128)S(1)}, u32[]{:S(2)}, u32[]{:S(2)}) collective-permute-start(f32[72,256]{1,0:T(8,128)S(1)} %get-tuple-element.23), channel_id=1, source_target_pairs={{32,64},{96,128},{160,192},{64,32},{128,96},{192,160},{33,65},{97,... | collective-permute-start | bytes 221192 | tf_op jit(solution)/shard_map/ppermute | solution.py:456
  5.0 0.0 copy-done
  5.1 0.0 copy-done.1
  5.1 0.0 copy-done.2
  5.1 0.0 copy-done.3
  5.1 0.0 copy-done.4
  5.1 0.0 copy-done.6
  5.1 0.0 copy-start.5
  5.1 0.7 %copy-done.5 = f32[32,65]{1,0:T(8,128)S(1)} copy-done((f32[32,65]{1,0:T(8,128)S(1)}, f32[32,65]{1,0:T(8,128)}, u32[]{:S(2)}) %copy-start.5) | copy-done | bytes 8344
  5.8 0.9 %shard_map.130 = (bf16[64,72]{1,0:T(8,128)(2,1)S(1)}, bf16[192,192]{1,0:T(8,128)(2,1)S(1)}, bf16[32,64]{1,0:T(8,128)(2,1)S(1)}, bf16[64,32]{1,0:T(8,128)(2,1)S(1...) custom-call(f32[64,73]{1,0:T(8,128)S(1)} %copy-done.4, ...), custom_call_target="tpu_custom_call" | custom-call | flops 1000000 | bytes 1000000 | tf_op jit(solution)/shard_map/pallas_call | solution.py:481
  6.7 0.0 collective-permute-done.swap_one_ref.row_one_ref
  6.7 0.0 collective-permute-done.1.swap_two_ref.row_two_ref
  6.7 0.2 shard_map.131
  6.9 4.0 %collective-permute-start.2 = (f32[24,128]{1,0:T(8,128)S(1)}, f32[24,128]{1,0:T(8,128)S(1)}, u32[]{:S(2)}, u32[]{:S(2)}) collective-permute-start(f32[24,128]{1,0:T(8,128)S(1)} %get-tuple-element.25), channel_id=1, source_target_pairs={{1,2},{3,4},{5,6},{7,8},{9,10},{11,12},{13,14},{15,16},{17,18},{19... | collective-permute-start | bytes 36872 | tf_op jit(solution)/shard_map/ppermute | solution.py:456
  11.0 0.1 collective-permute-start.3
  11.1 1.3 %collective-permute-done.2.col_one_ref = f32[24,128]{1,0:T(8,128)S(1)} collective-permute-done((f32[24,128]{1,0:T(8,128)S(1)}, f32[24,128]{1,0:T(8,128)S(1)}, u32[]{:S(2)}, u32[]{:S(2)}) %collective-permute-start.2) | collective-permute-done | bytes 12320 | tf_op jit(solution)/shard_map/ppermute | solution.py:456
  12.3 0.0 collective-permute-done.3.col_two_ref
  12.4 8.0 %shard_map.132 = (f32[8,8,256]{2,1,0:T(8,128)}, f32[384,128]{1,0:T(8,128)S(1)}) custom-call(f32[17,8,256]{2,1,0:T(8,128)S(1)} %convert_add_fusion.own_ref, f32[72,256]{1,0:T(8,128)S(1)} %collective-permute-done.swap_one_ref.row_one_ref, f32[72,256]{1,0:T(8,128)S(1)} %collective-permute-done.1.swap_two_ref.row_two_ref, ...), custom_call_target="tpu_custom_call" | custom-call | flops 10000000 | bytes 10000000 | tf_op jit(solution)/shard_map/pallas_call | solution.py:499
  20.4 15.8 %all_to_all.15 = f32[16,24,128]{2,1,0:T(8,128)S(1)} all-to-all(f32[16,24,128]{2,1,0:T(8,128)S(1)} %bitcast.5), channel_id=1, replica_groups=mesh['gx'=8,'gy_0'=4,'gy_1'=4,'gy_2'=2] {'gy_0','gy_1'}, dimensions={0} | all-to-all | bytes 393216 | tf_op jit(solution)/shard_map/all_to_all | solution.py:463
  36.2 0.3 collective-permute-start.4
  36.5 1.0 %collective-permute-done.4 = f32[24,128]{1,0:T(8,128)S(1)} collective-permute-done((f32[24,128]{1,0:T(8,128)S(1)}, f32[24,128]{1,0:T(8,128)S(1)}, u32[]{:S(2)}, u32[]{:S(2)}) %collective-permute-start.4) | collective-permute-done | bytes 12320 | tf_op jit(solution)/shard_map/ppermute | solution.py:464
  37.5 19.2 %all_to_all.16 = f32[8,24,128]{2,1,0:T(8,128)S(1)} all-to-all(f32[8,24,128]{2,1,0:T(8,128)S(1)} %broadcast_in_dim.10), channel_id=1, replica_groups=mesh['gx'=8,'gy_0'=4,'gy_1'=4,'gy_2'=2] {'gx'}, dimensions={0} | all-to-all | bytes 196608 | tf_op jit(solution)/shard_map/all_to_all | solution.py:467
  56.7 10.2 %all_to_all.17 = f32[16,24,128]{2,1,0:T(8,128)S(1)} all-to-all(f32[16,24,128]{2,1,0:T(8,128)S(1)} %broadcast_in_dim.11), channel_id=1, replica_groups=mesh['gx'=8,'gy_0'=4,'gy_1'=4,'gy_2'=2] {'gy_0','gy_1'}, dimensions={0} | all-to-all | bytes 393216 | tf_op jit(solution)/shard_map/all_to_all | solution.py:469
  66.9 1.2 %shard_map.133 = (f32[64,73]{1,0:T(8,128)}, f32[64,577]{1,0:T(8,128)}, f32[32,65]{1,0:T(8,128)}) custom-call(f32[384,128]{1,0:T(8,128)S(1)} %bitcast.4, f32[64,73]{1,0:T(8,128)S(1)} %copy-done.2, f32[64,577]{1,0:T(8,128)S(1)} %copy-done, f32[32,65]{1,0:T(8,128)S(1)} %copy-done.3, f32[160,128]{1,0:T(8,128)S(1)} %get-tuple-element.35.choose_ref, ...), custom_call_target="tpu_custom_call" | custom-call | flops 1000000 | bytes 1000000 | tf_op jit(solution)/shard_map/pallas_call | solution.py:516
  (5 shorter events, 0.1 us)
Async XLA Ops:
  0.6 4.4 %copy-start = (f32[64,577]{1,0:T(8,128)S(1)}, f32[64,577]{1,0:T(8,128)}, u32[]{:S(2)}) copy-start(f32[64,577]{1,0:T(8,128)} %d2_ref.3) | copy-start | bytes 443140
  0.6 4.4 %copy-start.1 = (f32[64,577]{1,0:T(8,128)S(1)}, f32[64,577]{1,0:T(8,128)}, u32[]{:S(2)}) copy-start(f32[64,577]{1,0:T(8,128)} %two_ref.1) | copy-start | bytes 443140
  1.6 3.5 %copy-start.2 = (f32[64,73]{1,0:T(8,128)S(1)}, f32[64,73]{1,0:T(8,128)}, u32[]{:S(2)}) copy-start(f32[64,73]{1,0:T(8,128)} %d1_ref.3) | copy-start | bytes 56068
  1.6 3.5 %copy-start.3 = (f32[32,65]{1,0:T(8,128)S(1)}, f32[32,65]{1,0:T(8,128)}, u32[]{:S(2)}) copy-start(f32[32,65]{1,0:T(8,128)} %d3_ref.3) | copy-start | bytes 24964
  1.6 3.5 %copy-start.4 = (f32[64,73]{1,0:T(8,128)S(1)}, f32[64,73]{1,0:T(8,128)}, u32[]{:S(2)}) copy-start(f32[64,73]{1,0:T(8,128)} %one_ref.1) | copy-start | bytes 56068
  1.7 5.0 %collective-permute-start = (f32[72,256]{1,0:T(8,128)S(1)}, f32[72,256]{1,0:T(8,128)S(1)}, u32[]{:S(2)}, u32[]{:S(2)}) collective-permute-start(f32[72,256]{1,0:T(8,128)S(1)} %get-tuple-element.22), channel_id=1, source_target_pairs={{0,32},{64,96},{128,160},{192,224},{32,0},{96,64},{160,128},{224,1... | collective-permute-start | bytes 221192 | tf_op jit(solution)/shard_map/ppermute | solution.py:456
  4.2 0.8 %copy-start.6 = (s32[160]{0:T(256)S(1)}, s32[160]{0:T(256)}, u32[]{:S(2)}) copy-start(s32[160]{0:T(256)} %param.19) | copy-start | bytes 1924
  4.2 2.5 %collective-permute-start.1 = (f32[72,256]{1,0:T(8,128)S(1)}, f32[72,256]{1,0:T(8,128)S(1)}, u32[]{:S(2)}, u32[]{:S(2)}) collective-permute-start(f32[72,256]{1,0:T(8,128)S(1)} %get-tuple-element.23), channel_id=1, source_target_pairs={{32,64},{96,128},{160,192},{64,32},{128,96},{192,160},{33,65},{97,... | collective-permute-start | bytes 221192 | tf_op jit(solution)/shard_map/ppermute | solution.py:456
  5.1 0.7 %copy-start.5 = (f32[32,65]{1,0:T(8,128)S(1)}, f32[32,65]{1,0:T(8,128)}, u32[]{:S(2)}) copy-start(f32[32,65]{1,0:T(8,128)} %head_ref.1) | copy-start | bytes 24964
  6.9 5.4 %collective-permute-start.2 = (f32[24,128]{1,0:T(8,128)S(1)}, f32[24,128]{1,0:T(8,128)S(1)}, u32[]{:S(2)}, u32[]{:S(2)}) collective-permute-start(f32[24,128]{1,0:T(8,128)S(1)} %get-tuple-element.25), channel_id=1, source_target_pairs={{1,2},{3,4},{5,6},{7,8},{9,10},{11,12},{13,14},{15,16},{17,18},{19... | collective-permute-start | bytes 36872 | tf_op jit(solution)/shard_map/ppermute | solution.py:456
  11.0 1.4 %collective-permute-start.3 = (f32[24,128]{1,0:T(8,128)S(1)}, f32[24,128]{1,0:T(8,128)S(1)}, u32[]{:S(2)}, u32[]{:S(2)}) collective-permute-start(f32[24,128]{1,0:T(8,128)S(1)} %get-tuple-element.26), channel_id=1, source_target_pairs={{0,1},{2,3},{4,5},{6,7},{8,9},{10,11},{12,13},{14,15},{16,17},{18,... | collective-permute-start | bytes 36872 | tf_op jit(solution)/shard_map/ppermute | solution.py:456
  36.2 1.3 %collective-permute-start.4 = (f32[24,128]{1,0:T(8,128)S(1)}, f32[24,128]{1,0:T(8,128)S(1)}, u32[]{:S(2)}, u32[]{:S(2)}) collective-permute-start(f32[24,128]{1,0:T(8,128)S(1)} %reduce_sum.18), channel_id=1, source_target_pairs={{0,1},{1,0},{2,3},{3,2},{4,5},{5,4},{6,7},{7,6},{8,9},{9,8},{10,11... | collective-permute-start | bytes 36872 | tf_op jit(solution)/shard_map/ppermute | solution.py:464

commit v6 on v5

--- a/solution.py
+++ b/solution.py
@@ -312,39 +312,38 @@
             lanes([e[:, :W].astype(BF) for e in e2]),
         )
 
-    def tail_one(own):
-        def body(rs):
-            h2, slope, p = second_layer(hm1, rs)
-            n = len(rs)
-            e3s = []
-            for r, pr in zip(rs, cut(p, n)):
-                x, diff = slopes(xc1, r)
-                wet = part(wet_s, r, 8)[...]
-                c = [0.25 * pr[8 * k : 8 * k + 8] for k in range(4)]
-                move = [c[k] * diff[k] for k in range(4)]
-                new = x + wet * (move[0] + move[1] + move[2] + move[3])
-                if own:
-                    part(fin, r, 8)[...] = new
-                g = wet * (new - part(tgt, r, 8)[...])
-                wg = wet * g
-                t = [wg * c[k] for k in range(4)]
-                left = g - t[0] - t[1] - t[2] - t[3]
-                part(rem, r, 8)[...] = left + turned(t[2], 1) + turned(t[3], -1)
-                part(up, r, 8)[...] = t[0]
-                part(down, r, 8)[...] = t[1]
-                e3s.append(
-                    jnp.concatenate(
-                        [wg * move[k] * (1.0 - pr[8 * k : 8 * k + 8]) for k in range(4)], axis=0
-                    )
+    def of_block(rs, arrays):
+        return [v for r, v in zip(rs, arrays) if 0 <= r - REACH < H]
+
+    def tail_one(rs):
+        h2, slope, p = second_layer(hm1, rs)
+        n = len(rs)
+        e3s = []
+        for r, pr in zip(rs, cut(p, n)):
+            x, diff = slopes(xc1, r)
+            wet = part(wet_s, r, 8)[...]
+            c = [0.25 * pr[8 * k : 8 * k + 8] for k in range(4)]
+            move = [c[k] * diff[k] for k in range(4)]
+            new = x + wet * (move[0] + move[1] + move[2] + move[3])
+            if 0 <= r - REACH < H:
+                part(fin, r, 8)[...] = new
+            g = wet * (new - part(tgt, r, 8)[...])
+            wg = wet * g
+            t = [wg * c[k] for k in range(4)]
+            left = g - t[0] - t[1] - t[2] - t[3]
+            part(rem, r, 8)[...] = left + turned(t[2], 1) + turned(t[3], -1)
+            part(up, r, 8)[...] = t[0]
+            part(down, r, 8)[...] = t[1]
+            e3s.append(
+                jnp.concatenate(
+                    [wg * move[k] * (1.0 - pr[8 * k : 8 * k + 8]) for k in range(4)], axis=0
                 )
-            e2 = dot(w3t_ref[...], lanes([e.astype(BF) for e in e3s])) * slope
-            e2s = cut(e2, n)
-            for r, e in zip(rs, e2s):
-                part(em1, r, 64)[...] = e.astype(BF)
-            if own:
-                tail_grads(rs, e3s, e2s, cut(h2, n), hc1)
-
-        return body
+            )
+        e2 = dot(w3t_ref[...], lanes([e.astype(BF) for e in e3s])) * slope
+        e2s = cut(e2, n)
+        for r, e in zip(rs, e2s):
+            part(em1, r, 64)[...] = e.astype(BF)
+        tail_grads(of_block(rs, rs), of_block(rs, e3s), of_block(rs, e2s), of_block(rs, cut(h2, n)), hc1)
 
     def first_error(em, sp1, rs):
         return [v * part(sp1, r, 64)[...] for r, v in zip(rs, conv(w2t_ref[...], em, rs))]
@@ -356,15 +355,11 @@
             lanes([part(xc, r - 1, 24, 0, 72)[:, :width].astype(BF) for r in rs]),
         )
 
-    def first_one(own):
-        def body(rs):
-            e1 = first_error(em1, sp11, rs)
-            for r, e in zip(rs, e1):
-                part(e1s, r, 64)[...] = e.astype(BF)
-            if own:
-                first_grads(rs, e1, xc1, W)
-
-        return body
+    def first_one(rs):
+        e1 = first_error(em1, sp11, rs)
+        for r, e in zip(rs, e1):
+            part(e1s, r, 64)[...] = e.astype(BF)
+        first_grads(of_block(rs, rs), of_block(rs, e1), xc1, W)
 
     def back_zero(rs):
         y = dot(w1t_ref[...], lanes([part(e1s, r - 1, 64, 0, 192)[...] for r in rs]))
@@ -386,14 +381,12 @@
     loop(-5, 13, 9, first_layer(xc0, hm0, hc0, sp10))
     loop(-4, 12, 16, tail_zero)
     loop(-3, 11, 14, first_layer(xc1, hm1, hc1, sp11))
-    tail_one(False)([4, 5, 14, 15])
-    loop(0, 8, 8, tail_one(True))
+    loop(-2, 10, 12, tail_one)
     for r in range(H):
         final_v[:, r, :] = fin[(r + REACH) * 8 : (r + REACH) * 8 + 8, :W]
     out = pltpu.make_async_copy(final_v, final_ref, sem)
     out.start()
-    first_one(False)([5, 14])
-    loop(0, 8, 8, first_one(True))
+    loop(-1, 9, 10, first_one)
     loop(0, 8, 8, back_zero)
     loop(-1, 9, 10, first_zero)
 

time: 69.2 us -> 68.8 us (level)
  no operation moved by 1% of the time
where the time goes in v6:
time: 68.8 us; the launch traced here: 67.8 us
  blocking collectives  45.2 us (66%)
  Pallas kernels  10 us (15%)
  starting transfers between devices  7.79 us (11%)
  waiting for transfers between devices  2.22 us (3%)
  other arithmetic  0.98 us (1%)
  between operations  0.82 us (1%)
  local copies, waits for them, and re-layouts  0.77 us (1%)
    all_to_all x1, blocking collectives, total_of(): own = jnp.sum(lax.all_to_all(copies, 'gx', 0, 0, tiled=True), axis=0)  19.2 us
    all_to_all x1, blocking collectives, total_of(): own = jnp.sum(lax.all_to_all(pieces, near, 0, 0, tiled=True), axis=0)  15.8 us
    all_to_all x1, blocking collectives, total_of(): return lax.all_to_all(copies, near, 0, 0, tiled=True).reshape(grad.shape)  10.2 us
    pallas_call x1, Pallas kernels, per_device(): kernel(main, [shape((LEV, H, W)), shape((384, 128))], 10 ** 7, 40, in_spe...  7.66 us
    ppermute x2, starting transfers between devices, exchange(): lax.ppermute(first, axis, swaps[0])  6.6 us
  transfers between devices with their start and end apart: 5, of which 2 were waited for; matrix products, arithmetic and copies ran while one was open for 0% of the time, Pallas kernels for 1%

profile of v6, /device:TPU:1, one launch (start us, length us, event | category | flops | bytes accessed | tf_op | source)
XLA Modules:
  0.0 67.8 jit_solution(4860103920049486047)
XLA Ops:
  0.6 0.0 copy-start
  0.6 0.0 copy-start.1
  0.7 0.9 %convert_add_fusion.own_ref = f32[17,8,256]{2,1,0:T(8,128)S(1)} fusion(s32[1,8,256]{2,1,0:T(8,128)} %bitcast.7, f32[8,8,256]{2,1,0:T(8,128)} %param.11, f32[8,8,256]{2,1,0:T(8,128)} %param.10), kind=kLoop, calls=%fused_computation | loop fusion | flops 104448 | bytes 278528 | tf_op jit(solution)/shard_map/add | solution.py:471
  1.6 0.0 copy-start.2
  1.6 0.0 copy-start.3
  1.6 0.0 copy-start.4
  1.6 0.1 shard_map.129
  1.7 2.6 %collective-permute-start = (f32[72,256]{1,0:T(8,128)S(1)}, f32[72,256]{1,0:T(8,128)S(1)}, u32[]{:S(2)}, u32[]{:S(2)}) collective-permute-start(f32[72,256]{1,0:T(8,128)S(1)} %get-tuple-element.22), channel_id=1, source_target_pairs={{0,32},{64,96},{128,160},{192,224},{32,0},{96,64},{160,128},{224,1... | collective-permute-start | bytes 221192 | tf_op jit(solution)/shard_map/ppermute | solution.py:449
  4.2 0.0 copy-start.6
  4.2 0.8 %collective-permute-start.1 = (f32[72,256]{1,0:T(8,128)S(1)}, f32[72,256]{1,0:T(8,128)S(1)}, u32[]{:S(2)}, u32[]{:S(2)}) collective-permute-start(f32[72,256]{1,0:T(8,128)S(1)} %get-tuple-element.23), channel_id=1, source_target_pairs={{32,64},{96,128},{160,192},{64,32},{128,96},{192,160},{33,65},{97,... | collective-permute-start | bytes 221192 | tf_op jit(solution)/shard_map/ppermute | solution.py:449
  5.0 0.0 copy-done
  5.1 0.0 copy-done.1
  5.1 0.0 copy-done.2
  5.1 0.0 copy-done.3
  5.1 0.0 copy-done.4
  5.1 0.0 copy-done.6
  5.1 0.0 copy-start.5
  5.1 0.7 %copy-done.5 = f32[32,65]{1,0:T(8,128)S(1)} copy-done((f32[32,65]{1,0:T(8,128)S(1)}, f32[32,65]{1,0:T(8,128)}, u32[]{:S(2)}) %copy-start.5) | copy-done | bytes 8344
  5.8 0.9 %shard_map.130 = (bf16[64,72]{1,0:T(8,128)(2,1)S(1)}, bf16[192,192]{1,0:T(8,128)(2,1)S(1)}, bf16[32,64]{1,0:T(8,128)(2,1)S(1)}, bf16[64,32]{1,0:T(8,128)(2,1)S(1...) custom-call(f32[64,73]{1,0:T(8,128)S(1)} %copy-done.4, ...), custom_call_target="tpu_custom_call" | custom-call | flops 1000000 | bytes 1000000 | tf_op jit(solution)/shard_map/pallas_call | solution.py:474
  6.7 0.0 collective-permute-done.swap_one_ref.row_one_ref
  6.7 0.0 collective-permute-done.1.swap_two_ref.row_two_ref
  6.7 0.2 shard_map.131
  6.9 4.0 %collective-permute-start.2 = (f32[24,128]{1,0:T(8,128)S(1)}, f32[24,128]{1,0:T(8,128)S(1)}, u32[]{:S(2)}, u32[]{:S(2)}) collective-permute-start(f32[24,128]{1,0:T(8,128)S(1)} %get-tuple-element.25), channel_id=1, source_target_pairs={{1,2},{3,4},{5,6},{7,8},{9,10},{11,12},{13,14},{15,16},{17,18},{19... | collective-permute-start | bytes 36872 | tf_op jit(solution)/shard_map/ppermute | solution.py:449
  11.0 0.1 collective-permute-start.3
  11.1 1.3 %collective-permute-done.2.col_one_ref = f32[24,128]{1,0:T(8,128)S(1)} collective-permute-done((f32[24,128]{1,0:T(8,128)S(1)}, f32[24,128]{1,0:T(8,128)S(1)}, u32[]{:S(2)}, u32[]{:S(2)}) %collective-permute-start.2) | collective-permute-done | bytes 12320 | tf_op jit(solution)/shard_map/ppermute | solution.py:449
  12.3 0.0 collective-permute-done.3.col_two_ref
  12.4 7.7 %shard_map.132 = (f32[8,8,256]{2,1,0:T(8,128)}, f32[384,128]{1,0:T(8,128)S(1)}) custom-call(f32[17,8,256]{2,1,0:T(8,128)S(1)} %convert_add_fusion.own_ref, f32[72,256]{1,0:T(8,128)S(1)} %collective-permute-done.swap_one_ref.row_one_ref, f32[72,256]{1,0:T(8,128)S(1)} %collective-permute-done.1.swap_two_ref.row_two_ref, ...), custom_call_target="tpu_custom_call" | custom-call | flops 10000000 | bytes 10000000 | tf_op jit(solution)/shard_map/pallas_call | solution.py:492
  20.0 15.8 %all_to_all.15 = f32[16,24,128]{2,1,0:T(8,128)S(1)} all-to-all(f32[16,24,128]{2,1,0:T(8,128)S(1)} %bitcast.5), channel_id=1, replica_groups=mesh['gx'=8,'gy_0'=4,'gy_1'=4,'gy_2'=2] {'gy_0','gy_1'}, dimensions={0} | all-to-all | bytes 393216 | tf_op jit(solution)/shard_map/all_to_all | solution.py:456
  35.8 0.3 collective-permute-start.4
  36.2 0.9 %collective-permute-done.4 = f32[24,128]{1,0:T(8,128)S(1)} collective-permute-done((f32[24,128]{1,0:T(8,128)S(1)}, f32[24,128]{1,0:T(8,128)S(1)}, u32[]{:S(2)}, u32[]{:S(2)}) %collective-permute-start.4) | collective-permute-done | bytes 12320 | tf_op jit(solution)/shard_map/ppermute | solution.py:457
  37.1 19.2 %all_to_all.16 = f32[8,24,128]{2,1,0:T(8,128)S(1)} all-to-all(f32[8,24,128]{2,1,0:T(8,128)S(1)} %broadcast_in_dim.10), channel_id=1, replica_groups=mesh['gx'=8,'gy_0'=4,'gy_1'=4,'gy_2'=2] {'gx'}, dimensions={0} | all-to-all | bytes 196608 | tf_op jit(solution)/shard_map/all_to_all | solution.py:460
  56.4 10.2 %all_to_all.17 = f32[16,24,128]{2,1,0:T(8,128)S(1)} all-to-all(f32[16,24,128]{2,1,0:T(8,128)S(1)} %broadcast_in_dim.11), channel_id=1, replica_groups=mesh['gx'=8,'gy_0'=4,'gy_1'=4,'gy_2'=2] {'gy_0','gy_1'}, dimensions={0} | all-to-all | bytes 393216 | tf_op jit(solution)/shard_map/all_to_all | solution.py:462
  66.6 1.2 %shard_map.133 = (f32[64,73]{1,0:T(8,128)}, f32[64,577]{1,0:T(8,128)}, f32[32,65]{1,0:T(8,128)}) custom-call(f32[384,128]{1,0:T(8,128)S(1)} %bitcast.4, f32[64,73]{1,0:T(8,128)S(1)} %copy-done.2, f32[64,577]{1,0:T(8,128)S(1)} %copy-done, f32[32,65]{1,0:T(8,128)S(1)} %copy-done.3, f32[160,128]{1,0:T(8,128)S(1)} %get-tuple-element.35.choose_ref, ...), custom_call_target="tpu_custom_call" | custom-call | flops 1000000 | bytes 1000000 | tf_op jit(solution)/shard_map/pallas_call | solution.py:509
  (5 shorter events, 0.1 us)
Async XLA Ops:
  0.6 4.4 %copy-start = (f32[64,577]{1,0:T(8,128)S(1)}, f32[64,577]{1,0:T(8,128)}, u32[]{:S(2)}) copy-start(f32[64,577]{1,0:T(8,128)} %d2_ref.3) | copy-start | bytes 443140
  0.6 4.4 %copy-start.1 = (f32[64,577]{1,0:T(8,128)S(1)}, f32[64,577]{1,0:T(8,128)}, u32[]{:S(2)}) copy-start(f32[64,577]{1,0:T(8,128)} %two_ref.1) | copy-start | bytes 443140
  1.6 3.5 %copy-start.2 = (f32[64,73]{1,0:T(8,128)S(1)}, f32[64,73]{1,0:T(8,128)}, u32[]{:S(2)}) copy-start(f32[64,73]{1,0:T(8,128)} %d1_ref.3) | copy-start | bytes 56068
  1.6 3.5 %copy-start.3 = (f32[32,65]{1,0:T(8,128)S(1)}, f32[32,65]{1,0:T(8,128)}, u32[]{:S(2)}) copy-start(f32[32,65]{1,0:T(8,128)} %d3_ref.3) | copy-start | bytes 24964
  1.6 3.5 %copy-start.4 = (f32[64,73]{1,0:T(8,128)S(1)}, f32[64,73]{1,0:T(8,128)}, u32[]{:S(2)}) copy-start(f32[64,73]{1,0:T(8,128)} %one_ref.1) | copy-start | bytes 56068
  1.7 5.0 %collective-permute-start = (f32[72,256]{1,0:T(8,128)S(1)}, f32[72,256]{1,0:T(8,128)S(1)}, u32[]{:S(2)}, u32[]{:S(2)}) collective-permute-start(f32[72,256]{1,0:T(8,128)S(1)} %get-tuple-element.22), channel_id=1, source_target_pairs={{0,32},{64,96},{128,160},{192,224},{32,0},{96,64},{160,128},{224,1... | collective-permute-start | bytes 221192 | tf_op jit(solution)/shard_map/ppermute | solution.py:449
  4.2 0.8 %copy-start.6 = (s32[160]{0:T(256)S(1)}, s32[160]{0:T(256)}, u32[]{:S(2)}) copy-start(s32[160]{0:T(256)} %param.19) | copy-start | bytes 1924
  4.2 2.5 %collective-permute-start.1 = (f32[72,256]{1,0:T(8,128)S(1)}, f32[72,256]{1,0:T(8,128)S(1)}, u32[]{:S(2)}, u32[]{:S(2)}) collective-permute-start(f32[72,256]{1,0:T(8,128)S(1)} %get-tuple-element.23), channel_id=1, source_target_pairs={{32,64},{96,128},{160,192},{64,32},{128,96},{192,160},{33,65},{97,... | collective-permute-start | bytes 221192 | tf_op jit(solution)/shard_map/ppermute | solution.py:449
  5.1 0.7 %copy-start.5 = (f32[32,65]{1,0:T(8,128)S(1)}, f32[32,65]{1,0:T(8,128)}, u32[]{:S(2)}) copy-start(f32[32,65]{1,0:T(8,128)} %head_ref.1) | copy-start | bytes 24964
  6.9 5.4 %collective-permute-start.2 = (f32[24,128]{1,0:T(8,128)S(1)}, f32[24,128]{1,0:T(8,128)S(1)}, u32[]{:S(2)}, u32[]{:S(2)}) collective-permute-start(f32[24,128]{1,0:T(8,128)S(1)} %get-tuple-element.25), channel_id=1, source_target_pairs={{1,2},{3,4},{5,6},{7,8},{9,10},{11,12},{13,14},{15,16},{17,18},{19... | collective-permute-start | bytes 36872 | tf_op jit(solution)/shard_map/ppermute | solution.py:449
  11.0 1.4 %collective-permute-start.3 = (f32[24,128]{1,0:T(8,128)S(1)}, f32[24,128]{1,0:T(8,128)S(1)}, u32[]{:S(2)}, u32[]{:S(2)}) collective-permute-start(f32[24,128]{1,0:T(8,128)S(1)} %get-tuple-element.26), channel_id=1, source_target_pairs={{0,1},{2,3},{4,5},{6,7},{8,9},{10,11},{12,13},{14,15},{16,17},{18,... | collective-permute-start | bytes 36872 | tf_op jit(solution)/shard_map/ppermute | solution.py:449
  35.8 1.3 %collective-permute-start.4 = (f32[24,128]{1,0:T(8,128)S(1)}, f32[24,128]{1,0:T(8,128)S(1)}, u32[]{:S(2)}, u32[]{:S(2)}) collective-permute-start(f32[24,128]{1,0:T(8,128)S(1)} %reduce_sum.18), channel_id=1, source_target_pairs={{0,1},{1,0},{2,3},{3,2},{4,5},{5,4},{6,7},{7,6},{8,9},{9,8},{10,11... | collective-permute-start | bytes 36872 | tf_op jit(solution)/shard_map/ppermute | solution.py:457

commit v7 on v6

--- a/solution.py
+++ b/solution.py
@@ -288,8 +288,10 @@
         h2, slope, p = second_layer(hm0, rs)
         n = len(rs)
         for r, h2r, sr, pr in zip(rs, cut(h2, n), cut(slope, n), cut(p, n)):
-            part(h2s, r, 64)[...] = h2r
-            part(sp2, r, 64)[...] = sr
+            own = 0 <= r - REACH < H
+            if own:
+                part(h2s, r, 64)[...] = h2r
+                part(sp2, r, 64)[...] = sr
             x, diff = slopes(xc0, r)
             wet = part(wet_s, r, 8)[...]
             change = jnp.zeros_like(x)
@@ -297,7 +299,8 @@
                 pk = pr[8 * k : 8 * k + 8]
                 move = 0.25 * pk * diff[k]
                 change = change + move
-                part(wd, r, 32, 8 * k, 8)[...] = wet * move * (1.0 - pk)
+                if own:
+                    part(wd, r, 32, 8 * k, 8)[...] = wet * move * (1.0 - pk)
             for k, piece in enumerate(thrice(x + wet * change)):
                 part(xc1, r, 24, 8 * k, 8)[...] = piece
 

time: 68.8 us -> 68.9 us (level)
  no operation moved by 1% of the time
where the time goes in v7:
time: 68.9 us; the launch traced here: 67.9 us
  blocking collectives  45.2 us (66%)
  Pallas kernels  10 us (15%)
  starting transfers between devices  7.79 us (11%)
  waiting for transfers between devices  2.22 us (3%)
  other arithmetic  0.98 us (1%)
  between operations  0.82 us (1%)
  local copies, waits for them, and re-layouts  0.77 us (1%)
    all_to_all x1, blocking collectives, total_of(): own = jnp.sum(lax.all_to_all(copies, 'gx', 0, 0, tiled=True), axis=0)  19.2 us
    all_to_all x1, blocking collectives, total_of(): own = jnp.sum(lax.all_to_all(pieces, near, 0, 0, tiled=True), axis=0)  15.8 us
    all_to_all x1, blocking collectives, total_of(): return lax.all_to_all(copies, near, 0, 0, tiled=True).reshape(grad.shape)  10.2 us
    pallas_call x1, Pallas kernels, per_device(): kernel(main, [shape((LEV, H, W)), shape((384, 128))], 10 ** 7, 40, in_spe...  7.7 us
    ppermute x2, starting transfers between devices, exchange(): lax.ppermute(first, axis, swaps[0])  6.6 us
  transfers between devices with their start and end apart: 5, of which 2 were waited for; matrix products, arithmetic and copies ran while one was open for 0% of the time, Pallas kernels for 1%

profile of v7, /device:TPU:1, one launch (start us, length us, event | category | flops | bytes accessed | tf_op | source)
XLA Modules:
  0.0 67.9 jit_solution(16712923993364576503)
XLA Ops:
  0.6 0.0 copy-start
  0.6 0.0 copy-start.1
  0.7 0.9 %convert_add_fusion.own_ref = f32[17,8,256]{2,1,0:T(8,128)S(1)} fusion(s32[1,8,256]{2,1,0:T(8,128)} %bitcast.7, f32[8,8,256]{2,1,0:T(8,128)} %param.11, f32[8,8,256]{2,1,0:T(8,128)} %param.10), kind=kLoop, calls=%fused_computation | loop fusion | flops 104448 | bytes 278528 | tf_op jit(solution)/shard_map/add | solution.py:474
  1.6 0.0 copy-start.2
  1.6 0.0 copy-start.3
  1.6 0.0 copy-start.4
  1.6 0.1 shard_map.129
  1.7 2.6 %collective-permute-start = (f32[72,256]{1,0:T(8,128)S(1)}, f32[72,256]{1,0:T(8,128)S(1)}, u32[]{:S(2)}, u32[]{:S(2)}) collective-permute-start(f32[72,256]{1,0:T(8,128)S(1)} %get-tuple-element.22), channel_id=1, source_target_pairs={{0,32},{64,96},{128,160},{192,224},{32,0},{96,64},{160,128},{224,1... | collective-permute-start | bytes 221192 | tf_op jit(solution)/shard_map/ppermute | solution.py:452
  4.2 0.0 copy-start.6
  4.2 0.8 %collective-permute-start.1 = (f32[72,256]{1,0:T(8,128)S(1)}, f32[72,256]{1,0:T(8,128)S(1)}, u32[]{:S(2)}, u32[]{:S(2)}) collective-permute-start(f32[72,256]{1,0:T(8,128)S(1)} %get-tuple-element.23), channel_id=1, source_target_pairs={{32,64},{96,128},{160,192},{64,32},{128,96},{192,160},{33,65},{97,... | collective-permute-start | bytes 221192 | tf_op jit(solution)/shard_map/ppermute | solution.py:452
  5.0 0.0 copy-done
  5.1 0.0 copy-done.1
  5.1 0.0 copy-done.2
  5.1 0.0 copy-done.3
  5.1 0.0 copy-done.4
  5.1 0.0 copy-done.6
  5.1 0.0 copy-start.5
  5.1 0.7 %copy-done.5 = f32[32,65]{1,0:T(8,128)S(1)} copy-done((f32[32,65]{1,0:T(8,128)S(1)}, f32[32,65]{1,0:T(8,128)}, u32[]{:S(2)}) %copy-start.5) | copy-done | bytes 8344
  5.8 0.9 %shard_map.130 = (bf16[64,72]{1,0:T(8,128)(2,1)S(1)}, bf16[192,192]{1,0:T(8,128)(2,1)S(1)}, bf16[32,64]{1,0:T(8,128)(2,1)S(1)}, bf16[64,32]{1,0:T(8,128)(2,1)S(1...) custom-call(f32[64,73]{1,0:T(8,128)S(1)} %copy-done.4, ...), custom_call_target="tpu_custom_call" | custom-call | flops 1000000 | bytes 1000000 | tf_op jit(solution)/shard_map/pallas_call | solution.py:477
  6.7 0.0 collective-permute-done.swap_one_ref.row_one_ref
  6.7 0.0 collective-permute-done.1.swap_two_ref.row_two_ref
  6.7 0.2 shard_map.131
  6.9 4.0 %collective-permute-start.2 = (f32[24,128]{1,0:T(8,128)S(1)}, f32[24,128]{1,0:T(8,128)S(1)}, u32[]{:S(2)}, u32[]{:S(2)}) collective-permute-start(f32[24,128]{1,0:T(8,128)S(1)} %get-tuple-element.25), channel_id=1, source_target_pairs={{1,2},{3,4},{5,6},{7,8},{9,10},{11,12},{13,14},{15,16},{17,18},{19... | collective-permute-start | bytes 36872 | tf_op jit(solution)/shard_map/ppermute | solution.py:452
  11.0 0.1 collective-permute-start.3
  11.1 1.3 %collective-permute-done.2.col_one_ref = f32[24,128]{1,0:T(8,128)S(1)} collective-permute-done((f32[24,128]{1,0:T(8,128)S(1)}, f32[24,128]{1,0:T(8,128)S(1)}, u32[]{:S(2)}, u32[]{:S(2)}) %collective-permute-start.2) | collective-permute-done | bytes 12320 | tf_op jit(solution)/shard_map/ppermute | solution.py:452
  12.3 0.0 collective-permute-done.3.col_two_ref
  12.4 7.7 %shard_map.132 = (f32[8,8,256]{2,1,0:T(8,128)}, f32[384,128]{1,0:T(8,128)S(1)}) custom-call(f32[17,8,256]{2,1,0:T(8,128)S(1)} %convert_add_fusion.own_ref, f32[72,256]{1,0:T(8,128)S(1)} %collective-permute-done.swap_one_ref.row_one_ref, f32[72,256]{1,0:T(8,128)S(1)} %collective-permute-done.1.swap_two_ref.row_two_ref, ...), custom_call_target="tpu_custom_call" | custom-call | flops 10000000 | bytes 10000000 | tf_op jit(solution)/shard_map/pallas_call | solution.py:495
  20.1 15.8 %all_to_all.15 = f32[16,24,128]{2,1,0:T(8,128)S(1)} all-to-all(f32[16,24,128]{2,1,0:T(8,128)S(1)} %bitcast.5), channel_id=1, replica_groups=mesh['gx'=8,'gy_0'=4,'gy_1'=4,'gy_2'=2] {'gy_0','gy_1'}, dimensions={0} | all-to-all | bytes 393216 | tf_op jit(solution)/shard_map/all_to_all | solution.py:459
  35.9 0.3 collective-permute-start.4
  36.2 0.9 %collective-permute-done.4 = f32[24,128]{1,0:T(8,128)S(1)} collective-permute-done((f32[24,128]{1,0:T(8,128)S(1)}, f32[24,128]{1,0:T(8,128)S(1)}, u32[]{:S(2)}, u32[]{:S(2)}) %collective-permute-start.4) | collective-permute-done | bytes 12320 | tf_op jit(solution)/shard_map/ppermute | solution.py:460
  37.2 19.2 %all_to_all.16 = f32[8,24,128]{2,1,0:T(8,128)S(1)} all-to-all(f32[8,24,128]{2,1,0:T(8,128)S(1)} %broadcast_in_dim.10), channel_id=1, replica_groups=mesh['gx'=8,'gy_0'=4,'gy_1'=4,'gy_2'=2] {'gx'}, dimensions={0} | all-to-all | bytes 196608 | tf_op jit(solution)/shard_map/all_to_all | solution.py:463
  56.4 10.2 %all_to_all.17 = f32[16,24,128]{2,1,0:T(8,128)S(1)} all-to-all(f32[16,24,128]{2,1,0:T(8,128)S(1)} %broadcast_in_dim.11), channel_id=1, replica_groups=mesh['gx'=8,'gy_0'=4,'gy_1'=4,'gy_2'=2] {'gy_0','gy_1'}, dimensions={0} | all-to-all | bytes 393216 | tf_op jit(solution)/shard_map/all_to_all | solution.py:465
  66.6 1.2 %shard_map.133 = (f32[64,73]{1,0:T(8,128)}, f32[64,577]{1,0:T(8,128)}, f32[32,65]{1,0:T(8,128)}) custom-call(f32[384,128]{1,0:T(8,128)S(1)} %bitcast.4, f32[64,73]{1,0:T(8,128)S(1)} %copy-done.2, f32[64,577]{1,0:T(8,128)S(1)} %copy-done, f32[32,65]{1,0:T(8,128)S(1)} %copy-done.3, f32[160,128]{1,0:T(8,128)S(1)} %get-tuple-element.35.choose_ref, ...), custom_call_target="tpu_custom_call" | custom-call | flops 1000000 | bytes 1000000 | tf_op jit(solution)/shard_map/pallas_call | solution.py:512
  (5 shorter events, 0.1 us)
Async XLA Ops:
  0.6 4.4 %copy-start = (f32[64,577]{1,0:T(8,128)S(1)}, f32[64,577]{1,0:T(8,128)}, u32[]{:S(2)}) copy-start(f32[64,577]{1,0:T(8,128)} %d2_ref.3) | copy-start | bytes 443140
  0.6 4.4 %copy-start.1 = (f32[64,577]{1,0:T(8,128)S(1)}, f32[64,577]{1,0:T(8,128)}, u32[]{:S(2)}) copy-start(f32[64,577]{1,0:T(8,128)} %two_ref.1) | copy-start | bytes 443140
  1.6 3.5 %copy-start.2 = (f32[64,73]{1,0:T(8,128)S(1)}, f32[64,73]{1,0:T(8,128)}, u32[]{:S(2)}) copy-start(f32[64,73]{1,0:T(8,128)} %d1_ref.3) | copy-start | bytes 56068
  1.6 3.5 %copy-start.3 = (f32[32,65]{1,0:T(8,128)S(1)}, f32[32,65]{1,0:T(8,128)}, u32[]{:S(2)}) copy-start(f32[32,65]{1,0:T(8,128)} %d3_ref.3) | copy-start | bytes 24964
  1.6 3.5 %copy-start.4 = (f32[64,73]{1,0:T(8,128)S(1)}, f32[64,73]{1,0:T(8,128)}, u32[]{:S(2)}) copy-start(f32[64,73]{1,0:T(8,128)} %one_ref.1) | copy-start | bytes 56068
  1.7 5.0 %collective-permute-start = (f32[72,256]{1,0:T(8,128)S(1)}, f32[72,256]{1,0:T(8,128)S(1)}, u32[]{:S(2)}, u32[]{:S(2)}) collective-permute-start(f32[72,256]{1,0:T(8,128)S(1)} %get-tuple-element.22), channel_id=1, source_target_pairs={{0,32},{64,96},{128,160},{192,224},{32,0},{96,64},{160,128},{224,1... | collective-permute-start | bytes 221192 | tf_op jit(solution)/shard_map/ppermute | solution.py:452
  4.2 0.8 %copy-start.6 = (s32[160]{0:T(256)S(1)}, s32[160]{0:T(256)}, u32[]{:S(2)}) copy-start(s32[160]{0:T(256)} %param.19) | copy-start | bytes 1924
  4.2 2.5 %collective-permute-start.1 = (f32[72,256]{1,0:T(8,128)S(1)}, f32[72,256]{1,0:T(8,128)S(1)}, u32[]{:S(2)}, u32[]{:S(2)}) collective-permute-start(f32[72,256]{1,0:T(8,128)S(1)} %get-tuple-element.23), channel_id=1, source_target_pairs={{32,64},{96,128},{160,192},{64,32},{128,96},{192,160},{33,65},{97,... | collective-permute-start | bytes 221192 | tf_op jit(solution)/shard_map/ppermute | solution.py:452
  5.1 0.7 %copy-start.5 = (f32[32,65]{1,0:T(8,128)S(1)}, f32[32,65]{1,0:T(8,128)}, u32[]{:S(2)}) copy-start(f32[32,65]{1,0:T(8,128)} %head_ref.1) | copy-start | bytes 24964
  6.9 5.4 %collective-permute-start.2 = (f32[24,128]{1,0:T(8,128)S(1)}, f32[24,128]{1,0:T(8,128)S(1)}, u32[]{:S(2)}, u32[]{:S(2)}) collective-permute-start(f32[24,128]{1,0:T(8,128)S(1)} %get-tuple-element.25), channel_id=1, source_target_pairs={{1,2},{3,4},{5,6},{7,8},{9,10},{11,12},{13,14},{15,16},{17,18},{19... | collective-permute-start | bytes 36872 | tf_op jit(solution)/shard_map/ppermute | solution.py:452
  11.0 1.4 %collective-permute-start.3 = (f32[24,128]{1,0:T(8,128)S(1)}, f32[24,128]{1,0:T(8,128)S(1)}, u32[]{:S(2)}, u32[]{:S(2)}) collective-permute-start(f32[24,128]{1,0:T(8,128)S(1)} %get-tuple-element.26), channel_id=1, source_target_pairs={{0,1},{2,3},{4,5},{6,7},{8,9},{10,11},{12,13},{14,15},{16,17},{18,... | collective-permute-start | bytes 36872 | tf_op jit(solution)/shard_map/ppermute | solution.py:452
  35.9 1.3 %collective-permute-start.4 = (f32[24,128]{1,0:T(8,128)S(1)}, f32[24,128]{1,0:T(8,128)S(1)}, u32[]{:S(2)}, u32[]{:S(2)}) collective-permute-start(f32[24,128]{1,0:T(8,128)S(1)} %reduce_sum.18), channel_id=1, source_target_pairs={{0,1},{1,0},{2,3},{3,2},{4,5},{5,4},{6,7},{7,6},{8,9},{9,8},{10,11... | collective-permute-start | bytes 36872 | tf_op jit(solution)/shard_map/ppermute | solution.py:460
